TPU v7x, 256 devices: a whole 4x4x8 slice. The times are simulated.
256 devices in a mesh: slab: 4 (over y), dom: 64 (over z, x, core).
Axes of the slice: x: 4, y: 4, z: 8, core: 2. Of those that a mesh axis runs over, the one named last changes fastest.
Arguments:
- disp: float32 [64, 96, 32, 384], P('dom', 'slab'), may hold values from -6 to 6
- f_ext: bfloat16 [64, 96, 32, 384], P('dom', 'slab'), may hold values from -6 to 6
- inv_diag: bfloat16 [64, 96, 32, 384], P('dom', 'slab'), may hold values from 0.049804688 to 0.29882812
- k_self: bfloat16 [384, 384], replicated, may hold values from -0.3125 to 0.3125
- k_layer: bfloat16 [384, 384], replicated, may hold values from -0.3125 to 0.3125
- k_side: bfloat16 [384, 384], replicated, may hold values from -0.3125 to 0.3125
- mortar: bfloat16 [64, 4, 128, 128, 128], P('dom', 'slab'), as said below
- gap0: float32 [64, 4, 128, 128], P('dom', 'slab'), may hold values from -1 to 1
- normals: float32 [64, 4, 32, 384], P('dom', 'slab'), may hold values from -4 to 4
- seg_slave: int32 [64, 4, 128], P('dom', 'slab'), may hold values from 0 to 31
- seg_src: int32 [64, 4, 128], P('dom', 'slab'), may hold values from 0 to 63, as said below
- seg_master: int32 [64, 4, 128], P('dom', 'slab'), may hold values from 0 to 31
Outputs:
- field: float32 [64, 96, 32, 384], P('dom', 'slab')
Inputs may be any that keep to these rules, and one draw needn't show every extreme that they name: `seg_src`: among the 128 segments of one partition no dom index is named more than 4 times, and one is named exactly 4 times. `mortar`: each segment's projection has independent entries off its diagonal.
All inputs are finite; a program needn't handle non-finite values.
Results may differ from a plain program's by a relative error of at most 0.0017.
Values may be sent and summed in bfloat16 or wider, within the bound.
No kernel may reach another device: no remote copies, remote signals or barrier semaphores. Data moves between devices by JAX's collectives and lax.ppermute only.
A program may use at most 64 MiB of HBM per device.

v0:
```python
import jax
import jax.numpy as jnp
from jax import lax
from jax.sharding import PartitionSpec as P

ITERS = 2


PENALTY = 2.0


def with_halo(block, sides, width):
    for axis, dim in sides:
        count = lax.axis_size(axis)
        forward = [(i, i + 1) for i in range(count - 1)]
        backward = [(target, source) for source, target in forward]
        low = lax.ppermute(
            lax.slice_in_dim(block, block.shape[dim] - width, None, axis=dim), axis, forward
        )
        high = lax.ppermute(lax.slice_in_dim(block, 0, width, axis=dim), axis, backward)
        block = jnp.concatenate([low, block, high], axis=dim)
    return block


def stiffness(rounded, k_self, k_layer, k_side):
    width = rounded.shape[-1]
    padded = with_halo(rounded, (("slab", 0),), 1)
    zero_block = jnp.zeros_like(rounded[:, :1])
    left = jnp.concatenate([zero_block, rounded[:, :-1]], axis=1)
    right = jnp.concatenate([rounded[:, 1:], zero_block], axis=1)

    def product(block, weight):
        return jnp.dot(block.reshape(-1, width), weight, preferred_element_type=jnp.float32)

    total = product(rounded, k_self) + product(padded[:-2], k_layer) + product(padded[2:], k_layer)
    total = total + product(left, k_side) + product(right, k_side)
    return total.reshape(rounded.shape)


def contact_terms(slave_rows, master_rows, mortar_part, gap_part, normal_rows):
    segs, width = master_rows.shape
    nodes = width // 3
    mapped = jnp.einsum(
        "snm,scm->scn",
        mortar_part,
        master_rows.reshape(segs, 3, nodes),
        preferred_element_type=jnp.float32,
    )
    normal3 = normal_rows.reshape(segs, 3, nodes)
    gap = gap_part + jnp.sum(normal3 * (mapped - slave_rows.reshape(segs, 3, nodes)), axis=1)
    pressure = PENALTY * jnp.maximum(-gap, 0.0)
    pushed = pressure[:, None, :] * normal3
    pushed_b = pushed.astype(jnp.bfloat16)
    back = -jnp.einsum("snm,scn->scm", mortar_part, pushed_b, preferred_element_type=jnp.float32)
    return (pushed.reshape(segs, width), back.reshape(segs, width))


def on_device(
    disp,
    f_ext,
    inv_diag,
    k_self,
    k_layer,
    k_side,
    mortar,
    gap0,
    normals,
    seg_slave,
    seg_src,
    seg_master,
):
    field = disp[0]
    load = f_ext[0].astype(jnp.float32)
    scale = inv_diag[0].astype(jnp.float32)
    mortar_own = mortar[0, 0]
    gap_own = gap0[0, 0]
    normal_own = normals[0, 0]
    slave_ids = seg_slave[0, 0]
    source_ids = seg_src[0, 0]
    master_ids = seg_master[0, 0]
    blocks = field.shape[1]
    domains = lax.axis_size("dom")
    normal_rows = normal_own[slave_ids]
    block_ids = jnp.arange(blocks, dtype=jnp.int32)
    slave_pick = (slave_ids[:, None] == block_ids[None, :]).astype(jnp.float32)
    for step in range(ITERS):
        rounded = field.astype(jnp.bfloat16)
        internal = stiffness(rounded, k_self, k_layer, k_side)
        surface = rounded[0]
        slave_rows = field[0][slave_ids]
        everyone = lax.all_gather(surface, "dom", axis=0, tiled=True)
        targets = source_ids * blocks + master_ids
        master_rows = everyone[targets]
        pushed, back = contact_terms(slave_rows, master_rows, mortar_own, gap_own, normal_rows)
        spread = jax.ops.segment_sum(back, targets, num_segments=domains * blocks)
        master_force = lax.psum_scatter(spread, "dom", scatter_dimension=0, tiled=True)
        slave_force = jnp.dot(slave_pick.T, pushed, precision=lax.Precision.HIGHEST)
        residual = load - internal
        residual = residual.at[0].add(-(slave_force + master_force))
        field = field + scale * residual
    return field[None]


def solution(mesh):
    in_specs = (
        P("dom", "slab", None, None),
        P("dom", "slab", None, None),
        P("dom", "slab", None, None),
        P(),
        P(),
        P(),
        P("dom", "slab", None, None, None),
        P("dom", "slab", None, None),
        P("dom", "slab", None, None),
        P("dom", "slab", None),
        P("dom", "slab", None),
        P("dom", "slab", None),
    )
    out_specs = P("dom", "slab", None, None)
    return jax.shard_map(
        on_device, mesh=mesh, in_specs=in_specs, out_specs=out_specs, check_vma=False
    )
```

profile of v0, /device:TPU:1, one launch (start us, length us, event | category | flops | bytes accessed | tf_op | source)
XLA Modules:
  0.0 482.9 jit_solution(8138441477089905866)
XLA Ops:
  6.5 1.8 fusion.64
  8.4 0.6 fusion.68
  9.1 0.8 gather_fusion
  10.0 0.1 copy.18
  10.2 0.2 copy-done.2
  10.4 1.4 gather_fusion.2
  11.9 1.1 copy.16
  12.9 0.8 copy.17
  13.8 77.5 %all-gather.5.cloned.1.call-done = bf16[1,2048,384]{2,1,0:T(8,128)(2,1)} async-done(((bf16[1,32,384]{2,1,0:T(8,128)(2,1)}), bf16[1,2048,384]{2,1,0:T(8,128)(2,1)}) %all-gather.5.cloned.1.call-update) | async-done | bytes 1572880 | tf_op jit(solution)/shard_map/all_gather | solution.py:91
  91.3 2.5 gather_fusion.1
  93.9 0.1 copy.15
  94.0 4.5 fusion.38
  98.7 0.1 copy.21
  98.9 3.4 fusion.23
  102.2 0.1 copy.22
  102.4 0.1 copy.23
  102.5 3.1 scatter_custom_fusion
  105.7 0.7 copy-done.15
  106.4 1.3 collective-permute-start.1
  107.7 4.0 collective-permute-start
  111.7 0.3 fusion.67
  112.0 0.2 concatenate.32
  112.2 0.7 copy-done.12
  112.9 0.5 fusion.69
  113.5 0.5 fusion.70
  114.2 0.5 convolution_add_fusion.5
  114.7 0.5 fusion.12
  115.2 0.5 convolution_add_fusion.3
  115.7 0.6 copy-done.10
  116.3 1.1 convert_subtract_fusion.1
  117.6 122.5 %reduce-scatter.3.cloned.1.call-done = f32[32,384]{1,0:T(8,128)} async-done(((f32[2048,384]{1,0:T(8,128)}), f32[32,384]{1,0:T(8,128)}) %reduce-scatter.3.cloned.1.call-update) | async-done | bytes 49168 | tf_op jit(solution)/shard_map/reduce_scatter | solution.py:96
  240.0 1.7 fusion.48
  241.8 1.7 fusion.62
  243.5 0.6 fusion.66
  244.1 0.2 reduce-scatter.5.cloned.1.call-start
  244.4 0.8 gather_fusion.4
  245.3 0.2 copy.27
  245.4 79.7 %all-gather.7.cloned.1.call-done = bf16[1,2048,384]{2,1,0:T(8,128)(2,1)} async-done(((bf16[1,32,384]{2,1,0:T(8,128)(2,1)}), bf16[1,2048,384]{2,1,0:T(8,128)(2,1)}) %all-gather.7.cloned.1.call-update) | async-done | bytes 1572880 | tf_op jit(solution)/shard_map/all_gather | solution.py:91
  325.2 2.5 gather_fusion.3
  327.7 0.1 copy.25
  327.9 4.5 fusion.35
  332.6 0.1 copy.31
  332.7 3.4 fusion.32
  336.1 0.1 copy.32
  336.2 0.1 copy.33
  336.4 3.1 scatter_custom_fusion.1
  339.5 0.7 copy-done.16
  340.2 1.3 collective-permute-start.3
  341.5 4.0 collective-permute-start.2
  345.5 0.3 fusion.65
  345.8 0.2 concatenate.36
  346.0 0.7 copy-done.13
  346.8 0.5 fusion.71
  347.3 0.5 fusion.72
  348.0 0.5 convolution_add_fusion.2
  348.5 0.5 fusion.13
  349.1 0.5 convolution_add_fusion
  349.6 0.6 copy-done.11
  350.1 0.1 convert_subtract_fusion
  350.3 0.7 mul.78
  351.0 1.7 copy.30
  352.7 121.2 %reduce-scatter.5.cloned.1.call-done = f32[32,384]{1,0:T(8,128)} async-done(((f32[2048,384]{1,0:T(8,128)}), f32[32,384]{1,0:T(8,128)}) %reduce-scatter.5.cloned.1.call-update) | async-done | bytes 49168 | tf_op jit(solution)/shard_map/reduce_scatter | solution.py:96
  473.9 1.2 fusion.44
  475.2 1.2 fusion.16
  (69 shorter events, 1.5 us)
Async XLA Ops:
  6.5 107.6 %copy-start = (bf16[384,384]{1,0:T(8,128)(2,1)S(1)}, bf16[384,384]{1,0:T(8,128)(2,1)}, u32[]{:S(2)}) copy-start(bf16[384,384]{1,0:T(8,128)(2,1)} %param.20) | copy-start | bytes 884740
  6.5 2.5 copy-start.18
  6.5 2.6 copy-start.1
  6.5 84.7 %all-gather.5.cloned.1.call-start = ((), (), s32[]{:S(2)}) async-start(), calls=%async_computation.4 | async-start | bytes 1597440 | tf_op jit(solution)/shard_map/all_gather | solution.py:91
  9.0 231.0 %reduce-scatter.3.cloned.1.call-start = ((), (), s32[]{:S(2)}) async-start(), calls=%async_computation.2 | async-start | bytes 3194880 | tf_op jit(solution)/shard_map/reduce_scatter | solution.py:96
  9.1 1.3 copy-start.2
  10.0 88.7 %copy-start.5 = (f32[128,384]{0,1:T(8,128)}, f32[128,384]{0,1:T(8,128)S(1)}, u32[]{:S(2)}) copy-start(f32[128,384]{0,1:T(8,128)S(1)} %copy.13) | copy-start | bytes 589828
  10.4 83.6 %copy-start.8 = (f32[128,3,128]{2,1,0:T(4,128)}, f32[128,3,128]{2,1,0:T(4,128)S(1)}, u32[]{:S(2)}) copy-start(f32[128,3,128]{2,1,0:T(4,128)S(1)} %copy.18) | copy-start | bytes 589828
  10.4 3.4 copy-start.19
  10.4 3.3 copy-start.20
  94.0 4.5 copy-start.14
  105.7 0.7 copy-start.15
  105.7 2.0 copy-start.17
  105.7 219.5 %all-gather.7.cloned.1.call-start = ((), (), s32[]{:S(2)}) async-start(), calls=%async_computation.5 | async-start | bytes 1597440 | tf_op jit(solution)/shard_map/all_gather | solution.py:91
  106.4 7.7 %collective-permute-start.1 = (bf16[1,32,384]{2,1,0:T(8,128)(2,1)S(1)}, bf16[1,32,384]{2,1,0:T(8,128)(2,1)S(1)}, u32[]{:S(2)}, u32[]{:S(2)}) collective-permute-start(bf16[1,32,384]{2,1,0:T(8,128)(2,1)S(1)} %copy-done.15), channel_id=1, source_target_pairs={{64,0},{128,64},{192,128},{65,1},{129,65},{193,129},{66,2},{130,66... | collective-permute-start | bytes 73736 | tf_op jit(solution)/shard_map/ppermute | solution.py:20
  107.7 6.4 %collective-permute-start = (bf16[1,32,384]{2,1,0:T(8,128)(2,1)S(1)}, bf16[1,32,384]{2,1,0:T(8,128)(2,1)S(1)}, u32[]{:S(2)}, u32[]{:S(2)}) collective-permute-start(bf16[1,32,384]{2,1,0:T(8,128)(2,1)S(1)} %copy-done.17), channel_id=1, source_target_pairs={{0,64},{64,128},{128,192},{1,65},{65,129},{129,193},{2,66},{66,130... | collective-permute-start | bytes 73736 | tf_op jit(solution)/shard_map/ppermute | solution.py:17
  112.0 1.0 copy-start.12
  112.2 1.3 copy-start.3
  115.2 1.1 copy-start.10
  244.1 229.8 %reduce-scatter.5.cloned.1.call-start = ((), (), s32[]{:S(2)}) async-start(), calls=%async_computation.3 | async-start | bytes 3194880 | tf_op jit(solution)/shard_map/reduce_scatter | solution.py:96
  245.1 82.8 %copy-start.9 = (f32[128,3,128]{2,1,0:T(4,128)S(1)}, f32[128,3,128]{2,1,0:T(4,128)}, u32[]{:S(2)}) copy-start(f32[128,3,128]{2,1,0:T(4,128)} %copy-done.8) | copy-start | bytes 589828
  327.9 4.6 copy-start.6
  339.5 0.7 copy-start.16
  340.2 7.6 %collective-permute-start.3 = (bf16[1,32,384]{2,1,0:T(8,128)(2,1)S(1)}, bf16[1,32,384]{2,1,0:T(8,128)(2,1)S(1)}, u32[]{:S(2)}, u32[]{:S(2)}) collective-permute-start(bf16[1,32,384]{2,1,0:T(8,128)(2,1)S(1)} %copy-done.16), channel_id=1, source_target_pairs={{64,0},{128,64},{192,128},{65,1},{129,65},{193,129},{66,2},{130,66... | collective-permute-start | bytes 73736 | tf_op jit(solution)/shard_map/ppermute | solution.py:20
  341.5 6.4 %collective-permute-start.2 = (bf16[1,32,384]{2,1,0:T(8,128)(2,1)}, bf16[1,32,384]{2,1,0:T(8,128)(2,1)S(1)}, u32[]{:S(2)}, u32[]{:S(2)}) collective-permute-start(bf16[1,32,384]{2,1,0:T(8,128)(2,1)} %get-tuple-element.38), channel_id=1, source_target_pairs={{0,64},{64,128},{128,192},{1,65},{65,129},{129,193},{2,66},{66,130... | collective-permute-start | bytes 73736 | tf_op jit(solution)/shard_map/ppermute | solution.py:17
  345.8 1.0 copy-start.13
  346.0 1.3 copy-start.4
  349.0 1.1 copy-start.11
  350.3 124.9 %copy-start.7 = (bf16[1,24,32,384]{3,2,1,0:T(8,128)(2,1)S(1)}, bf16[1,24,32,384]{3,2,1,0:T(8,128)(2,1)}, u32[]{:S(2)}) copy-start(bf16[1,24,32,384]{3,2,1,0:T(8,128)(2,1)} %param.18) | copy-start | bytes 1769476
Sparse Core Ops, SparseCore 0:
  10.1 81.1 all-gather.4
  105.8 134.1 reduce-scatter.2
  244.2 80.8 all-gather.6
  339.6 134.2 reduce-scatter.4
where the time goes:
time: 488 us; the launch traced here: 483 us
  waiting for transfers between devices  401 us (82%)
  matrix products  23.8 us (5%)
  local copies, waits for them, and re-layouts  21 us (4%)
  between operations  13.8 us (3%)
  other arithmetic  12.6 us (3%)
  starting transfers between devices  10.8 us (2%)
    reduce_scatter x2, waiting for transfers between devices, on_device(): lax.psum_scatter(spread, 'dom', scatter_dimension=0, tiled=True)  244 us
    all_gather x2, waiting for transfers between devices, on_device(): everyone = lax.all_gather(surface, 'dom', axis=0, tiled=True)  157 us
  transfers between devices with their start and end apart: 8, of which 4 were waited for; matrix products, arithmetic and copies ran while one was open for 3% of the time, Pallas kernels for 0%

commit v1 on v0

v1 whole, which is shorter than its diff:
```python
import jax
import jax.numpy as jnp
from jax import lax
from jax.sharding import PartitionSpec as P

ITERS = 2
PENALTY = 2.0
CAPACITY = 4


def shift(block, axis, step):
    count = lax.axis_size(axis)
    pairs = [(i, i + step) for i in range(count) if 0 <= i + step < count]
    return lax.ppermute(block, axis, pairs)


def stiffness(rounded, low, high, k_all):
    layers, blocks, width = rounded.shape
    stacked = jnp.concatenate([low, rounded, high], axis=0)
    prod = jnp.dot(
        stacked.reshape(-1, width), k_all, preferred_element_type=jnp.float32
    ).reshape(layers + 2, blocks, 3 * width)
    own, layer, side = prod[1:-1, :, :width], prod[:, :, width : 2 * width], prod[1:-1, :, 2 * width :]
    side = jnp.pad(side, ((0, 0), (1, 1), (0, 0)))
    return own + layer[:-2] + layer[2:] + side[:, :-2] + side[:, 2:]


def exchange(rows):
    domains = lax.axis_size("dom")
    parts = rows.reshape(domains, CAPACITY, -1)
    return lax.all_to_all(parts, "dom", 0, 0, tiled=True).reshape(rows.shape)


def on_device(
    disp, f_ext, inv_diag, k_self, k_layer, k_side, mortar, gap0, normals, seg_slave, seg_src, seg_master
):
    field = disp[0]
    load = f_ext[0].astype(jnp.float32)
    scale = inv_diag[0].astype(jnp.float32)
    mortar_own = mortar[0, 0]
    gap_own = gap0[0, 0]
    normal_own = normals[0, 0]
    slave_ids = seg_slave[0, 0]
    source_ids = seg_src[0, 0]
    master_ids = seg_master[0, 0]
    blocks, width = field.shape[1:]
    segs = slave_ids.shape[0]
    nodes = width // 3
    slots = lax.axis_size("dom") * CAPACITY
    bf16 = jnp.bfloat16

    places = jnp.arange(segs, dtype=jnp.int32)
    same = (source_ids[:, None] == source_ids[None, :]) & (places[None, :] < places[:, None])
    slot = source_ids * CAPACITY + jnp.sum(same.astype(jnp.int32), axis=1)
    hit = slot[:, None] == jnp.arange(slots, dtype=jnp.int32)[None, :]
    asked = jnp.sum(jnp.where(hit, master_ids[:, None] + 1, 0), axis=0) - 1
    wanted = exchange(asked[:, None])
    block_ids = jnp.arange(blocks, dtype=jnp.int32)
    send_pick = (wanted == block_ids[None, :]).astype(bf16)
    recv_pick = hit.astype(bf16)
    slave_pick = (slave_ids[:, None] == block_ids[None, :]).astype(jnp.float32)

    def pick(mask, rows):
        return jnp.dot(mask, rows, preferred_element_type=jnp.float32)

    normal3 = jnp.dot(slave_pick, normal_own, precision=lax.Precision.HIGHEST).reshape(segs, 3, nodes)
    k_all = jnp.concatenate([k_self, k_layer, k_side], axis=1)
    for step in range(ITERS):
        rounded = field.astype(bf16)
        arrived = exchange(pick(send_pick, rounded[0]).astype(bf16))
        low = shift(rounded[-1:], "slab", 1)
        high = shift(rounded[:1], "slab", -1)
        internal = stiffness(rounded, low, high, k_all)
        master_rows = pick(recv_pick, arrived).astype(bf16).reshape(segs, 3, nodes)
        slave_rows = jnp.dot(slave_pick, field[0], precision=lax.Precision.HIGHEST).reshape(segs, 3, nodes)
        mapped = jnp.einsum("snm,scm->scn", mortar_own, master_rows, preferred_element_type=jnp.float32)
        gap = gap_own + jnp.sum(normal3 * (mapped - slave_rows), axis=1)
        pressure = PENALTY * jnp.maximum(-gap, 0.0)
        pushed = pressure[:, None, :] * normal3
        back = -jnp.einsum("snm,scn->scm", mortar_own, pushed.astype(bf16), preferred_element_type=jnp.float32)
        returned = exchange(pick(recv_pick.T, back.astype(bf16).reshape(segs, width)).astype(bf16))
        master_force = pick(send_pick.T, returned)
        slave_force = jnp.dot(slave_pick.T, pushed.reshape(segs, width), precision=lax.Precision.HIGHEST)
        residual = load - internal
        residual = residual.at[0].add(-(slave_force + master_force))
        field = field + scale * residual
    return field[None]


def solution(mesh):
    in_specs = (
        P("dom", "slab", None, None),
        P("dom", "slab", None, None),
        P("dom", "slab", None, None),
        P(),
        P(),
        P(),
        P("dom", "slab", None, None, None),
        P("dom", "slab", None, None),
        P("dom", "slab", None, None),
        P("dom", "slab", None),
        P("dom", "slab", None),
        P("dom", "slab", None),
    )
    return jax.shard_map(
        on_device, mesh=mesh, in_specs=in_specs, out_specs=P("dom", "slab", None, None), check_vma=False
    )
```

time: 488 us -> 137 us (0.28)
  waiting for transfers between devices: 401 us -> 31 us
  starting transfers between devices: 10.8 us -> 51.1 us
  between operations: 13.8 us -> 0.53 us
  local copies, waits for them, and re-layouts: 21 us -> 14.1 us
    reduce_scatter x2 -> x0, waiting for transfers between devices: 244 us -> none  [on_device(): lax.psum_scatter(spread, 'dom', scatter_dimension=0, tiled=True)]
    all_gather x2 -> x0, waiting for transfers between devices: 157 us -> none  [on_device(): everyone = lax.all_gather(surface, 'dom', axis=0, tiled=True)]
    all_to_all x0 -> x5, starting transfers between devices: none -> 40.8 us  [exchange(): return lax.all_to_all(parts, 'dom', 0, 0, tiled=True).reshape(rows.shape)]
    all_to_all x0 -> x5, waiting for transfers between devices: none -> 27.6 us  [exchange(): return lax.all_to_all(parts, 'dom', 0, 0, tiled=True).reshape(rows.shape)]
    gather x10 -> x0, local copies, waits for them, and re-layouts: 9.41 us -> none  [the longest x4 5.15 us: on_device(): master_rows = everyone[targets]]
    scatter-add x2 -> x0, other arithmetic: 6.25 us -> none  [on_device(): spread = jax.ops.segment_sum(back, targets, num_segments=domains * blocks)]
    sub x2, other arithmetic: 1.28 us -> 6.64 us  [on_device(): residual = load - internal]
    dot_general x16 -> x19, matrix products: 23.8 us -> 24.1 us  [the longest x2 9.05 us: on_device(): jnp.einsum('snm,scm->scn', mortar_own, master_rows, preferred_element_typ...]
  transfers between devices with their start and end apart: 8 -> 9, of which waited for: 4 -> 5; matrix products, arithmetic and copies ran while one was open for 3% -> 13% of each run, Pallas kernels for 0% -> 0%
where the time goes in v1:
time: 137 us; the launch traced here: 136 us
  starting transfers between devices  51.1 us (37%)
  waiting for transfers between devices  31 us (23%)
  matrix products  24.1 us (18%)
  other arithmetic  15.4 us (11%)
  local copies, waits for them, and re-layouts  14.1 us (10%)
    all_to_all x5, starting transfers between devices, exchange(): return lax.all_to_all(parts, 'dom', 0, 0, tiled=True).reshape(rows.shape)  40.8 us
    all_to_all x5, waiting for transfers between devices, exchange(): return lax.all_to_all(parts, 'dom', 0, 0, tiled=True).reshape(rows.shape)  27.6 us
    ppermute x4, starting transfers between devices, shift(): return lax.ppermute(block, axis, pairs)  10.3 us
    dot_general x2, matrix products, on_device(): jnp.einsum('snm,scm->scn', mortar_own, master_rows, preferred_element_typ...  9.05 us
    dot_general x2, matrix products, on_device(): jnp.einsum('snm,scn->scm', mortar_own, pushed.astype(bf16), preferred_ele...  6.76 us
    sub x2, other arithmetic, on_device(): residual = load - internal  6.64 us
    unnamed x29, local copies, waits for them, and re-layouts  4.63 us
    dot_general x2, matrix products, stiffness(): jnp.dot(stacked.reshape(-1, width), k_all, preferred_element_type=jnp.flo...  3.74 us
  transfers between devices with their start and end apart: 9, of which 5 were waited for; matrix products, arithmetic and copies ran while one was open for 13% of the time, Pallas kernels for 0%

profile of v1, /device:TPU:1, one launch (start us, length us, event | category | flops | bytes accessed | tf_op | source)
XLA Modules:
  0.0 136.3 jit_solution(6098436516157056181)
XLA Ops:
  0.0 0.7 add_bitcast_fusion
  0.7 0.9 convert_reduce_fusion
  1.6 0.7 multiply_add_fusion
  2.4 0.7 sub.20
  3.1 13.0 %all-to-all-start = ((s32[64,4,1]{1,2,0:T(1,128)}), s32[64,4,1]{1,2,0:T(1,128)S(1)}, u32[]{:S(2)}, u32[]{:S(2)}) async-start(s32[64,4,1]{1,2,0:T(1,128)} %bitcast.11), calls=%async_computation | async-start | bytes 65536 | tf_op jit(solution)/shard_map/all_to_all | solution.py:31
  16.1 1.4 %bitcast_convert_fusion = bf16[24,32,384]{2,1,0:T(8,128)(2,1)S(1)} fusion(f32[1,24,32,384]{3,2,1,0:T(8,128)} %param.16), kind=kLoop, calls=%fused_computation.27 | loop fusion | flops 294912 | bytes 1769472 | tf_op jit(solution)/shard_map/convert_element_type | solution.py:69
  17.5 3.3 %collective-permute-start = (bf16[1,32,384]{2,1,0:T(8,128)(2,1)S(1)}, bf16[1,32,384]{2,1,0:T(8,128)(2,1)S(1)}, u32[]{:S(2)}, u32[]{:S(2)}) collective-permute-start(bf16[1,32,384]{2,1,0:T(8,128)(2,1)S(1)} %get-tuple-element.37), channel_id=1, source_target_pairs={{0,64},{64,128},{128,192},{1,65},{65,129},{129,193},{2,66},{66,130... | collective-permute-start | bytes 73736 | tf_op jit(solution)/shard_map/ppermute | solution.py:14
  20.9 1.3 collective-permute-start.1
  22.2 3.2 %all-to-all-done = s32[64,4,1]{1,2,0:T(1,128)S(1)} async-done(((s32[64,4,1]{1,2,0:T(1,128)}), s32[64,4,1]{1,2,0:T(1,128)S(1)}, u32[]{:S(2)}, u32[]{:S(2)}) %all-to-all-start) | async-done | bytes 1056 | tf_op jit(solution)/shard_map/all_to_all | solution.py:31
  25.4 0.5 broadcast.96
  25.9 0.7 reduce.7
  26.7 0.3 convolution_convert_fusion.1
  27.0 0.7 reshape.178
  27.7 7.4 %all-to-all-start.1 = ((bf16[64,4,384]{2,1,0:T(4,128)(2,1)}), bf16[64,4,384]{2,1,0:T(4,128)(2,1)S(1)}, u32[]{:S(2)}, u32[]{:S(2)}) async-start(bf16[64,4,384]{2,1,0:T(4,128)(2,1)} %reshape.178), calls=%async_computation.1 | async-start | bytes 393216 | tf_op jit(solution)/shard_map/all_to_all | solution.py:31
  35.1 0.4 fusion.69
  35.6 1.2 fusion.35
  36.9 1.8 %copy-done.2 = f32[26,32,1152]{2,1,0:T(8,128)} copy-done((f32[26,32,1152]{2,1,0:T(8,128)}, f32[26,32,1152]{2,1,0:T(8,128)S(1)}, u32[]{:S(2)}) %copy-start.2) | copy-done | bytes 3833880
  38.7 1.1 slice.132
  39.8 7.3 %all-to-all-done.1 = bf16[64,4,384]{2,1,0:T(4,128)(2,1)S(1)} async-done(((bf16[64,4,384]{2,1,0:T(4,128)(2,1)}), bf16[64,4,384]{2,1,0:T(4,128)(2,1)S(1)}, u32[]{:S(2)}, u32[]{:S(2)}) %all-to-all-start.1) | async-done | bytes 196640 | tf_op jit(solution)/shard_map/all_to_all | solution.py:31
  47.2 0.2 convolution_convert_fusion.5
  47.5 0.1 copy.61
  47.7 4.5 %fusion.6 = f32[128,3,128]{2,1,0:T(4,128)S(1)} fusion(bf16[128,3,128]{2,1,0:T(4,128)(2,1)S(1)} %copy.61, bf16[1,1,128,128,128]{4,3,2,1,0:T(8,128)(2,1)} %param.22), kind=kOutput, calls=%fused_computation.6 | convolution fusion | flops 12582912 | bytes 4489216 | tf_op jit(solution)/shard_map/snm,scm->scn/dot_general | solution.py:76
  52.2 0.2 copy.63
  52.4 0.4 fusion.29
  52.8 0.7 fusion.94
  53.5 0.1 copy.65
  53.6 3.4 %fusion.24 = bf16[128,3,128]{2,1,0:T(4,128)(2,1)S(1)} fusion(bf16[128,3,128]{2,1,0:T(4,128)(2,1)S(1)} %copy.65, bf16[1,1,128,128,128]{4,3,2,1,0:T(8,128)(2,1)} %param.22), kind=kOutput, calls=%fused_computation.35 | convolution fusion | flops 12681216 | bytes 4390912 | tf_op jit(solution)/shard_map/snm,scn->scm/dot_general | solution.py:80
  57.0 0.1 copy.66
  57.2 0.3 convolution_convert_fusion.3
  57.5 0.7 reshape.183
  58.2 4.5 %all-to-all-start.2 = ((bf16[64,4,384]{2,1,0:T(4,128)(2,1)}), bf16[64,4,384]{2,1,0:T(4,128)(2,1)S(1)}, u32[]{:S(2)}, u32[]{:S(2)}) async-start(bf16[64,4,384]{2,1,0:T(4,128)(2,1)} %reshape.183), calls=%async_computation.2 | async-start | bytes 393216 | tf_op jit(solution)/shard_map/all_to_all | solution.py:31
  62.7 3.3 %convert_subtract_fusion.1 = f32[24,32,384]{2,1,0:T(8,128)S(1)} fusion(f32[24,32,384]{2,1,0:T(8,128)} %slice.132, f32[26,32,1152]{2,1,0:T(8,128)} %copy-done.2, bf16[1,24,32,384]{3,2,1,0:T(8,128)(2,1)S(1)} %copy-done.5), kind=kLoop, calls=%fused_computation.13 | loop fusion | flops 1769472 | bytes 6488064 | tf_op jit(solution)/shard_map/sub | solution.py:84
  66.1 0.2 fusion.76
  66.3 8.5 %all-to-all-done.2 = bf16[64,4,384]{2,1,0:T(4,128)(2,1)S(1)} async-done(((bf16[64,4,384]{2,1,0:T(4,128)(2,1)}), bf16[64,4,384]{2,1,0:T(4,128)(2,1)S(1)}, u32[]{:S(2)}, u32[]{:S(2)}) %all-to-all-start.2) | async-done | bytes 196640 | tf_op jit(solution)/shard_map/all_to_all | solution.py:31
  74.8 0.7 reshape.184
  75.6 1.2 fusion.73
  76.8 2.3 %fusion.92 = (bf16[24,32,384]{2,1,0:T(8,128)(2,1)S(1)}, f32[24,32,384]{2,1,0:T(8,128)}) fusion(f32[24,32,384]{2,1,0:T(8,128)S(1)} %fusion.73, bf16[1,24,32,384]{3,2,1,0:T(8,128)(2,1)} %param.18, f32[1,24,32,384]{3,2,1,0:T(8,128)S(1)} %copy-done.3), kind=kLoop, calls=%fused_computation.120 | loop fusion | flops 1179648 | bytes 4718592 | tf_op jit(solution)/shard_map/convert_element_type | solution.py:69
  79.1 0.8 copy-done.8
  79.9 0.3 convolution_convert_fusion
  80.2 0.7 reshape.186
  80.9 4.4 %all-to-all-start.3 = ((bf16[64,4,384]{2,1,0:T(4,128)(2,1)}), bf16[64,4,384]{2,1,0:T(4,128)(2,1)S(1)}, u32[]{:S(2)}, u32[]{:S(2)}) async-start(bf16[64,4,384]{2,1,0:T(4,128)(2,1)} %reshape.186), calls=%async_computation.3 | async-start | bytes 393216 | tf_op jit(solution)/shard_map/all_to_all | solution.py:31
  85.4 0.8 fusion.95
  86.1 4.2 %collective-permute-start.2 = (bf16[1,32,384]{2,1,0:T(8,128)(2,1)S(1)}, bf16[1,32,384]{2,1,0:T(8,128)(2,1)S(1)}, u32[]{:S(2)}, u32[]{:S(2)}) collective-permute-start(bf16[1,32,384]{2,1,0:T(8,128)(2,1)S(1)} %get-tuple-element.35), channel_id=1, source_target_pairs={{0,64},{64,128},{128,192},{1,65},{65,129},{129,193},{2,66},{66,130... | collective-permute-start | bytes 73736 | tf_op jit(solution)/shard_map/ppermute | solution.py:14
  90.4 1.5 %collective-permute-start.3 = (bf16[1,32,384]{2,1,0:T(8,128)(2,1)S(1)}, bf16[1,32,384]{2,1,0:T(8,128)(2,1)S(1)}, u32[]{:S(2)}, u32[]{:S(2)}) collective-permute-start(bf16[1,32,384]{2,1,0:T(8,128)(2,1)S(1)} %get-tuple-element.36), channel_id=1, source_target_pairs={{64,0},{128,64},{192,128},{65,1},{129,65},{193,129},{66,2},{130,66... | collective-permute-start | bytes 73736 | tf_op jit(solution)/shard_map/ppermute | solution.py:14
  91.9 3.4 %collective-permute-done.3 = bf16[1,32,384]{2,1,0:T(8,128)(2,1)S(1)} collective-permute-done((bf16[1,32,384]{2,1,0:T(8,128)(2,1)S(1)}, bf16[1,32,384]{2,1,0:T(8,128)(2,1)S(1)}, u32[]{:S(2)}, u32[]{:S(2)}) %collective-permute-start.3) | collective-permute-done | bytes 24608 | tf_op jit(solution)/shard_map/ppermute | solution.py:14
  95.3 2.5 %fusion.41 = f32[26,32,1152]{2,1,0:T(8,128)S(1)} fusion(bf16[1,32,384]{2,1,0:T(8,128)(2,1)S(1)} %collective-permute-done.3, bf16[24,32,384]{2,1,0:T(8,128)(2,1)} %copy-done.8, bf16[1,32,384]{2,1,0:T(8,128)(2,1)S(1)} %collective-permute-done.2, bf16[384,384]{1,0:T(8,128)(2,1)} %param.21, bf16[384,384]{1,0:T(8,128)(2,1)} %param.20, bf16[384,384]{1,0:T(8,128)(2,1)} %param.19), kind=kOutput, calls=%fused_computation.57 | convolution fusion | flops 739393536 | bytes 5357568 | tf_op jit(solution)/shard_map/dot_general | solution.py:20
  97.8 1.8 %copy-done.1 = f32[26,32,1152]{2,1,0:T(8,128)} copy-done((f32[26,32,1152]{2,1,0:T(8,128)}, f32[26,32,1152]{2,1,0:T(8,128)S(1)}, u32[]{:S(2)}) %copy-start.1) | copy-done | bytes 3833880
  99.6 1.1 slice.139
  100.8 0.2 convolution_convert_fusion.4
  101.1 0.1 copy.68
  101.3 4.5 %fusion.2 = f32[128,3,128]{2,1,0:T(4,128)S(1)} fusion(bf16[128,3,128]{2,1,0:T(4,128)(2,1)S(1)} %copy.68, bf16[1,1,128,128,128]{4,3,2,1,0:T(8,128)(2,1)} %param.22), kind=kOutput, calls=%fused_computation.2 | convolution fusion | flops 12582912 | bytes 4489216 | tf_op jit(solution)/shard_map/snm,scm->scn/dot_general | solution.py:76
  105.8 0.2 copy.70
  106.0 0.4 fusion.30
  106.4 0.1 copy.72
  106.6 3.4 %fusion.21 = bf16[128,3,128]{2,1,0:T(4,128)(2,1)S(1)} fusion(bf16[128,3,128]{2,1,0:T(4,128)(2,1)S(1)} %copy.72, bf16[1,1,128,128,128]{4,3,2,1,0:T(8,128)(2,1)} %param.22), kind=kOutput, calls=%fused_computation.34 | convolution fusion | flops 12681216 | bytes 4390912 | tf_op jit(solution)/shard_map/snm,scn->scm/dot_general | solution.py:80
  109.9 0.1 copy.73
  110.1 0.3 convolution_convert_fusion.2
  110.4 0.7 reshape.191
  111.2 11.5 %all-to-all-start.4 = ((bf16[64,4,384]{2,1,0:T(4,128)(2,1)}), bf16[64,4,384]{2,1,0:T(4,128)(2,1)S(1)}, u32[]{:S(2)}, u32[]{:S(2)}) async-start(bf16[64,4,384]{2,1,0:T(4,128)(2,1)} %reshape.191), calls=%async_computation.4 | async-start | bytes 393216 | tf_op jit(solution)/shard_map/all_to_all | solution.py:31
  122.7 3.3 %convert_subtract_fusion = f32[24,32,384]{2,1,0:T(8,128)S(1)} fusion(f32[24,32,384]{2,1,0:T(8,128)} %slice.139, f32[26,32,1152]{2,1,0:T(8,128)} %copy-done.1, bf16[1,24,32,384]{3,2,1,0:T(8,128)(2,1)S(1)} %copy-done.5), kind=kLoop, calls=%fused_computation.12 | loop fusion | flops 1769472 | bytes 6488064 | tf_op jit(solution)/shard_map/sub | solution.py:84
  126.0 0.2 fusion.77
  126.2 8.5 %all-to-all-done.4 = bf16[64,4,384]{2,1,0:T(4,128)(2,1)S(1)} async-done(((bf16[64,4,384]{2,1,0:T(4,128)(2,1)}), bf16[64,4,384]{2,1,0:T(4,128)(2,1)S(1)}, u32[]{:S(2)}, u32[]{:S(2)}) %all-to-all-start.4) | async-done | bytes 196640 | tf_op jit(solution)/shard_map/all_to_all | solution.py:31
  134.8 0.3 fusion.72
  135.1 1.2 fusion.10
  (42 shorter events, 0.8 us)
Async XLA Ops:
  0.0 35.1 %copy-start = (f32[1,1,32,384]{3,2,1,0:T(8,128)S(1)}, f32[1,1,32,384]{3,2,1,0:T(8,128)}, u32[]{:S(2)}) copy-start(f32[1,1,32,384]{3,2,1,0:T(8,128)} %param.24) | copy-start | bytes 147460
  3.1 22.3 %all-to-all-start = ((s32[64,4,1]{1,2,0:T(1,128)}), s32[64,4,1]{1,2,0:T(1,128)S(1)}, u32[]{:S(2)}, u32[]{:S(2)}) async-start(s32[64,4,1]{1,2,0:T(1,128)} %bitcast.11), calls=%async_computation | async-start | bytes 65536 | tf_op jit(solution)/shard_map/all_to_all | solution.py:31
  16.1 19.0 %copy-start.10 = (s32[1,1,128]{2,1,0:T(1,128)S(1)}, s32[1,1,128]{2,1,0:T(1,128)}, u32[]{:S(2)}) copy-start(s32[1,1,128]{2,1,0:T(1,128)} %param.25) | copy-start | bytes 1540
  16.1 19.4 %copy-start.9 = (f32[1,1,128,128]{3,2,1,0:T(8,128)S(1)}, f32[1,1,128,128]{3,2,1,0:T(8,128)}, u32[]{:S(2)}) copy-start(f32[1,1,128,128]{3,2,1,0:T(8,128)} %param.23) | copy-start | bytes 196612
  17.5 18.1 %copy-start.11 = (bf16[384,384]{1,0:T(8,128)(2,1)S(1)}, bf16[384,384]{1,0:T(8,128)(2,1)}, u32[]{:S(2)}) copy-start(bf16[384,384]{1,0:T(8,128)(2,1)} %param.21) | copy-start | bytes 884740
  17.5 18.1 %copy-start.12 = (bf16[384,384]{1,0:T(8,128)(2,1)S(1)}, bf16[384,384]{1,0:T(8,128)(2,1)}, u32[]{:S(2)}) copy-start(bf16[384,384]{1,0:T(8,128)(2,1)} %param.20) | copy-start | bytes 884740
  17.5 18.1 %copy-start.13 = (bf16[384,384]{1,0:T(8,128)(2,1)S(1)}, bf16[384,384]{1,0:T(8,128)(2,1)}, u32[]{:S(2)}) copy-start(bf16[384,384]{1,0:T(8,128)(2,1)} %param.19) | copy-start | bytes 884740
  17.5 18.1 %collective-permute-start = (bf16[1,32,384]{2,1,0:T(8,128)(2,1)S(1)}, bf16[1,32,384]{2,1,0:T(8,128)(2,1)S(1)}, u32[]{:S(2)}, u32[]{:S(2)}) collective-permute-start(bf16[1,32,384]{2,1,0:T(8,128)(2,1)S(1)} %get-tuple-element.37), channel_id=1, source_target_pairs={{0,64},{64,128},{128,192},{1,65},{65,129},{129,193},{2,66},{66,130... | collective-permute-start | bytes 73736 | tf_op jit(solution)/shard_map/ppermute | solution.py:14
  20.9 14.7 %collective-permute-start.1 = (bf16[1,32,384]{2,1,0:T(8,128)(2,1)S(1)}, bf16[1,32,384]{2,1,0:T(8,128)(2,1)S(1)}, u32[]{:S(2)}, u32[]{:S(2)}) collective-permute-start(bf16[1,32,384]{2,1,0:T(8,128)(2,1)S(1)} %get-tuple-element.38), channel_id=1, source_target_pairs={{64,0},{128,64},{192,128},{65,1},{129,65},{193,129},{66,2},{130,66... | collective-permute-start | bytes 73736 | tf_op jit(solution)/shard_map/ppermute | solution.py:14
  27.7 19.4 %all-to-all-start.1 = ((bf16[64,4,384]{2,1,0:T(4,128)(2,1)}), bf16[64,4,384]{2,1,0:T(4,128)(2,1)S(1)}, u32[]{:S(2)}, u32[]{:S(2)}) async-start(bf16[64,4,384]{2,1,0:T(4,128)(2,1)} %reshape.178), calls=%async_computation.1 | async-start | bytes 393216 | tf_op jit(solution)/shard_map/all_to_all | solution.py:31
  36.9 1.8 %copy-start.2 = (f32[26,32,1152]{2,1,0:T(8,128)}, f32[26,32,1152]{2,1,0:T(8,128)S(1)}, u32[]{:S(2)}) copy-start(f32[26,32,1152]{2,1,0:T(8,128)S(1)} %fusion.35) | copy-start | bytes 11501572
  47.7 4.7 %copy-start.3 = (f32[1,24,32,384]{3,2,1,0:T(8,128)S(1)}, f32[1,24,32,384]{3,2,1,0:T(8,128)}, u32[]{:S(2)}) copy-start(f32[1,24,32,384]{3,2,1,0:T(8,128)} %param.16) | copy-start | bytes 3538948
  57.0 5.7 %copy-start.5 = (bf16[1,24,32,384]{3,2,1,0:T(8,128)(2,1)S(1)}, bf16[1,24,32,384]{3,2,1,0:T(8,128)(2,1)}, u32[]{:S(2)}) copy-start(bf16[1,24,32,384]{3,2,1,0:T(8,128)(2,1)} %param.17) | copy-start | bytes 1769476
  58.2 16.6 %all-to-all-start.2 = ((bf16[64,4,384]{2,1,0:T(4,128)(2,1)}), bf16[64,4,384]{2,1,0:T(4,128)(2,1)S(1)}, u32[]{:S(2)}, u32[]{:S(2)}) async-start(bf16[64,4,384]{2,1,0:T(4,128)(2,1)} %reshape.183), calls=%async_computation.2 | async-start | bytes 393216 | tf_op jit(solution)/shard_map/all_to_all | solution.py:31
  62.7 3.3 %copy-start.7 = (f32[128,3,128]{0,2,1:T(8,128)S(1)}, f32[128,3,128]{0,2,1:T(8,128)}, u32[]{:S(2)}) copy-start(f32[128,3,128]{0,2,1:T(8,128)} %get-tuple-element.34) | copy-start | bytes 589828
  79.1 0.8 copy-start.8
  80.9 19.8 %all-to-all-start.3 = ((bf16[64,4,384]{2,1,0:T(4,128)(2,1)}), bf16[64,4,384]{2,1,0:T(4,128)(2,1)S(1)}, u32[]{:S(2)}, u32[]{:S(2)}) async-start(bf16[64,4,384]{2,1,0:T(4,128)(2,1)} %reshape.186), calls=%async_computation.3 | async-start | bytes 393216 | tf_op jit(solution)/shard_map/all_to_all | solution.py:31
  86.1 5.7 %collective-permute-start.2 = (bf16[1,32,384]{2,1,0:T(8,128)(2,1)S(1)}, bf16[1,32,384]{2,1,0:T(8,128)(2,1)S(1)}, u32[]{:S(2)}, u32[]{:S(2)}) collective-permute-start(bf16[1,32,384]{2,1,0:T(8,128)(2,1)S(1)} %get-tuple-element.35), channel_id=1, source_target_pairs={{0,64},{64,128},{128,192},{1,65},{65,129},{129,193},{2,66},{66,130... | collective-permute-start | bytes 73736 | tf_op jit(solution)/shard_map/ppermute | solution.py:14
  90.4 4.9 %collective-permute-start.3 = (bf16[1,32,384]{2,1,0:T(8,128)(2,1)S(1)}, bf16[1,32,384]{2,1,0:T(8,128)(2,1)S(1)}, u32[]{:S(2)}, u32[]{:S(2)}) collective-permute-start(bf16[1,32,384]{2,1,0:T(8,128)(2,1)S(1)} %get-tuple-element.36), channel_id=1, source_target_pairs={{64,0},{128,64},{192,128},{65,1},{129,65},{193,129},{66,2},{130,66... | collective-permute-start | bytes 73736 | tf_op jit(solution)/shard_map/ppermute | solution.py:14
  97.8 1.8 %copy-start.1 = (f32[26,32,1152]{2,1,0:T(8,128)}, f32[26,32,1152]{2,1,0:T(8,128)S(1)}, u32[]{:S(2)}) copy-start(f32[26,32,1152]{2,1,0:T(8,128)S(1)} %fusion.41) | copy-start | bytes 11501572
  101.3 4.7 %copy-start.4 = (f32[24,32,384]{2,1,0:T(8,128)S(1)}, f32[24,32,384]{2,1,0:T(8,128)}, u32[]{:S(2)}) copy-start(f32[24,32,384]{2,1,0:T(8,128)} %get-tuple-element.32) | copy-start | bytes 3538948
  111.2 23.6 %all-to-all-start.4 = ((bf16[64,4,384]{2,1,0:T(4,128)(2,1)}), bf16[64,4,384]{2,1,0:T(4,128)(2,1)S(1)}, u32[]{:S(2)}, u32[]{:S(2)}) async-start(bf16[64,4,384]{2,1,0:T(4,128)(2,1)} %reshape.191), calls=%async_computation.4 | async-start | bytes 393216 | tf_op jit(solution)/shard_map/all_to_all | solution.py:31
  126.0 9.1 %copy-start.6 = (bf16[1,24,32,384]{3,2,1,0:T(8,128)(2,1)S(1)}, bf16[1,24,32,384]{3,2,1,0:T(8,128)(2,1)}, u32[]{:S(2)}) copy-start(bf16[1,24,32,384]{3,2,1,0:T(8,128)(2,1)} %param.18) | copy-start | bytes 1769476

commit v2 on v1

v2 whole, which is shorter than its diff:
```python
import jax
import jax.numpy as jnp
from jax import lax
from jax.experimental import pallas as pl
from jax.experimental.pallas import tpu as pltpu
from jax.sharding import PartitionSpec as P

PENALTY = 2.0
CAPACITY = 4
GROUP = 16
PARTS = 2
VMEM = pltpu.VMEM
HBM = pl.BlockSpec(memory_space=pltpu.HBM)
BF16 = jnp.bfloat16
F32 = jnp.float32


def dot(a, b, dims=((1,), (0,))):
    return lax.dot_general(a, b, (dims, ((), ())), preferred_element_type=F32)


def iota(shape, axis):
    return lax.broadcasted_iota(jnp.int32, shape, axis)


def shaped(shape, dtype):
    return jax.ShapeDtypeStruct(shape, dtype)


def in_hbm(*arrays):
    return [pltpu.with_memory_space_constraint(array, pltpu.HBM) for array in arrays]


def staged(body, ins, outs, scratch=(), tokens=(), loose=(), free_outs=False):
    ins = [item if isinstance(item, tuple) else (item, ()) for item in ins]
    operands = [array if i in loose else in_hbm(array)[0] for i, (array, _) in enumerate(ins)]
    held = [VMEM(part_shape(array, index), array.dtype) for array, index in ins]
    given = [VMEM(out.shape, out.dtype) for out in outs]

    def kernel(*refs):
        refs = list(refs)

        def pop(count):
            taken = refs[:count]
            del refs[:count]
            return taken

        sources, _, targets = pop(len(ins)), pop(len(tokens)), pop(len(outs))
        inside, leaving, (in_sems, out_sems), extra = pop(len(ins)), pop(len(outs)), pop(2), refs
        loads = {}
        for i, (source, ref, (_, index)) in enumerate(zip(sources, inside, ins)):
            loads[i] = pltpu.make_async_copy(source.at[index] if index else source, ref, in_sems.at[i])
            loads[i].start()

        def take(i):
            if i in loads:
                loads.pop(i).wait()
            return inside[i]

        stores = []

        def give(i, index=None):
            source, target = leaving[i], targets[i]
            if index is not None:
                source, target = source.at[index], target.at[index]
            stores.append(pltpu.make_async_copy(source, target, out_sems.at[i]))
            stores[-1].start()

        body(take, leaving, give, *extra)
        assert not loads
        for store in stores:
            store.wait()

    sems = [pltpu.SemaphoreType.DMA((len(ins),)), pltpu.SemaphoreType.DMA((len(outs),))]
    return pl.pallas_call(
        kernel,
        out_shape=tuple(out if free_outs else pltpu.HBM(out.shape, out.dtype) for out in outs),
        in_specs=[pl.BlockSpec(memory_space=pl.ANY)] * (len(ins) + len(tokens)),
        out_specs=(pl.BlockSpec(memory_space=pl.ANY),) * len(outs),
        scratch_shapes=held + given + sems + list(scratch),
        compiler_params=pltpu.CompilerParams(vmem_limit_bytes=32 * 2**20),
    )(*operands, *tokens)


def part_shape(array, index):
    kept = [i.size for i in index if not isinstance(i, int)]
    return tuple(kept) + array.shape[len(index) :]


def slots_of(src, count):
    segs = src.shape[1]
    named = (iota((count, segs), 0) == src).astype(BF16)
    earlier = (iota((segs, segs), 0) < iota((segs, segs), 1)).astype(BF16)
    before = dot(named, earlier)
    rank = jnp.sum(named.astype(F32) * before, axis=0, keepdims=True).astype(jnp.int32)
    return named, rank


def request_kernel(blocks, take, out, give):
    src, master = take(0)[0], take(1)[0]
    count = out[0].shape[0]
    named, rank = slots_of(src, count)
    segs = named.shape[1]
    wants = (iota((CAPACITY * blocks, segs), 0) == rank * blocks + master).astype(BF16)
    out[0][...] = dot(named, wants, ((1,), (1,)))
    give(0)


def split3(rows):
    high = rows.astype(BF16)
    rest = rows - high.astype(F32)
    mid = rest.astype(BF16)
    low = (rest - mid.astype(F32)).astype(BF16)
    return jnp.concatenate([high, mid, low], axis=0)


def prep_kernel(take, out, give):
    put_ref, get_ref, take_ref, sum_ref, normal_rows_ref, low_ref, high_ref = out
    high_ref[...] = take(3)[...].astype(BF16)
    low_ref[...] = take(4)[...].astype(BF16)
    give(5)
    give(6)
    src, slave, normals = take(0)[0], take(1)[0], take(2)[...]
    blocks = normals.shape[0]
    slots, segs = put_ref.shape
    _, rank = slots_of(src, slots // CAPACITY)
    put = (iota((slots, segs), 0) == src * CAPACITY + rank).astype(F32)
    put_ref[...] = put.astype(BF16)
    give(0)
    get_ref[...] = jnp.transpose(put).astype(BF16)
    give(1)
    spread = (lax.rem(iota((4 * blocks, segs), 0), blocks) == slave).astype(F32)
    pick = jnp.transpose(spread)[:, : 3 * blocks].astype(BF16)
    take_ref[...] = pick
    give(2)
    once = spread[:blocks].astype(BF16)
    sum_ref[...] = jnp.concatenate([once, once], axis=1)
    give(3)
    normal_rows_ref[...] = dot(pick, split3(normals))
    give(4)


def place(rows, scratch, out_ref):
    scratch[...] = rows
    for i in range(out_ref.shape[0]):
        out_ref[i] = scratch[CAPACITY * i : CAPACITY * (i + 1), :].astype(BF16)


def gathered(in_ref, scratch):
    for i in range(in_ref.shape[0]):
        scratch[CAPACITY * i : CAPACITY * (i + 1), :] = in_ref[i].astype(F32)
    return scratch[...].astype(BF16)


def copies(rows):
    return jnp.concatenate([rows] * CAPACITY, axis=0)


def first_kernel(take, out, give, scratch):
    pick_ref, out_ref = out
    slots, wide = pick_ref.shape
    count, blocks = slots // CAPACITY, wide // CAPACITY
    expand = (lax.div(iota((slots, count), 0), CAPACITY) == iota((slots, count), 1)).astype(BF16)
    mine = lax.div(iota((slots, wide), 1), blocks) == lax.rem(iota((slots, wide), 0), CAPACITY)
    rows = dot(expand, take(0)[...].astype(BF16))
    pick = jnp.where(mine, rows, 0.0).astype(BF16)
    pick_ref[...] = pick
    give(0)
    place(dot(pick, copies(take(1)[...].astype(BF16))), scratch, out_ref)
    give(1)


def contact_kernel(take, out, give, scratch, back_ref):
    out_ref, pushed_ref = out
    segs = back_ref.shape[0]
    nodes = back_ref.shape[1] // 3
    member = lax.rem(iota((3 * GROUP, nodes), 0), GROUP)
    place_in = lax.rem(member, 4)
    block_of = lax.div(member, 4)
    odd = lax.rem(place_in, 2) == 1
    late = place_in >= 2
    zero = jnp.zeros((3 * GROUP, nodes), BF16)
    slave = dot(take(3)[...], split3(take(4)[...]))
    arrived = gathered(take(0), scratch)
    master = dot(take(1)[...], arrived).astype(BF16)
    normal_ref, gap_ref = take(5), take(6)

    def columns(rows):
        return [rows[:, c * nodes : (c + 1) * nodes] for c in range(3)]

    def choose(parts):
        result = parts[0]
        for b in range(1, GROUP // 4):
            result = jnp.where(block_of == b, parts[b], result)
        return result

    for g in range(segs // GROUP):
        own = slice(GROUP * g, GROUP * (g + 1))
        um = jnp.concatenate(columns(master[own]), axis=0)
        us = jnp.concatenate(columns(slave[own]), axis=0)
        normal = jnp.concatenate(columns(normal_ref[own, :]), axis=0)
        mortar_ref = take(7 + g)
        weights = []
        for s in range(0, GROUP, 4):
            left = mortar_ref[s : s + 2].reshape(2 * nodes, nodes)
            right = mortar_ref[s + 2 : s + 4].reshape(2 * nodes, nodes)
            weights.append(jnp.concatenate([left, right], axis=1))
        lhs = jnp.concatenate([jnp.where(late, zero, um), jnp.where(late, um, zero)], axis=1)
        parts = []
        for w in weights:
            r = dot(lhs, w, ((1,), (1,)))
            parts.append(jnp.where(odd, r[:, nodes:], r[:, :nodes]))
        mapped = choose(parts)
        terms = normal * (mapped - us)
        gap = gap_ref[own, :] + (terms[:GROUP] + terms[GROUP : 2 * GROUP] + terms[2 * GROUP :])
        pressure = PENALTY * jnp.maximum(-gap, 0.0)
        pushed = jnp.concatenate([pressure] * 3, axis=0) * normal
        high = pushed.astype(BF16)
        rest = (pushed - high.astype(F32)).astype(BF16)
        lhs = jnp.concatenate([jnp.where(odd, zero, high), jnp.where(odd, high, zero)], axis=1)
        parts = []
        for w in weights:
            r = dot(lhs, w)
            parts.append(jnp.where(late, r[:, nodes:], r[:, :nodes]))
        back = (-choose(parts)).astype(BF16)
        for c in range(3):
            rows = slice(GROUP * c, GROUP * (c + 1))
            cols = slice(nodes * c, nodes * (c + 1))
            back_ref[own, cols] = back[rows]
            pushed_ref[own, cols] = high[rows]
            pushed_ref[segs + GROUP * g : segs + GROUP * (g + 1), cols] = rest[rows]
    give(1)
    place(dot(take(2)[...], back_ref[...]), scratch, out_ref)
    give(0)


def bulk_kernel(take, out, give, rounded_ref, product_ref):
    out_ref, base_ref, *last_refs = out
    _, layers, blocks, width = out_ref.shape
    rows = layers * blocks
    step = (rows + 2 * blocks) // PARTS
    low_ref, high_ref, field_ref, layer_ref = take(0), take(1), take(2), take(3)
    rounded_ref[:blocks] = low_ref[...]
    rounded_ref[blocks : 2 * blocks] = layer_ref[...].astype(BF16)
    for l in range(1, layers):
        rounded_ref[(l + 1) * blocks : (l + 2) * blocks] = field_ref[0, l].astype(BF16)
    rounded_ref[rows + blocks :] = high_ref[...]
    weight_refs = [take(i) for i in (4, 5, 6)]

    @pl.loop(0, PARTS)
    def multiply(p):
        here = pl.ds(pl.multiple_of(p * step, 16), step)
        part = rounded_ref[here]
        for k, weight_ref in enumerate(weight_refs):
            product_ref[here, k * width : (k + 1) * width] = dot(part, weight_ref[...])

    block = iota((blocks, width), 0)

    def inner(l):
        def product(layer, k):
            return product_ref[pl.ds(pl.multiple_of(layer * blocks, blocks), blocks), k * width : (k + 1) * width]

        side = product(l + 1, 2)
        left = jnp.where(block == 0, 0.0, pltpu.roll(side, 1, 0))
        right = jnp.where(block == blocks - 1, 0.0, pltpu.roll(side, blocks - 1, 0))
        return product(l + 1, 0) + (product(l, 1) + product(l + 2, 1)) + (left + right)

    load_ref, scale_ref = take(7), take(8)

    def stepped(old, l, force):
        return old + scale_ref[0, l].astype(F32) * (load_ref[0, l].astype(F32) - force)

    base_ref[...] = stepped(layer_ref[...], 0, inner(0) + dot(take(10)[...], take(9)[...]))
    give(1)

    @pl.loop(1, layers)
    def update(l):
        out_ref[0, l] = stepped(field_ref[0, l], l, inner(l))

    give(0, (0, pl.ds(1, layers - 1)))
    for last_ref in last_refs:
        last_ref[...] = out_ref[0, layers - 1].astype(BF16)
        give(2)


def summed(take, scratch):
    sums = dot(take(1)[...], gathered(take(0), scratch), ((0,), (0,)))
    base, scale = take(2)[...], take(3)[...].astype(F32)
    blocks = base.shape[0]
    total = sums[:blocks]
    for k in range(1, CAPACITY):
        total = total + sums[k * blocks : (k + 1) * blocks]
    return base - scale * total


def next_kernel(take, out, give, scratch):
    out_ref, layer_ref, high_ref = out
    first = summed(take, scratch)
    layer_ref[...] = first
    give(1)
    surface = first.astype(BF16)
    high_ref[...] = surface
    give(2)
    place(dot(take(1)[...], copies(surface)), scratch, out_ref)
    give(0)


def last_kernel(in_hbm, pick_hbm, base_hbm, scale_hbm, field_hbm, out_hbm, in_ref, pick_ref, base_ref, scale_ref, scratch, layer_ref, sems):
    pairs = [(in_hbm, in_ref), (pick_hbm, pick_ref), (base_hbm, base_ref), (scale_hbm.at[0, 0], scale_ref)]
    loads = {i: pltpu.make_async_copy(source, ref, sems.at[i]) for i, (source, ref) in enumerate(pairs)}
    for load in loads.values():
        load.start()

    def take(i):
        loads[i].wait()
        return pairs[i][1]

    layer_ref[...] = summed(take, scratch)
    store = pltpu.make_async_copy(layer_ref, out_hbm.at[0, 0], sems.at[4])
    store.start()
    store.wait()


def shift(block, step):
    count = lax.axis_size("slab")
    pairs = [(i, i + step) for i in range(count) if 0 <= i + step < count]
    return lax.ppermute(block, "slab", pairs)


def exchange(parts):
    return lax.all_to_all(parts, "dom", 0, 0, tiled=True)


def on_device(
    disp, f_ext, inv_diag, k_self, k_layer, k_side, mortar, gap0, normals, seg_slave, seg_src, seg_master
):
    _, layers, blocks, width = disp.shape
    segs = seg_slave.shape[2]
    count = lax.axis_size("dom")
    slots = count * CAPACITY
    wide = CAPACITY * blocks
    rows_scratch = VMEM((slots, width), F32)
    message = shaped((count, CAPACITY, width), BF16)
    edge = shaped((blocks, width), BF16)
    layer = shaped((blocks, width), F32)

    (asked,) = staged(
        lambda *refs: request_kernel(blocks, *refs), [seg_src, seg_master], [shaped((count, wide), F32)], free_outs=True
    )
    put, get, pick3, back_sum, normal_rows, low, high = staged(
        prep_kernel,
        [seg_src, seg_slave, (normals, (0, 0)), (disp, (0, 0)), (disp, (0, layers - 1))],
        [
            shaped((slots, segs), BF16),
            shaped((segs, slots), BF16),
            shaped((segs, 3 * blocks), BF16),
            shaped((blocks, 2 * segs), BF16),
            shaped((segs, width), F32),
            edge,
            edge,
        ],
        tokens=[asked],
    )
    asked = exchange(asked.reshape(count, 1, wide)).reshape(count, wide)
    pick, sent = staged(
        first_kernel, [asked, (disp, (0, 0))], [shaped((slots, wide), BF16), message], [rows_scratch], tokens=in_hbm(put), loose=(0,)
    )

    def contact(arrived, layer0, low, high):
        pieces = [(mortar, (0, 0, pl.ds(GROUP * g, GROUP))) for g in range(segs // GROUP)]
        return staged(
            contact_kernel,
            [arrived, get, put, pick3, layer0, normal_rows, (gap0, (0, 0))] + pieces,
            [message, shaped((2 * segs, width), BF16)],
            [rows_scratch, VMEM((segs, width), BF16)],
            tokens=[low, high],
        )

    def bulk(field, layer0, low, high, pushed, keep_last):
        outs = [shaped(disp.shape, F32), layer] + ([edge] if keep_last else [])
        rows = (layers + 2) * blocks
        return staged(
            bulk_kernel,
            [low, high, field, layer0, k_self, k_layer, k_side, f_ext, inv_diag, pushed, back_sum],
            outs,
            [VMEM((rows, width), BF16), VMEM((rows, 3 * width), F32)],
            loose=(0, 1),
        )

    arrived = exchange(sent)
    low, high = shift(low, 1), shift(high, -1)
    sent, pushed = contact(arrived, (disp, (0, 0)), low, high)
    returned = exchange(sent)
    field, base, last = bulk(disp, (disp, (0, 0)), low, high, pushed, True)
    sent, layer0, high = staged(
        next_kernel, [returned, pick, base, (inv_diag, (0, 0))], [message, layer, edge], [rows_scratch]
    )
    arrived = exchange(sent)
    low, high = shift(last, 1), shift(high, -1)
    sent, pushed = contact(arrived, layer0, low, high)
    returned = exchange(sent)
    field, base = bulk(field, layer0, low, high, pushed, False)
    return pl.pallas_call(
        last_kernel,
        out_shape=pltpu.HBM(disp.shape, F32),
        in_specs=[HBM] * 5,
        out_specs=HBM,
        scratch_shapes=[
            VMEM(message.shape, BF16),
            VMEM(pick.shape, BF16),
            VMEM(base.shape, F32),
            VMEM(base.shape, BF16),
            rows_scratch,
            VMEM(base.shape, F32),
            pltpu.SemaphoreType.DMA((5,)),
        ],
        input_output_aliases={4: 0},
        compiler_params=pltpu.CompilerParams(vmem_limit_bytes=32 * 2**20),
    )(*in_hbm(returned, pick, base, inv_diag, field))


def solution(mesh):
    in_specs = (
        P("dom", "slab", None, None),
        P("dom", "slab", None, None),
        P("dom", "slab", None, None),
        P(),
        P(),
        P(),
        P("dom", "slab", None, None, None),
        P("dom", "slab", None, None),
        P("dom", "slab", None, None),
        P("dom", "slab", None),
        P("dom", "slab", None),
        P("dom", "slab", None),
    )
    return jax.shard_map(
        on_device, mesh=mesh, in_specs=in_specs, out_specs=P("dom", "slab", None, None), check_vma=False
    )
```

time: 137 us -> 118 us (0.86)
  Pallas kernels: 0 us -> 31.9 us
  matrix products: 24.1 us -> 0 us
  other arithmetic: 15.4 us -> 0 us
  local copies, waits for them, and re-layouts: 14.1 us -> 2.71 us
  waiting for transfers between devices: 31 us -> 36.3 us
  starting transfers between devices: 51.1 us -> 46.3 us
    pallas_call x0 -> x9, Pallas kernels: none -> 31.9 us  [the longest x8 30.1 us: staged(): pl.pallas_call(kernel, out_shape=tuple((out if free_outs else pltpu.HBM(o...]
    dot_general x19 -> x0, matrix products: 24.1 us -> none  [the longest x2 9.05 us: on_device(): jnp.einsum('snm,scm->scn', mortar_own, master_rows, preferred_element_typ...]
    sub x3 -> x0, other arithmetic: 6.64 us -> none  [the longest x2 6.64 us: on_device(): residual = load - internal]
    convert_element_type x4 -> x0, other arithmetic: 4.44 us -> none  [the longest x2 3.72 us: on_device(): rounded = field.astype(bf16)]
    reshape x10 -> x0, local copies, waits for them, and re-layouts: 4.09 us -> none  [the longest x4 2.93 us: exchange(): parts = rows.reshape(domains, CAPACITY, -1)]
    ppermute x4, waiting for transfers between devices: 3.38 us -> 7.33 us  [shift(): return lax.ppermute(block, 'slab', pairs)]
    all_to_all x5, starting transfers between devices: 40.8 us -> 37.3 us  [exchange(): return lax.all_to_all(parts, 'dom', 0, 0, tiled=True)]
    slice x4 -> x0, local copies, waits for them, and re-layouts: 2.97 us -> none  [the longest x2 2.2 us: stiffness(): prod[1:-1, :, 2 * width:]]
  transfers between devices with their start and end apart: 9 -> 9, of which waited for: 5 -> 7; matrix products, arithmetic and copies ran while one was open for 13% -> 0% of each run, Pallas kernels for 0% -> 11%
where the time goes in v2:
time: 118 us; the launch traced here: 117 us
  starting transfers between devices  46.3 us (39%)
  waiting for transfers between devices  36.3 us (31%)
  Pallas kernels  31.9 us (27%)
  local copies, waits for them, and re-layouts  2.71 us (2%)
    all_to_all x5, starting transfers between devices, exchange(): return lax.all_to_all(parts, 'dom', 0, 0, tiled=True)  37.3 us
    pallas_call x8, Pallas kernels, staged(): pl.pallas_call(kernel, out_shape=tuple((out if free_outs else pltpu.HBM(o...  30.1 us
    all_to_all x5, waiting for transfers between devices, exchange(): return lax.all_to_all(parts, 'dom', 0, 0, tiled=True)  29 us
    ppermute x4, starting transfers between devices, shift(): return lax.ppermute(block, 'slab', pairs)  9 us
    ppermute x4, waiting for transfers between devices, shift(): return lax.ppermute(block, 'slab', pairs)  7.33 us
    unnamed x14, local copies, waits for them, and re-layouts  2.71 us
  transfers between devices with their start and end apart: 9, of which 7 were waited for; matrix products, arithmetic and copies ran while one was open for 0% of the time, Pallas kernels for 11%

profile of v2, /device:TPU:1, one launch (start us, length us, event | category | flops | bytes accessed | tf_op | source)
XLA Modules:
  0.0 117.4 jit_solution(7113429202314321462)
XLA Ops:
  0.0 1.6 %shard_map.118.refs_5_ = f32[64,128]{1,0:T(8,128)} custom-call(s32[1,1,128]{2,1,0:T(1,128)} %refs_0_.3, s32[1,1,128]{2,1,0:T(1,128)} %refs_1_.3), custom_call_target="tpu_custom_call" | custom-call | tf_op jit(solution)/shard_map/pallas_call | solution.py:75
  1.6 13.0 %all-to-all-start = ((f32[64,1,128]{2,1,0:T(1,128)}), f32[64,1,128]{2,1,0:T(1,128)S(1)}, u32[]{:S(2)}, u32[]{:S(2)}) async-start(f32[64,1,128]{2,1,0:T(1,128)} %bitcast.1), calls=%async_computation | async-start | bytes 65536 | tf_op jit(solution)/shard_map/all_to_all | solution.py:331
  14.6 2.0 %shard_map.119 = (bf16[256,128]{1,0:T(8,128)(2,1)}, bf16[128,256]{1,0:T(8,128)(2,1)}, bf16[128,96]{1,0:T(8,128)(2,1)}, bf16[32,256]{1,0:T(8,128)(2,1)}, f32[128,...) custom-call(s32[1,1,128]{2,1,0:T(1,128)} %refs_0_.3, s32[1,1,128]{2,1,0:T(1,128)} %refs_1_.4, ...), custom_call_target="tpu_custom_call" | custom-call | tf_op jit(solution)/shard_map/pallas_call | solution.py:75
  16.6 0.0 copy-start.6
  16.6 0.0 copy-start.4
  16.6 7.4 %all-to-all-done = f32[64,1,128]{2,1,0:T(1,128)S(1)} async-done(((f32[64,1,128]{2,1,0:T(1,128)}), f32[64,1,128]{2,1,0:T(1,128)S(1)}, u32[]{:S(2)}, u32[]{:S(2)}) %all-to-all-start) | async-done | bytes 32800 | tf_op jit(solution)/shard_map/all_to_all | solution.py:331
  24.0 1.8 %shard_map.120 = (bf16[256,128]{1,0:T(8,128)(2,1)}, bf16[64,4,384]{2,1,0:T(4,128)(2,1)}) custom-call(f32[64,128]{1,0:T(8,128)S(1)} %bitcast.4, f32[1,24,32,384]{3,2,1,0:T(8,128)} %refs_3_.4, bf16[256,128]{1,0:T(8,128)(2,1)} %get-tuple-element.26.refs_2_), custom_call_target="tpu_custom_call" | custom-call | tf_op jit(solution)/shard_map/pallas_call | solution.py:75
  25.8 4.7 %all-to-all-start.1 = ((bf16[64,4,384]{2,1,0:T(4,128)(2,1)}), bf16[64,4,384]{2,1,0:T(4,128)(2,1)S(1)}, u32[]{:S(2)}, u32[]{:S(2)}) async-start(bf16[64,4,384]{2,1,0:T(4,128)(2,1)} %get-tuple-element.27), calls=%async_computation.1 | async-start | bytes 393216 | tf_op jit(solution)/shard_map/all_to_all | solution.py:331
  30.5 0.0 copy-done.6
  30.5 3.2 %collective-permute-start = (bf16[32,384]{1,0:T(8,128)(2,1)S(1)}, bf16[32,384]{1,0:T(8,128)(2,1)S(1)}, u32[]{:S(2)}, u32[]{:S(2)}) collective-permute-start(bf16[32,384]{1,0:T(8,128)(2,1)S(1)} %copy-done.6), channel_id=1, source_target_pairs={{0,64},{64,128},{128,192},{1,65},{65,129},{129,193},{2,66},{66,130... | collective-permute-start | bytes 73736 | tf_op jit(solution)/shard_map/ppermute | solution.py:327
  33.7 0.0 copy-done.4
  33.7 1.3 %collective-permute-start.1 = (bf16[32,384]{1,0:T(8,128)(2,1)S(1)}, bf16[32,384]{1,0:T(8,128)(2,1)S(1)}, u32[]{:S(2)}, u32[]{:S(2)}) collective-permute-start(bf16[32,384]{1,0:T(8,128)(2,1)S(1)} %copy-done.4), channel_id=1, source_target_pairs={{64,0},{128,64},{192,128},{65,1},{129,65},{193,129},{66,2},{130,66... | collective-permute-start | bytes 73736 | tf_op jit(solution)/shard_map/ppermute | solution.py:327
  35.0 0.0 collective-permute-done.refs_15_.refs_0_
  35.0 3.6 %collective-permute-done.1.refs_16_.refs_1_ = bf16[32,384]{1,0:T(8,128)(2,1)S(1)} collective-permute-done((bf16[32,384]{1,0:T(8,128)(2,1)S(1)}, bf16[32,384]{1,0:T(8,128)(2,1)S(1)}, u32[]{:S(2)}, u32[]{:S(2)}) %collective-permute-start.1) | collective-permute-done | bytes 24608 | tf_op jit(solution)/shard_map/ppermute | solution.py:327
  38.6 4.1 %all-to-all-done.1.refs_0_ = bf16[64,4,384]{2,1,0:T(4,128)(2,1)S(1)} async-done(((bf16[64,4,384]{2,1,0:T(4,128)(2,1)}), bf16[64,4,384]{2,1,0:T(4,128)(2,1)S(1)}, u32[]{:S(2)}, u32[]{:S(2)}) %all-to-all-start.1) | async-done | bytes 196640 | tf_op jit(solution)/shard_map/all_to_all | solution.py:331
  42.6 0.0 copy-start.1
  42.6 0.7 copy-done.1
  43.3 6.1 %shard_map.121 = (bf16[64,4,384]{2,1,0:T(4,128)(2,1)}, bf16[256,384]{1,0:T(8,128)(2,1)}) custom-call(bf16[64,4,384]{2,1,0:T(4,128)(2,1)} %copy-done.1, bf16[128,256]{1,0:T(8,128)(2,1)} %get-tuple-element.28.refs_1_, bf16[256,128]{1,0:T(8,128)(2,1)} %get-tuple-element.26.refs_2_, bf16[128,96]{1,0:T(8,128)(2,1)} %get-tuple-element.29.refs_3_, ...), custom_call_target="tpu_custom_call" | custom-call | tf_op jit(solution)/shard_map/pallas_call | solution.py:75
  49.4 7.5 %all-to-all-start.2 = ((bf16[64,4,384]{2,1,0:T(4,128)(2,1)}), bf16[64,4,384]{2,1,0:T(4,128)(2,1)S(1)}, u32[]{:S(2)}, u32[]{:S(2)}) async-start(bf16[64,4,384]{2,1,0:T(4,128)(2,1)} %get-tuple-element.33), calls=%async_computation.2 | async-start | bytes 393216 | tf_op jit(solution)/shard_map/all_to_all | solution.py:331
  56.9 5.3 %shard_map.122 = (f32[1,24,32,384]{3,2,1,0:T(8,128)}, f32[32,384]{1,0:T(8,128)}, bf16[32,384]{1,0:T(8,128)(2,1)}) custom-call(bf16[32,384]{1,0:T(8,128)(2,1)S(1)} %collective-permute-done.refs_15_.refs_0_, bf16[32,384]{1,0:T(8,128)(2,1)S(1)} %collective-permute-done.1.refs_16_.refs_1_, f32[1,24,32,384]{3,2,1,0:T(8,128)} %refs_3_.4, ...), custom_call_target="tpu_custom_call" | custom-call | tf_op jit(solution)/shard_map/pallas_call | solution.py:75
  62.2 0.0 copy-start.5
  62.2 6.7 %all-to-all-done.2.refs_0_ = bf16[64,4,384]{2,1,0:T(4,128)(2,1)S(1)} async-done(((bf16[64,4,384]{2,1,0:T(4,128)(2,1)}), bf16[64,4,384]{2,1,0:T(4,128)(2,1)S(1)}, u32[]{:S(2)}, u32[]{:S(2)}) %all-to-all-start.2) | async-done | bytes 196640 | tf_op jit(solution)/shard_map/all_to_all | solution.py:331
  68.9 0.0 copy-start.2
  68.9 0.7 copy-done.2
  69.6 2.2 %shard_map.123 = (bf16[64,4,384]{2,1,0:T(4,128)(2,1)}, f32[32,384]{1,0:T(8,128)}, bf16[32,384]{1,0:T(8,128)(2,1)}) custom-call(bf16[64,4,384]{2,1,0:T(4,128)(2,1)} %copy-done.2, bf16[256,128]{1,0:T(8,128)(2,1)} %get-tuple-element.34.refs_1_.pick_hbm, f32[32,384]{1,0:T(8,128)} %get-tuple-element.37.refs_2_, bf16[1,24,32,384]{3,2,1,0:T(8,128)(2,1)} %scale_hbm.1), custom_call_target="tpu_custom_call" | custom-call | tf_op jit(solution)/shard_map/pallas_call | solution.py:75
  71.8 4.5 %all-to-all-start.3 = ((bf16[64,4,384]{2,1,0:T(4,128)(2,1)}), bf16[64,4,384]{2,1,0:T(4,128)(2,1)S(1)}, u32[]{:S(2)}, u32[]{:S(2)}) async-start(bf16[64,4,384]{2,1,0:T(4,128)(2,1)} %get-tuple-element.38), calls=%async_computation.3 | async-start | bytes 393216 | tf_op jit(solution)/shard_map/all_to_all | solution.py:331
  76.3 0.0 copy-done.5
  76.3 3.2 %collective-permute-start.2 = (bf16[32,384]{1,0:T(8,128)(2,1)S(1)}, bf16[32,384]{1,0:T(8,128)(2,1)S(1)}, u32[]{:S(2)}, u32[]{:S(2)}) collective-permute-start(bf16[32,384]{1,0:T(8,128)(2,1)S(1)} %copy-done.5), channel_id=1, source_target_pairs={{0,64},{64,128},{128,192},{1,65},{65,129},{129,193},{2,66},{66,130... | collective-permute-start | bytes 73736 | tf_op jit(solution)/shard_map/ppermute | solution.py:327
  79.5 1.3 %collective-permute-start.3 = (bf16[32,384]{1,0:T(8,128)(2,1)}, bf16[32,384]{1,0:T(8,128)(2,1)S(1)}, u32[]{:S(2)}, u32[]{:S(2)}) collective-permute-start(bf16[32,384]{1,0:T(8,128)(2,1)} %get-tuple-element.41), channel_id=1, source_target_pairs={{64,0},{128,64},{192,128},{65,1},{129,65},{193,129},{66,2},{130,66... | collective-permute-start | bytes 73736 | tf_op jit(solution)/shard_map/ppermute | solution.py:327
  80.8 0.0 collective-permute-done.2.refs_15_.refs_0_
  80.8 3.8 %collective-permute-done.3.refs_16_.refs_1_ = bf16[32,384]{1,0:T(8,128)(2,1)S(1)} collective-permute-done((bf16[32,384]{1,0:T(8,128)(2,1)}, bf16[32,384]{1,0:T(8,128)(2,1)S(1)}, u32[]{:S(2)}, u32[]{:S(2)}) %collective-permute-start.3) | collective-permute-done | bytes 24608 | tf_op jit(solution)/shard_map/ppermute | solution.py:327
  84.6 3.8 %all-to-all-done.3.refs_0_ = bf16[64,4,384]{2,1,0:T(4,128)(2,1)S(1)} async-done(((bf16[64,4,384]{2,1,0:T(4,128)(2,1)}), bf16[64,4,384]{2,1,0:T(4,128)(2,1)S(1)}, u32[]{:S(2)}, u32[]{:S(2)}) %all-to-all-start.3) | async-done | bytes 196640 | tf_op jit(solution)/shard_map/all_to_all | solution.py:331
  88.4 0.0 copy-start
  88.4 0.7 copy-done
  89.1 6.1 %shard_map.124 = (bf16[64,4,384]{2,1,0:T(4,128)(2,1)}, bf16[256,384]{1,0:T(8,128)(2,1)}) custom-call(bf16[64,4,384]{2,1,0:T(4,128)(2,1)} %copy-done, bf16[128,256]{1,0:T(8,128)(2,1)} %get-tuple-element.28.refs_1_, bf16[256,128]{1,0:T(8,128)(2,1)} %get-tuple-element.26.refs_2_, bf16[128,96]{1,0:T(8,128)(2,1)} %get-tuple-element.29.refs_3_, ...), custom_call_target="tpu_custom_call" | custom-call | tf_op jit(solution)/shard_map/pallas_call | solution.py:75
  95.2 7.7 %all-to-all-start.4 = ((bf16[64,4,384]{2,1,0:T(4,128)(2,1)}), bf16[64,4,384]{2,1,0:T(4,128)(2,1)S(1)}, u32[]{:S(2)}, u32[]{:S(2)}) async-start(bf16[64,4,384]{2,1,0:T(4,128)(2,1)} %get-tuple-element.42), calls=%async_computation.4 | async-start | bytes 393216 | tf_op jit(solution)/shard_map/all_to_all | solution.py:331
  102.9 5.0 %shard_map.125 = (f32[1,24,32,384]{3,2,1,0:T(8,128)}, f32[32,384]{1,0:T(8,128)}) custom-call(bf16[32,384]{1,0:T(8,128)(2,1)S(1)} %collective-permute-done.2.refs_15_.refs_0_, bf16[32,384]{1,0:T(8,128)(2,1)S(1)} %collective-permute-done.3.refs_16_.refs_1_, f32[1,24,32,384]{3,2,1,0:T(8,128)} %get-tuple-element.43.refs_2_, ...), custom_call_target="tpu_custom_call" | custom-call | tf_op jit(solution)/shard_map/pallas_call | solution.py:75
  107.9 7.0 %all-to-all-done.4.in_hbm = bf16[64,4,384]{2,1,0:T(4,128)(2,1)S(1)} async-done(((bf16[64,4,384]{2,1,0:T(4,128)(2,1)}), bf16[64,4,384]{2,1,0:T(4,128)(2,1)S(1)}, u32[]{:S(2)}, u32[]{:S(2)}) %all-to-all-start.4) | async-done | bytes 196640 | tf_op jit(solution)/shard_map/all_to_all | solution.py:331
  114.9 0.0 copy-start.3
  114.9 0.7 copy-done.3
  115.6 1.8 %shard_map.126 = f32[1,24,32,384]{3,2,1,0:T(8,128)} custom-call(bf16[64,4,384]{2,1,0:T(4,128)(2,1)} %copy-done.3, bf16[256,128]{1,0:T(8,128)(2,1)} %get-tuple-element.34.refs_1_.pick_hbm, f32[32,384]{1,0:T(8,128)} %get-tuple-element.45.base_hbm, bf16[1,24,32,384]{3,2,1,0:T(8,128)(2,1)} %scale_hbm.1, ...), custom_call_target="tpu_custom_call", output_to_operand_aliasing={{}: (4, {})} | custom-call | tf_op jit(solution)/shard_map/pallas_call | solution.py:403
Async XLA Ops:
  1.6 22.4 %all-to-all-start = ((f32[64,1,128]{2,1,0:T(1,128)}), f32[64,1,128]{2,1,0:T(1,128)S(1)}, u32[]{:S(2)}, u32[]{:S(2)}) async-start(f32[64,1,128]{2,1,0:T(1,128)} %bitcast.1), calls=%async_computation | async-start | bytes 65536 | tf_op jit(solution)/shard_map/all_to_all | solution.py:331
  16.6 13.9 %copy-start.6 = (bf16[32,384]{1,0:T(8,128)(2,1)S(1)}, bf16[32,384]{1,0:T(8,128)(2,1)}, u32[]{:S(2)}) copy-start(bf16[32,384]{1,0:T(8,128)(2,1)} %get-tuple-element.31) | copy-start | bytes 73732
  16.6 17.1 %copy-start.4 = (bf16[32,384]{1,0:T(8,128)(2,1)S(1)}, bf16[32,384]{1,0:T(8,128)(2,1)}, u32[]{:S(2)}) copy-start(bf16[32,384]{1,0:T(8,128)(2,1)} %get-tuple-element.32) | copy-start | bytes 73732
  25.8 16.9 %all-to-all-start.1 = ((bf16[64,4,384]{2,1,0:T(4,128)(2,1)}), bf16[64,4,384]{2,1,0:T(4,128)(2,1)S(1)}, u32[]{:S(2)}, u32[]{:S(2)}) async-start(bf16[64,4,384]{2,1,0:T(4,128)(2,1)} %get-tuple-element.27), calls=%async_computation.1 | async-start | bytes 393216 | tf_op jit(solution)/shard_map/all_to_all | solution.py:331
  30.5 4.5 %collective-permute-start = (bf16[32,384]{1,0:T(8,128)(2,1)S(1)}, bf16[32,384]{1,0:T(8,128)(2,1)S(1)}, u32[]{:S(2)}, u32[]{:S(2)}) collective-permute-start(bf16[32,384]{1,0:T(8,128)(2,1)S(1)} %copy-done.6), channel_id=1, source_target_pairs={{0,64},{64,128},{128,192},{1,65},{65,129},{129,193},{2,66},{66,130... | collective-permute-start | bytes 73736 | tf_op jit(solution)/shard_map/ppermute | solution.py:327
  33.7 4.9 %collective-permute-start.1 = (bf16[32,384]{1,0:T(8,128)(2,1)S(1)}, bf16[32,384]{1,0:T(8,128)(2,1)S(1)}, u32[]{:S(2)}, u32[]{:S(2)}) collective-permute-start(bf16[32,384]{1,0:T(8,128)(2,1)S(1)} %copy-done.4), channel_id=1, source_target_pairs={{64,0},{128,64},{192,128},{65,1},{129,65},{193,129},{66,2},{130,66... | collective-permute-start | bytes 73736 | tf_op jit(solution)/shard_map/ppermute | solution.py:327
  42.6 0.7 copy-start.1
  49.4 19.5 %all-to-all-start.2 = ((bf16[64,4,384]{2,1,0:T(4,128)(2,1)}), bf16[64,4,384]{2,1,0:T(4,128)(2,1)S(1)}, u32[]{:S(2)}, u32[]{:S(2)}) async-start(bf16[64,4,384]{2,1,0:T(4,128)(2,1)} %get-tuple-element.33), calls=%async_computation.2 | async-start | bytes 393216 | tf_op jit(solution)/shard_map/all_to_all | solution.py:331
  62.2 14.0 %copy-start.5 = (bf16[32,384]{1,0:T(8,128)(2,1)S(1)}, bf16[32,384]{1,0:T(8,128)(2,1)}, u32[]{:S(2)}) copy-start(bf16[32,384]{1,0:T(8,128)(2,1)} %get-tuple-element.40) | copy-start | bytes 73732
  68.9 0.7 copy-start.2
  71.8 16.6 %all-to-all-start.3 = ((bf16[64,4,384]{2,1,0:T(4,128)(2,1)}), bf16[64,4,384]{2,1,0:T(4,128)(2,1)S(1)}, u32[]{:S(2)}, u32[]{:S(2)}) async-start(bf16[64,4,384]{2,1,0:T(4,128)(2,1)} %get-tuple-element.38), calls=%async_computation.3 | async-start | bytes 393216 | tf_op jit(solution)/shard_map/all_to_all | solution.py:331
  76.3 4.5 %collective-permute-start.2 = (bf16[32,384]{1,0:T(8,128)(2,1)S(1)}, bf16[32,384]{1,0:T(8,128)(2,1)S(1)}, u32[]{:S(2)}, u32[]{:S(2)}) collective-permute-start(bf16[32,384]{1,0:T(8,128)(2,1)S(1)} %copy-done.5), channel_id=1, source_target_pairs={{0,64},{64,128},{128,192},{1,65},{65,129},{129,193},{2,66},{66,130... | collective-permute-start | bytes 73736 | tf_op jit(solution)/shard_map/ppermute | solution.py:327
  79.5 5.1 %collective-permute-start.3 = (bf16[32,384]{1,0:T(8,128)(2,1)}, bf16[32,384]{1,0:T(8,128)(2,1)S(1)}, u32[]{:S(2)}, u32[]{:S(2)}) collective-permute-start(bf16[32,384]{1,0:T(8,128)(2,1)} %get-tuple-element.41), channel_id=1, source_target_pairs={{64,0},{128,64},{192,128},{65,1},{129,65},{193,129},{66,2},{130,66... | collective-permute-start | bytes 73736 | tf_op jit(solution)/shard_map/ppermute | solution.py:327
  88.4 0.7 copy-start
  95.2 19.7 %all-to-all-start.4 = ((bf16[64,4,384]{2,1,0:T(4,128)(2,1)}), bf16[64,4,384]{2,1,0:T(4,128)(2,1)S(1)}, u32[]{:S(2)}, u32[]{:S(2)}) async-start(bf16[64,4,384]{2,1,0:T(4,128)(2,1)} %get-tuple-element.42), calls=%async_computation.4 | async-start | bytes 393216 | tf_op jit(solution)/shard_map/all_to_all | solution.py:331
  114.9 0.7 copy-start.3

commit v3 on v2

--- a/solution.py
+++ b/solution.py
@@ -8,9 +8,11 @@
 PENALTY = 2.0
 CAPACITY = 4
 GROUP = 16
+STREAMS = 4
 PARTS = 2
 VMEM = pltpu.VMEM
 HBM = pl.BlockSpec(memory_space=pltpu.HBM)
+ANY = pl.BlockSpec(memory_space=pl.ANY)
 BF16 = jnp.bfloat16
 F32 = jnp.float32
 
@@ -31,7 +33,7 @@
     return [pltpu.with_memory_space_constraint(array, pltpu.HBM) for array in arrays]
 
 
-def staged(body, ins, outs, scratch=(), tokens=(), loose=(), free_outs=False):
+def staged(body, ins, outs, scratch=(), tokens=(), loose=(), free_outs=False, direct=None):
     ins = [item if isinstance(item, tuple) else (item, ()) for item in ins]
     operands = [array if i in loose else in_hbm(array)[0] for i, (array, _) in enumerate(ins)]
     held = [VMEM(part_shape(array, index), array.dtype) for array, index in ins]
@@ -45,6 +47,7 @@
             del refs[:count]
             return taken
 
+        landed = pop(0 if direct is None else 1)
         sources, _, targets = pop(len(ins)), pop(len(tokens)), pop(len(outs))
         inside, leaving, (in_sems, out_sems), extra = pop(len(ins)), pop(len(outs)), pop(2), refs
         loads = {}
@@ -66,20 +69,24 @@
             stores.append(pltpu.make_async_copy(source, target, out_sems.at[i]))
             stores[-1].start()
 
-        body(take, leaving, give, *extra)
+        body(*landed, take, leaving, give, *extra)
         assert not loads
         for store in stores:
             store.wait()
 
     sems = [pltpu.SemaphoreType.DMA((len(ins),)), pltpu.SemaphoreType.DMA((len(outs),))]
+    first, first_specs = [], []
+    if direct is not None:
+        first.append(pltpu.with_memory_space_constraint(direct, pltpu.VMEM))
+        first_specs.append(pl.BlockSpec(memory_space=VMEM))
     return pl.pallas_call(
         kernel,
         out_shape=tuple(out if free_outs else pltpu.HBM(out.shape, out.dtype) for out in outs),
-        in_specs=[pl.BlockSpec(memory_space=pl.ANY)] * (len(ins) + len(tokens)),
-        out_specs=(pl.BlockSpec(memory_space=pl.ANY),) * len(outs),
+        in_specs=first_specs + [ANY] * (len(ins) + len(tokens)),
+        out_specs=(ANY,) * len(outs),
         scratch_shapes=held + given + sems + list(scratch),
         compiler_params=pltpu.CompilerParams(vmem_limit_bytes=32 * 2**20),
-    )(*operands, *tokens)
+    )(*first, *operands, *tokens)
 
 
 def part_shape(array, index):
@@ -142,13 +149,16 @@
 
 def place(rows, scratch, out_ref):
     scratch[...] = rows
-    for i in range(out_ref.shape[0]):
-        out_ref[i] = scratch[CAPACITY * i : CAPACITY * (i + 1), :].astype(BF16)
+    for j in range(out_ref.shape[0] // 2):
+        both = scratch[2 * CAPACITY * j : 2 * CAPACITY * (j + 1), :].astype(BF16)
+        out_ref[2 * j] = both[:CAPACITY]
+        out_ref[2 * j + 1] = both[CAPACITY:]
 
 
 def gathered(in_ref, scratch):
-    for i in range(in_ref.shape[0]):
-        scratch[CAPACITY * i : CAPACITY * (i + 1), :] = in_ref[i].astype(F32)
+    for j in range(in_ref.shape[0] // 2):
+        both = jnp.concatenate([in_ref[2 * j].astype(F32), in_ref[2 * j + 1].astype(F32)], axis=0)
+        scratch[2 * CAPACITY * j : 2 * CAPACITY * (j + 1), :] = both
     return scratch[...].astype(BF16)
 
 
@@ -170,23 +180,45 @@
     give(1)
 
 
-def contact_kernel(take, out, give, scratch, back_ref):
-    out_ref, pushed_ref = out
-    segs = back_ref.shape[0]
-    nodes = back_ref.shape[1] // 3
+def columns(rows):
+    nodes = rows.shape[1] // 3
+    return [rows[:, c * nodes : (c + 1) * nodes] for c in range(3)]
+
+
+def stage_kernel(
+    token, mortar_hbm, get_hbm, put_hbm, normal_hbm, gap_hbm, pick_hbm, layer_hbm,
+    mortar_ref, get_ref, put_ref, normal_ref, known_ref, gap_ref, pick_ref, layer_ref, sems,
+):
+    pairs = [(layer_hbm.at[0, 0], layer_ref), (pick_hbm, pick_ref), (normal_hbm, normal_ref), (gap_hbm.at[0, 0], gap_ref)]
+    pairs += [(get_hbm, get_ref), (put_hbm, put_ref)]
+    part = mortar_ref.shape[0] // STREAMS
+    for k in range(STREAMS):
+        here = pl.ds(k * part, part)
+        pairs.append((mortar_hbm.at[0, 0, here], mortar_ref.at[here]))
+    loads = [pltpu.make_async_copy(source, target, sems.at[i]) for i, (source, target) in enumerate(pairs)]
+    for load in loads:
+        load.start()
+    for load in loads[:4]:
+        load.wait()
+    slave = dot(pick_ref[...], split3(layer_ref[...]))
+    x, y, z = columns(normal_ref[...] * slave)
+    known_ref[...] = gap_ref[...] - (x + y + z)
+    for load in loads[4:]:
+        load.wait()
+
+
+def contact_kernel(
+    in_ref, mortar_ref, get_ref, put_ref, normal_ref, known_ref, low_token, high_token,
+    out_hbm, pushed_hbm, scratch, back_ref, out_ref, pushed_ref, sems,
+):
+    segs, _, nodes = mortar_ref.shape
     member = lax.rem(iota((3 * GROUP, nodes), 0), GROUP)
     place_in = lax.rem(member, 4)
     block_of = lax.div(member, 4)
     odd = lax.rem(place_in, 2) == 1
     late = place_in >= 2
     zero = jnp.zeros((3 * GROUP, nodes), BF16)
-    slave = dot(take(3)[...], split3(take(4)[...]))
-    arrived = gathered(take(0), scratch)
-    master = dot(take(1)[...], arrived).astype(BF16)
-    normal_ref, gap_ref = take(5), take(6)
-
-    def columns(rows):
-        return [rows[:, c * nodes : (c + 1) * nodes] for c in range(3)]
+    master = dot(get_ref[...], gathered(in_ref, scratch)).astype(BF16)
 
     def choose(parts):
         result = parts[0]
@@ -197,11 +229,9 @@
     for g in range(segs // GROUP):
         own = slice(GROUP * g, GROUP * (g + 1))
         um = jnp.concatenate(columns(master[own]), axis=0)
-        us = jnp.concatenate(columns(slave[own]), axis=0)
         normal = jnp.concatenate(columns(normal_ref[own, :]), axis=0)
-        mortar_ref = take(7 + g)
         weights = []
-        for s in range(0, GROUP, 4):
+        for s in range(GROUP * g, GROUP * (g + 1), 4):
             left = mortar_ref[s : s + 2].reshape(2 * nodes, nodes)
             right = mortar_ref[s + 2 : s + 4].reshape(2 * nodes, nodes)
             weights.append(jnp.concatenate([left, right], axis=1))
@@ -210,9 +240,8 @@
         for w in weights:
             r = dot(lhs, w, ((1,), (1,)))
             parts.append(jnp.where(odd, r[:, nodes:], r[:, :nodes]))
-        mapped = choose(parts)
-        terms = normal * (mapped - us)
-        gap = gap_ref[own, :] + (terms[:GROUP] + terms[GROUP : 2 * GROUP] + terms[2 * GROUP :])
+        terms = normal * choose(parts)
+        gap = known_ref[own, :] + (terms[:GROUP] + terms[GROUP : 2 * GROUP] + terms[2 * GROUP :])
         pressure = PENALTY * jnp.maximum(-gap, 0.0)
         pushed = jnp.concatenate([pressure] * 3, axis=0) * normal
         high = pushed.astype(BF16)
@@ -229,9 +258,13 @@
             back_ref[own, cols] = back[rows]
             pushed_ref[own, cols] = high[rows]
             pushed_ref[segs + GROUP * g : segs + GROUP * (g + 1), cols] = rest[rows]
-    give(1)
-    place(dot(take(2)[...], back_ref[...]), scratch, out_ref)
-    give(0)
+    store = pltpu.make_async_copy(pushed_ref, pushed_hbm, sems.at[0])
+    store.start()
+    place(dot(put_ref[...], back_ref[...]), scratch, out_ref)
+    send = pltpu.make_async_copy(out_ref, out_hbm, sems.at[1])
+    send.start()
+    store.wait()
+    send.wait()
 
 
 def bulk_kernel(take, out, give, rounded_ref, product_ref):
@@ -283,9 +316,10 @@
         give(2)
 
 
-def summed(take, scratch):
-    sums = dot(take(1)[...], gathered(take(0), scratch), ((0,), (0,)))
-    base, scale = take(2)[...], take(3)[...].astype(F32)
+def summed(in_ref, take, scratch):
+    arrived = gathered(in_ref, scratch)
+    sums = dot(take(0)[...], arrived, ((0,), (0,)))
+    base, scale = take(1)[...], take(2)[...].astype(F32)
     blocks = base.shape[0]
     total = sums[:blocks]
     for k in range(1, CAPACITY):
@@ -293,20 +327,20 @@
     return base - scale * total
 
 
-def next_kernel(take, out, give, scratch):
+def next_kernel(in_ref, take, out, give, scratch):
     out_ref, layer_ref, high_ref = out
-    first = summed(take, scratch)
-    layer_ref[...] = first
+    first = summed(in_ref, take, scratch)
+    layer_ref[0, 0] = first
     give(1)
     surface = first.astype(BF16)
     high_ref[...] = surface
     give(2)
-    place(dot(take(1)[...], copies(surface)), scratch, out_ref)
+    place(dot(take(0)[...], copies(surface)), scratch, out_ref)
     give(0)
 
 
-def last_kernel(in_hbm, pick_hbm, base_hbm, scale_hbm, field_hbm, out_hbm, in_ref, pick_ref, base_ref, scale_ref, scratch, layer_ref, sems):
-    pairs = [(in_hbm, in_ref), (pick_hbm, pick_ref), (base_hbm, base_ref), (scale_hbm.at[0, 0], scale_ref)]
+def last_kernel(in_ref, pick_hbm, base_hbm, scale_hbm, field_hbm, out_hbm, pick_ref, base_ref, scale_ref, scratch, layer_ref, sems):
+    pairs = [(pick_hbm, pick_ref), (base_hbm, base_ref), (scale_hbm.at[0, 0], scale_ref)]
     loads = {i: pltpu.make_async_copy(source, ref, sems.at[i]) for i, (source, ref) in enumerate(pairs)}
     for load in loads.values():
         load.start()
@@ -315,8 +349,8 @@
         loads[i].wait()
         return pairs[i][1]
 
-    layer_ref[...] = summed(take, scratch)
-    store = pltpu.make_async_copy(layer_ref, out_hbm.at[0, 0], sems.at[4])
+    layer_ref[...] = summed(in_ref, take, scratch)
+    store = pltpu.make_async_copy(layer_ref, out_hbm.at[0, 0], sems.at[3])
     store.start()
     store.wait()
 
@@ -366,15 +400,45 @@
         first_kernel, [asked, (disp, (0, 0))], [shaped((slots, wide), BF16), message], [rows_scratch], tokens=in_hbm(put), loose=(0,)
     )
 
-    def contact(arrived, layer0, low, high):
-        pieces = [(mortar, (0, 0, pl.ds(GROUP * g, GROUP))) for g in range(segs // GROUP)]
-        return staged(
+    def stage(token, layer0):
+        held = [
+            pltpu.VMEM(mortar.shape[2:], BF16),
+            pltpu.VMEM(get.shape, BF16),
+            pltpu.VMEM(put.shape, BF16),
+            pltpu.VMEM(normal_rows.shape, F32),
+            pltpu.VMEM(gap0.shape[2:], F32),
+        ]
+        return pl.pallas_call(
+            stage_kernel,
+            out_shape=held,
+            in_specs=[ANY] * 8,
+            out_specs=[pl.BlockSpec(memory_space=VMEM)] * 5,
+            scratch_shapes=[
+                VMEM(gap0.shape[2:], F32),
+                VMEM(pick3.shape, BF16),
+                VMEM((blocks, width), F32),
+                pltpu.SemaphoreType.DMA((6 + STREAMS,)),
+            ],
+            compiler_params=pltpu.CompilerParams(vmem_limit_bytes=16 * 2**20),
+        )(*in_hbm(token, mortar, get, put, normal_rows, gap0, pick3, layer0))
+
+    def contact(arrived, staged_arrays, low, high):
+        ready = [pltpu.with_memory_space_constraint(array, pltpu.VMEM) for array in (arrived, *staged_arrays)]
+        pushed = shaped((2 * segs, width), BF16)
+        return pl.pallas_call(
             contact_kernel,
-            [arrived, get, put, pick3, layer0, normal_rows, (gap0, (0, 0))] + pieces,
-            [message, shaped((2 * segs, width), BF16)],
-            [rows_scratch, VMEM((segs, width), BF16)],
-            tokens=[low, high],
-        )
+            out_shape=[pltpu.HBM(message.shape, BF16), pltpu.HBM(pushed.shape, BF16)],
+            in_specs=[pl.BlockSpec(memory_space=VMEM)] * 6 + [ANY] * 2,
+            out_specs=[ANY] * 2,
+            scratch_shapes=[
+                rows_scratch,
+                VMEM((segs, width), BF16),
+                VMEM(message.shape, BF16),
+                VMEM(pushed.shape, BF16),
+                pltpu.SemaphoreType.DMA((2,)),
+            ],
+            compiler_params=pltpu.CompilerParams(vmem_limit_bytes=16 * 2**20),
+        )(*ready, low, high)
 
     def bulk(field, layer0, low, high, pushed, keep_last):
         outs = [shaped(disp.shape, F32), layer] + ([edge] if keep_last else [])
@@ -389,34 +453,33 @@
 
     arrived = exchange(sent)
     low, high = shift(low, 1), shift(high, -1)
-    sent, pushed = contact(arrived, (disp, (0, 0)), low, high)
+    sent, pushed = contact(arrived, stage(pick, disp), low, high)
     returned = exchange(sent)
     field, base, last = bulk(disp, (disp, (0, 0)), low, high, pushed, True)
     sent, layer0, high = staged(
-        next_kernel, [returned, pick, base, (inv_diag, (0, 0))], [message, layer, edge], [rows_scratch]
+        next_kernel, [pick, base, (inv_diag, (0, 0))], [message, shaped((1, 1, blocks, width), F32), edge], [rows_scratch], direct=returned
     )
     arrived = exchange(sent)
     low, high = shift(last, 1), shift(high, -1)
-    sent, pushed = contact(arrived, layer0, low, high)
+    sent, pushed = contact(arrived, stage(pick, layer0), low, high)
     returned = exchange(sent)
-    field, base = bulk(field, layer0, low, high, pushed, False)
+    field, base = bulk(field, (layer0, (0, 0)), low, high, pushed, False)
     return pl.pallas_call(
         last_kernel,
         out_shape=pltpu.HBM(disp.shape, F32),
-        in_specs=[HBM] * 5,
+        in_specs=[pl.BlockSpec(memory_space=VMEM)] + [HBM] * 4,
         out_specs=HBM,
         scratch_shapes=[
-            VMEM(message.shape, BF16),
             VMEM(pick.shape, BF16),
             VMEM(base.shape, F32),
             VMEM(base.shape, BF16),
             rows_scratch,
             VMEM(base.shape, F32),
-            pltpu.SemaphoreType.DMA((5,)),
+            pltpu.SemaphoreType.DMA((4,)),
         ],
         input_output_aliases={4: 0},
         compiler_params=pltpu.CompilerParams(vmem_limit_bytes=32 * 2**20),
-    )(*in_hbm(returned, pick, base, inv_diag, field))
+    )(pltpu.with_memory_space_constraint(returned, pltpu.VMEM), *in_hbm(pick, base, inv_diag, field))
 
 
 def solution(mesh):

time: 118 us -> 116 us (0.983)
  waiting for transfers between devices: 36.3 us -> 26.3 us
  local copies, waits for them, and re-layouts: 2.71 us -> 8.29 us
  starting transfers between devices: 46.3 us -> 48.5 us
    pallas_call x0 -> x4, Pallas kernels: none -> 12.7 us  [the longest x2 7.64 us: contact(): pl.pallas_call(contact_kernel, out_shape=[pltpu.HBM(message.shape, BF16),...]
    pallas_call x8 -> x6, Pallas kernels: 30.1 us -> 17.7 us  [staged(): pl.pallas_call(kernel, out_shape=tuple((out if free_outs else pltpu.HBM(o...]
    ppermute x4, waiting for transfers between devices: 7.33 us -> 0.01 us  [shift(): return lax.ppermute(block, 'slab', pairs)]
    unnamed x14, local copies, waits for them, and re-layouts: 2.71 us -> 8.29 us
    all_to_all x5, waiting for transfers between devices: 29 us -> 26.3 us  [exchange(): return lax.all_to_all(parts, 'dom', 0, 0, tiled=True)]
  transfers between devices with their start and end apart: 9 -> 9, of which waited for: 7 -> 5; matrix products, arithmetic and copies ran while one was open for 0% -> 0% of each run, Pallas kernels for 11% -> 15%
where the time goes in v3:
time: 116 us; the launch traced here: 115 us
  starting transfers between devices  48.5 us (42%)
  Pallas kernels  32.1 us (28%)
  waiting for transfers between devices  26.3 us (23%)
  local copies, waits for them, and re-layouts  8.29 us (7%)
    all_to_all x5, starting transfers between devices, exchange(): return lax.all_to_all(parts, 'dom', 0, 0, tiled=True)  38.5 us
    all_to_all x5, waiting for transfers between devices, exchange(): return lax.all_to_all(parts, 'dom', 0, 0, tiled=True)  26.3 us
    pallas_call x6, Pallas kernels, staged(): pl.pallas_call(kernel, out_shape=tuple((out if free_outs else pltpu.HBM(o...  17.7 us
    ppermute x4, starting transfers between devices, shift(): return lax.ppermute(block, 'slab', pairs)  10.1 us
    unnamed x14, local copies, waits for them, and re-layouts  8.29 us
    pallas_call x2, Pallas kernels, contact(): pl.pallas_call(contact_kernel, out_shape=[pltpu.HBM(message.shape, BF16),...  7.64 us
    pallas_call x2, Pallas kernels, stage(): pl.pallas_call(stage_kernel, out_shape=held, in_specs=[ANY] * 8, out_spec...  5.02 us
  transfers between devices with their start and end apart: 9, of which 5 were waited for; matrix products, arithmetic and copies ran while one was open for 0% of the time, Pallas kernels for 15%

profile of v3, /device:TPU:1, one launch (start us, length us, event | category | flops | bytes accessed | tf_op | source)
XLA Modules:
  0.0 115.4 jit_solution(16886042946870753828)
XLA Ops:
  0.0 1.6 %shard_map.118.refs_5_ = f32[64,128]{1,0:T(8,128)} custom-call(s32[1,1,128]{2,1,0:T(1,128)} %refs_0_.3, s32[1,1,128]{2,1,0:T(1,128)} %refs_1_.3), custom_call_target="tpu_custom_call" | custom-call | tf_op jit(solution)/shard_map/pallas_call | solution.py:82
  1.6 13.0 %all-to-all-start = ((f32[64,1,128]{2,1,0:T(1,128)}), f32[64,1,128]{2,1,0:T(1,128)S(1)}, u32[]{:S(2)}, u32[]{:S(2)}) async-start(f32[64,1,128]{2,1,0:T(1,128)} %bitcast.1), calls=%async_computation | async-start | bytes 65536 | tf_op jit(solution)/shard_map/all_to_all | solution.py:365
  14.6 2.0 %shard_map.119 = (bf16[256,128]{1,0:T(8,128)(2,1)}, bf16[128,256]{1,0:T(8,128)(2,1)}, bf16[128,96]{1,0:T(8,128)(2,1)}, bf16[32,256]{1,0:T(8,128)(2,1)}, f32[128,...) custom-call(s32[1,1,128]{2,1,0:T(1,128)} %refs_0_.3, s32[1,1,128]{2,1,0:T(1,128)} %refs_1_.4, ...), custom_call_target="tpu_custom_call" | custom-call | tf_op jit(solution)/shard_map/pallas_call | solution.py:82
  16.6 0.0 copy-start.6
  16.6 0.0 copy-start.5
  16.6 7.4 %all-to-all-done = f32[64,1,128]{2,1,0:T(1,128)S(1)} async-done(((f32[64,1,128]{2,1,0:T(1,128)}), f32[64,1,128]{2,1,0:T(1,128)S(1)}, u32[]{:S(2)}, u32[]{:S(2)}) %all-to-all-start) | async-done | bytes 32800 | tf_op jit(solution)/shard_map/all_to_all | solution.py:365
  24.0 1.7 %shard_map.120 = (bf16[256,128]{1,0:T(8,128)(2,1)}, bf16[64,4,384]{2,1,0:T(4,128)(2,1)}) custom-call(f32[64,128]{1,0:T(8,128)S(1)} %bitcast.4, f32[1,24,32,384]{3,2,1,0:T(8,128)} %refs_3_.4, bf16[256,128]{1,0:T(8,128)(2,1)} %get-tuple-element.36.refs_2_.put_hbm), custom_call_target="tpu_custom_call" | custom-call | tf_op jit(solution)/shard_map/pallas_call | solution.py:82
  25.8 4.7 %all-to-all-start.1 = ((bf16[64,4,384]{2,1,0:T(4,128)(2,1)}), bf16[64,4,384]{2,1,0:T(4,128)(2,1)S(1)}, u32[]{:S(2)}, u32[]{:S(2)}) async-start(bf16[64,4,384]{2,1,0:T(4,128)(2,1)} %get-tuple-element.37), calls=%async_computation.1 | async-start | bytes 393216 | tf_op jit(solution)/shard_map/all_to_all | solution.py:365
  30.5 0.0 copy-done.6
  30.5 3.2 %collective-permute-start = (bf16[32,384]{1,0:T(8,128)(2,1)S(1)}, bf16[32,384]{1,0:T(8,128)(2,1)S(1)}, u32[]{:S(2)}, u32[]{:S(2)}) collective-permute-start(bf16[32,384]{1,0:T(8,128)(2,1)S(1)} %copy-done.6), channel_id=1, source_target_pairs={{0,64},{64,128},{128,192},{1,65},{65,129},{129,193},{2,66},{66,130... | collective-permute-start | bytes 73736 | tf_op jit(solution)/shard_map/ppermute | solution.py:361
  33.7 0.0 copy-done.5
  33.7 1.3 %collective-permute-start.1 = (bf16[32,384]{1,0:T(8,128)(2,1)S(1)}, bf16[32,384]{1,0:T(8,128)(2,1)S(1)}, u32[]{:S(2)}, u32[]{:S(2)}) collective-permute-start(bf16[32,384]{1,0:T(8,128)(2,1)S(1)} %copy-done.5), channel_id=1, source_target_pairs={{64,0},{128,64},{192,128},{65,1},{129,65},{193,129},{66,2},{130,66... | collective-permute-start | bytes 73736 | tf_op jit(solution)/shard_map/ppermute | solution.py:361
  35.0 2.5 %shard_map.121 = (bf16[128,128,128]{2,1,0:T(8,128)(2,1)S(1)}, bf16[128,256]{1,0:T(8,128)(2,1)S(1)}, bf16[256,128]{1,0:T(8,128)(2,1)S(1)}, f32[128,384]{1,0:T(8,128)S(1)}, f32[128,128]{1,0:T(8,128)S(1)}) custom-call(bf16[256,128]{1,0:T(8,128)(2,1)} %get-tuple-element.38.token.refs_1_.pick_hbm, bf16[1,1,128,128,128]{4,3,2,1,0:T(8,128)(2,1)} %mortar_hbm.3, ...), custom_call_target="tpu_custom_call" | custom-call | tf_op jit(solution)/shard_map/pallas_call | solution.py:411
  37.5 0.0 copy-start.2
  37.6 1.9 %copy-done.2 = bf16[128,128,128]{2,1,0:T(8,128)(2,1)} copy-done((bf16[128,128,128]{2,1,0:T(8,128)(2,1)}, bf16[128,128,128]{2,1,0:T(8,128)(2,1)S(1)}, u32[]{:S(2)}) %copy-start.2) | copy-done | bytes 4194328
  39.5 0.0 collective-permute-done.low_token.refs_0_
  39.5 0.0 collective-permute-done.1.high_token.refs_1_
  39.5 3.2 %all-to-all-done.1.in_ref = bf16[64,4,384]{2,1,0:T(4,128)(2,1)S(1)} async-done(((bf16[64,4,384]{2,1,0:T(4,128)(2,1)}), bf16[64,4,384]{2,1,0:T(4,128)(2,1)S(1)}, u32[]{:S(2)}, u32[]{:S(2)}) %all-to-all-start.1) | async-done | bytes 196640 | tf_op jit(solution)/shard_map/all_to_all | solution.py:365
  42.7 0.0 copy-start.3
  42.7 2.2 %copy-done.3 = bf16[128,128,128]{2,1,0:T(8,128)(2,1)S(1)} copy-done((bf16[128,128,128]{2,1,0:T(8,128)(2,1)S(1)}, bf16[128,128,128]{2,1,0:T(8,128)(2,1)}, u32[]{:S(2)}) %copy-start.3) | copy-done | bytes 4194328
  44.9 3.8 %shard_map.122 = (bf16[64,4,384]{2,1,0:T(4,128)(2,1)}, bf16[256,384]{1,0:T(8,128)(2,1)}) custom-call(bf16[64,4,384]{2,1,0:T(4,128)(2,1)S(1)} %all-to-all-done.1.in_ref, bf16[128,128,128]{2,1,0:T(8,128)(2,1)S(1)} %copy-done.3, bf16[128,256]{1,0:T(8,128)(2,1)S(1)} %get-tuple-element.43.get_ref, bf16[256,128]{1,0:T(8,128)(2,1)S(1)} %get-tuple-element.44.put_ref, ...), custom_call_target="tpu_custom_call" | custom-call | tf_op jit(solution)/shard_map/pallas_call | solution.py:428
  48.7 7.5 %all-to-all-start.2 = ((bf16[64,4,384]{2,1,0:T(4,128)(2,1)}), bf16[64,4,384]{2,1,0:T(4,128)(2,1)S(1)}, u32[]{:S(2)}, u32[]{:S(2)}) async-start(bf16[64,4,384]{2,1,0:T(4,128)(2,1)} %get-tuple-element.49), calls=%async_computation.2 | async-start | bytes 393216 | tf_op jit(solution)/shard_map/all_to_all | solution.py:365
  56.2 5.3 %shard_map.123 = (f32[1,24,32,384]{3,2,1,0:T(8,128)}, f32[32,384]{1,0:T(8,128)}, bf16[32,384]{1,0:T(8,128)(2,1)}) custom-call(bf16[32,384]{1,0:T(8,128)(2,1)S(1)} %collective-permute-done.low_token.refs_0_, bf16[32,384]{1,0:T(8,128)(2,1)S(1)} %collective-permute-done.1.high_token.refs_1_, f32[1,24,32,384]{3,2,1,0:T(8,128)} %refs_3_.4, ...), custom_call_target="tpu_custom_call" | custom-call | tf_op jit(solution)/shard_map/pallas_call | solution.py:82
  61.6 0.0 copy-start.4
  61.6 6.7 %all-to-all-done.2.refs_0_ = bf16[64,4,384]{2,1,0:T(4,128)(2,1)S(1)} async-done(((bf16[64,4,384]{2,1,0:T(4,128)(2,1)}), bf16[64,4,384]{2,1,0:T(4,128)(2,1)S(1)}, u32[]{:S(2)}, u32[]{:S(2)}) %all-to-all-start.2) | async-done | bytes 196640 | tf_op jit(solution)/shard_map/all_to_all | solution.py:365
  68.3 2.0 %shard_map.124 = (bf16[64,4,384]{2,1,0:T(4,128)(2,1)}, f32[1,1,32,384]{3,2,1,0:T(8,128)}, bf16[32,384]{1,0:T(8,128)(2,1)}) custom-call(bf16[64,4,384]{2,1,0:T(4,128)(2,1)S(1)} %all-to-all-done.2.refs_0_, bf16[256,128]{1,0:T(8,128)(2,1)} %get-tuple-element.38.token.refs_1_.pick_hbm, f32[32,384]{1,0:T(8,128)} %get-tuple-element.52.refs_2_, ...), custom_call_target="tpu_custom_call" | custom-call | tf_op jit(solution)/shard_map/pallas_call | solution.py:82
  70.3 4.5 %all-to-all-start.3 = ((bf16[64,4,384]{2,1,0:T(4,128)(2,1)}), bf16[64,4,384]{2,1,0:T(4,128)(2,1)S(1)}, u32[]{:S(2)}, u32[]{:S(2)}) async-start(bf16[64,4,384]{2,1,0:T(4,128)(2,1)} %get-tuple-element.53), calls=%async_computation.3 | async-start | bytes 393216 | tf_op jit(solution)/shard_map/all_to_all | solution.py:365
  74.8 0.0 copy-done.4
  74.8 4.3 %collective-permute-start.2 = (bf16[32,384]{1,0:T(8,128)(2,1)S(1)}, bf16[32,384]{1,0:T(8,128)(2,1)S(1)}, u32[]{:S(2)}, u32[]{:S(2)}) collective-permute-start(bf16[32,384]{1,0:T(8,128)(2,1)S(1)} %copy-done.4), channel_id=1, source_target_pairs={{0,64},{64,128},{128,192},{1,65},{65,129},{129,193},{2,66},{66,130... | collective-permute-start | bytes 73736 | tf_op jit(solution)/shard_map/ppermute | solution.py:361
  79.1 1.3 %collective-permute-start.3 = (bf16[32,384]{1,0:T(8,128)(2,1)}, bf16[32,384]{1,0:T(8,128)(2,1)S(1)}, u32[]{:S(2)}, u32[]{:S(2)}) collective-permute-start(bf16[32,384]{1,0:T(8,128)(2,1)} %get-tuple-element.61), channel_id=1, source_target_pairs={{64,0},{128,64},{192,128},{65,1},{129,65},{193,129},{66,2},{130,66... | collective-permute-start | bytes 73736 | tf_op jit(solution)/shard_map/ppermute | solution.py:361
  80.4 2.5 %shard_map.125 = (bf16[128,128,128]{2,1,0:T(8,128)(2,1)S(1)}, bf16[128,256]{1,0:T(8,128)(2,1)S(1)}, bf16[256,128]{1,0:T(8,128)(2,1)S(1)}, f32[128,384]{1,0:T(8,128)S(1)}, f32[128,128]{1,0:T(8,128)S(1)}) custom-call(bf16[256,128]{1,0:T(8,128)(2,1)} %get-tuple-element.38.token.refs_1_.pick_hbm, bf16[1,1,128,128,128]{4,3,2,1,0:T(8,128)(2,1)} %mortar_hbm.3, ...), custom_call_target="tpu_custom_call" | custom-call | tf_op jit(solution)/shard_map/pallas_call | solution.py:411
  82.9 0.0 copy-start
  82.9 1.9 %copy-done = bf16[128,128,128]{2,1,0:T(8,128)(2,1)} copy-done((bf16[128,128,128]{2,1,0:T(8,128)(2,1)}, bf16[128,128,128]{2,1,0:T(8,128)(2,1)S(1)}, u32[]{:S(2)}) %copy-start) | copy-done | bytes 4194328
  84.8 0.0 collective-permute-done.2.low_token.refs_0_
  84.8 0.0 collective-permute-done.3.high_token.refs_1_
  84.8 2.1 %all-to-all-done.3.in_ref = bf16[64,4,384]{2,1,0:T(4,128)(2,1)S(1)} async-done(((bf16[64,4,384]{2,1,0:T(4,128)(2,1)}), bf16[64,4,384]{2,1,0:T(4,128)(2,1)S(1)}, u32[]{:S(2)}, u32[]{:S(2)}) %all-to-all-start.3) | async-done | bytes 196640 | tf_op jit(solution)/shard_map/all_to_all | solution.py:365
  86.9 0.0 copy-start.1
  86.9 2.2 %copy-done.1 = bf16[128,128,128]{2,1,0:T(8,128)(2,1)S(1)} copy-done((bf16[128,128,128]{2,1,0:T(8,128)(2,1)S(1)}, bf16[128,128,128]{2,1,0:T(8,128)(2,1)}, u32[]{:S(2)}) %copy-start.1) | copy-done | bytes 4194328
  89.1 3.8 %shard_map.126 = (bf16[64,4,384]{2,1,0:T(4,128)(2,1)}, bf16[256,384]{1,0:T(8,128)(2,1)}) custom-call(bf16[64,4,384]{2,1,0:T(4,128)(2,1)S(1)} %all-to-all-done.3.in_ref, bf16[128,128,128]{2,1,0:T(8,128)(2,1)S(1)} %copy-done.1, bf16[128,256]{1,0:T(8,128)(2,1)S(1)} %get-tuple-element.56.get_ref, bf16[256,128]{1,0:T(8,128)(2,1)S(1)} %get-tuple-element.57.put_ref, ...), custom_call_target="tpu_custom_call" | custom-call | tf_op jit(solution)/shard_map/pallas_call | solution.py:428
  92.9 8.7 %all-to-all-start.4 = ((bf16[64,4,384]{2,1,0:T(4,128)(2,1)}), bf16[64,4,384]{2,1,0:T(4,128)(2,1)S(1)}, u32[]{:S(2)}, u32[]{:S(2)}) async-start(bf16[64,4,384]{2,1,0:T(4,128)(2,1)} %get-tuple-element.62), calls=%async_computation.4 | async-start | bytes 393216 | tf_op jit(solution)/shard_map/all_to_all | solution.py:365
  101.7 5.1 %shard_map.127 = (f32[1,24,32,384]{3,2,1,0:T(8,128)}, f32[32,384]{1,0:T(8,128)}) custom-call(bf16[32,384]{1,0:T(8,128)(2,1)S(1)} %collective-permute-done.2.low_token.refs_0_, bf16[32,384]{1,0:T(8,128)(2,1)S(1)} %collective-permute-done.3.high_token.refs_1_, f32[1,24,32,384]{3,2,1,0:T(8,128)} %get-tuple-element.63.refs_2_, ...), custom_call_target="tpu_custom_call" | custom-call | tf_op jit(solution)/shard_map/pallas_call | solution.py:82
  106.7 7.0 %all-to-all-done.4.in_ref = bf16[64,4,384]{2,1,0:T(4,128)(2,1)S(1)} async-done(((bf16[64,4,384]{2,1,0:T(4,128)(2,1)}), bf16[64,4,384]{2,1,0:T(4,128)(2,1)S(1)}, u32[]{:S(2)}, u32[]{:S(2)}) %all-to-all-start.4) | async-done | bytes 196640 | tf_op jit(solution)/shard_map/all_to_all | solution.py:365
  113.7 1.7 %shard_map.128 = f32[1,24,32,384]{3,2,1,0:T(8,128)} custom-call(bf16[64,4,384]{2,1,0:T(4,128)(2,1)S(1)} %all-to-all-done.4.in_ref, bf16[256,128]{1,0:T(8,128)(2,1)} %get-tuple-element.38.token.refs_1_.pick_hbm, f32[32,384]{1,0:T(8,128)} %get-tuple-element.65.base_hbm, bf16[1,24,32,384]{3,2,1,0:T(8,128)(2,1)} %scale_hbm.1, ...), custom_call_target="tpu_custom_call", output_to_operand_aliasing={{}: (4, {})} | custom-call | tf_op jit(solution)/shard_map/pallas_call | solution.py:467
Async XLA Ops:
  1.6 22.4 %all-to-all-start = ((f32[64,1,128]{2,1,0:T(1,128)}), f32[64,1,128]{2,1,0:T(1,128)S(1)}, u32[]{:S(2)}, u32[]{:S(2)}) async-start(f32[64,1,128]{2,1,0:T(1,128)} %bitcast.1), calls=%async_computation | async-start | bytes 65536 | tf_op jit(solution)/shard_map/all_to_all | solution.py:365
  16.6 13.9 %copy-start.6 = (bf16[32,384]{1,0:T(8,128)(2,1)S(1)}, bf16[32,384]{1,0:T(8,128)(2,1)}, u32[]{:S(2)}) copy-start(bf16[32,384]{1,0:T(8,128)(2,1)} %get-tuple-element.47) | copy-start | bytes 73732
  16.6 17.1 %copy-start.5 = (bf16[32,384]{1,0:T(8,128)(2,1)S(1)}, bf16[32,384]{1,0:T(8,128)(2,1)}, u32[]{:S(2)}) copy-start(bf16[32,384]{1,0:T(8,128)(2,1)} %get-tuple-element.48) | copy-start | bytes 73732
  25.8 16.9 %all-to-all-start.1 = ((bf16[64,4,384]{2,1,0:T(4,128)(2,1)}), bf16[64,4,384]{2,1,0:T(4,128)(2,1)S(1)}, u32[]{:S(2)}, u32[]{:S(2)}) async-start(bf16[64,4,384]{2,1,0:T(4,128)(2,1)} %get-tuple-element.37), calls=%async_computation.1 | async-start | bytes 393216 | tf_op jit(solution)/shard_map/all_to_all | solution.py:365
  30.5 9.0 %collective-permute-start = (bf16[32,384]{1,0:T(8,128)(2,1)S(1)}, bf16[32,384]{1,0:T(8,128)(2,1)S(1)}, u32[]{:S(2)}, u32[]{:S(2)}) collective-permute-start(bf16[32,384]{1,0:T(8,128)(2,1)S(1)} %copy-done.6), channel_id=1, source_target_pairs={{0,64},{64,128},{128,192},{1,65},{65,129},{129,193},{2,66},{66,130... | collective-permute-start | bytes 73736 | tf_op jit(solution)/shard_map/ppermute | solution.py:361
  33.7 5.8 %collective-permute-start.1 = (bf16[32,384]{1,0:T(8,128)(2,1)S(1)}, bf16[32,384]{1,0:T(8,128)(2,1)S(1)}, u32[]{:S(2)}, u32[]{:S(2)}) collective-permute-start(bf16[32,384]{1,0:T(8,128)(2,1)S(1)} %copy-done.5), channel_id=1, source_target_pairs={{64,0},{128,64},{192,128},{65,1},{129,65},{193,129},{66,2},{130,66... | collective-permute-start | bytes 73736 | tf_op jit(solution)/shard_map/ppermute | solution.py:361
  37.5 2.0 %copy-start.2 = (bf16[128,128,128]{2,1,0:T(8,128)(2,1)}, bf16[128,128,128]{2,1,0:T(8,128)(2,1)S(1)}, u32[]{:S(2)}) copy-start(bf16[128,128,128]{2,1,0:T(8,128)(2,1)S(1)} %get-tuple-element.42.mortar_ref) | copy-start | bytes 12582916
  42.7 2.2 %copy-start.3 = (bf16[128,128,128]{2,1,0:T(8,128)(2,1)S(1)}, bf16[128,128,128]{2,1,0:T(8,128)(2,1)}, u32[]{:S(2)}) copy-start(bf16[128,128,128]{2,1,0:T(8,128)(2,1)} %copy-done.2) | copy-start | bytes 12582916
  48.7 19.6 %all-to-all-start.2 = ((bf16[64,4,384]{2,1,0:T(4,128)(2,1)}), bf16[64,4,384]{2,1,0:T(4,128)(2,1)S(1)}, u32[]{:S(2)}, u32[]{:S(2)}) async-start(bf16[64,4,384]{2,1,0:T(4,128)(2,1)} %get-tuple-element.49), calls=%async_computation.2 | async-start | bytes 393216 | tf_op jit(solution)/shard_map/all_to_all | solution.py:365
  61.6 13.2 %copy-start.4 = (bf16[32,384]{1,0:T(8,128)(2,1)S(1)}, bf16[32,384]{1,0:T(8,128)(2,1)}, u32[]{:S(2)}) copy-start(bf16[32,384]{1,0:T(8,128)(2,1)} %get-tuple-element.60) | copy-start | bytes 73732
  70.3 16.6 %all-to-all-start.3 = ((bf16[64,4,384]{2,1,0:T(4,128)(2,1)}), bf16[64,4,384]{2,1,0:T(4,128)(2,1)S(1)}, u32[]{:S(2)}, u32[]{:S(2)}) async-start(bf16[64,4,384]{2,1,0:T(4,128)(2,1)} %get-tuple-element.53), calls=%async_computation.3 | async-start | bytes 393216 | tf_op jit(solution)/shard_map/all_to_all | solution.py:365
  74.8 10.1 %collective-permute-start.2 = (bf16[32,384]{1,0:T(8,128)(2,1)S(1)}, bf16[32,384]{1,0:T(8,128)(2,1)S(1)}, u32[]{:S(2)}, u32[]{:S(2)}) collective-permute-start(bf16[32,384]{1,0:T(8,128)(2,1)S(1)} %copy-done.4), channel_id=1, source_target_pairs={{0,64},{64,128},{128,192},{1,65},{65,129},{129,193},{2,66},{66,130... | collective-permute-start | bytes 73736 | tf_op jit(solution)/shard_map/ppermute | solution.py:361
  79.1 5.8 %collective-permute-start.3 = (bf16[32,384]{1,0:T(8,128)(2,1)}, bf16[32,384]{1,0:T(8,128)(2,1)S(1)}, u32[]{:S(2)}, u32[]{:S(2)}) collective-permute-start(bf16[32,384]{1,0:T(8,128)(2,1)} %get-tuple-element.61), channel_id=1, source_target_pairs={{64,0},{128,64},{192,128},{65,1},{129,65},{193,129},{66,2},{130,66... | collective-permute-start | bytes 73736 | tf_op jit(solution)/shard_map/ppermute | solution.py:361
  82.9 2.0 %copy-start = (bf16[128,128,128]{2,1,0:T(8,128)(2,1)}, bf16[128,128,128]{2,1,0:T(8,128)(2,1)S(1)}, u32[]{:S(2)}) copy-start(bf16[128,128,128]{2,1,0:T(8,128)(2,1)S(1)} %get-tuple-element.55.mortar_ref) | copy-start | bytes 12582916
  86.9 2.2 %copy-start.1 = (bf16[128,128,128]{2,1,0:T(8,128)(2,1)S(1)}, bf16[128,128,128]{2,1,0:T(8,128)(2,1)}, u32[]{:S(2)}) copy-start(bf16[128,128,128]{2,1,0:T(8,128)(2,1)} %copy-done) | copy-start | bytes 12582916
  92.9 20.8 %all-to-all-start.4 = ((bf16[64,4,384]{2,1,0:T(4,128)(2,1)}), bf16[64,4,384]{2,1,0:T(4,128)(2,1)S(1)}, u32[]{:S(2)}, u32[]{:S(2)}) async-start(bf16[64,4,384]{2,1,0:T(4,128)(2,1)} %get-tuple-element.62), calls=%async_computation.4 | async-start | bytes 393216 | tf_op jit(solution)/shard_map/all_to_all | solution.py:365

commit v4 on v3

--- a/solution.py
+++ b/solution.py
@@ -13,6 +13,7 @@
 VMEM = pltpu.VMEM
 HBM = pl.BlockSpec(memory_space=pltpu.HBM)
 ANY = pl.BlockSpec(memory_space=pl.ANY)
+IN_VMEM = pl.BlockSpec(memory_space=VMEM)
 BF16 = jnp.bfloat16
 F32 = jnp.float32
 
@@ -33,11 +34,12 @@
     return [pltpu.with_memory_space_constraint(array, pltpu.HBM) for array in arrays]
 
 
-def staged(body, ins, outs, scratch=(), tokens=(), loose=(), free_outs=False, direct=None):
+def staged(body, ins, outs, scratch=(), tokens=(), loose=(), free_outs=False, direct=(), kept=()):
     ins = [item if isinstance(item, tuple) else (item, ()) for item in ins]
     operands = [array if i in loose else in_hbm(array)[0] for i, (array, _) in enumerate(ins)]
     held = [VMEM(part_shape(array, index), array.dtype) for array, index in ins]
-    given = [VMEM(out.shape, out.dtype) for out in outs]
+    given = [VMEM(out.shape, out.dtype) for i, out in enumerate(outs) if i not in kept]
+    here = [pltpu.with_memory_space_constraint(array, pltpu.VMEM) for array in direct]
 
     def kernel(*refs):
         refs = list(refs)
@@ -47,9 +49,9 @@
             del refs[:count]
             return taken
 
-        landed = pop(0 if direct is None else 1)
-        sources, _, targets = pop(len(ins)), pop(len(tokens)), pop(len(outs))
-        inside, leaving, (in_sems, out_sems), extra = pop(len(ins)), pop(len(outs)), pop(2), refs
+        landed, sources, _, targets = pop(len(here)), pop(len(ins)), pop(len(tokens)), pop(len(outs))
+        inside, leaving, (in_sems, out_sems), extra = pop(len(ins)), pop(len(given)), pop(2), refs
+        leaving = [targets[i] if i in kept else leaving.pop(0) for i in range(len(outs))]
         loads = {}
         for i, (source, ref, (_, index)) in enumerate(zip(sources, inside, ins)):
             loads[i] = pltpu.make_async_copy(source.at[index] if index else source, ref, in_sems.at[i])
@@ -74,19 +76,20 @@
         for store in stores:
             store.wait()
 
-    sems = [pltpu.SemaphoreType.DMA((len(ins),)), pltpu.SemaphoreType.DMA((len(outs),))]
-    first, first_specs = [], []
-    if direct is not None:
-        first.append(pltpu.with_memory_space_constraint(direct, pltpu.VMEM))
-        first_specs.append(pl.BlockSpec(memory_space=VMEM))
+    def space(i, out):
+        return out if free_outs else (pltpu.VMEM if i in kept else pltpu.HBM)(out.shape, out.dtype)
+
     return pl.pallas_call(
         kernel,
-        out_shape=tuple(out if free_outs else pltpu.HBM(out.shape, out.dtype) for out in outs),
-        in_specs=first_specs + [ANY] * (len(ins) + len(tokens)),
-        out_specs=(ANY,) * len(outs),
-        scratch_shapes=held + given + sems + list(scratch),
+        out_shape=tuple(space(i, out) for i, out in enumerate(outs)),
+        in_specs=[IN_VMEM] * len(here) + [ANY] * (len(ins) + len(tokens)),
+        out_specs=tuple(IN_VMEM if i in kept else ANY for i in range(len(outs))),
+        scratch_shapes=held
+        + given
+        + [pltpu.SemaphoreType.DMA((max(len(ins), 1),)), pltpu.SemaphoreType.DMA((len(outs),))]
+        + list(scratch),
         compiler_params=pltpu.CompilerParams(vmem_limit_bytes=32 * 2**20),
-    )(*first, *operands, *tokens)
+    )(*here, *operands, *tokens)
 
 
 def part_shape(array, index):
@@ -122,8 +125,10 @@
 
 
 def prep_kernel(take, out, give):
-    put_ref, get_ref, take_ref, sum_ref, normal_rows_ref, low_ref, high_ref = out
-    high_ref[...] = take(3)[...].astype(BF16)
+    put_ref, get_ref, take_ref, sum_ref, normal_rows_ref, low_ref, high_ref, surface_ref = out
+    surface = take(3)[...].astype(BF16)
+    surface_ref[...] = copies(surface)
+    high_ref[...] = surface
     low_ref[...] = take(4)[...].astype(BF16)
     give(5)
     give(6)
@@ -166,17 +171,17 @@
     return jnp.concatenate([rows] * CAPACITY, axis=0)
 
 
-def first_kernel(take, out, give, scratch):
+def first_kernel(asked_ref, surface_ref, take, out, give, scratch):
     pick_ref, out_ref = out
     slots, wide = pick_ref.shape
     count, blocks = slots // CAPACITY, wide // CAPACITY
     expand = (lax.div(iota((slots, count), 0), CAPACITY) == iota((slots, count), 1)).astype(BF16)
     mine = lax.div(iota((slots, wide), 1), blocks) == lax.rem(iota((slots, wide), 0), CAPACITY)
-    rows = dot(expand, take(0)[...].astype(BF16))
+    rows = dot(expand, asked_ref[...].astype(BF16))
     pick = jnp.where(mine, rows, 0.0).astype(BF16)
     pick_ref[...] = pick
     give(0)
-    place(dot(pick, copies(take(1)[...].astype(BF16))), scratch, out_ref)
+    place(dot(pick, surface_ref[...]), scratch, out_ref)
     give(1)
 
 
@@ -208,10 +213,18 @@
 
 
 def contact_kernel(
-    in_ref, mortar_ref, get_ref, put_ref, normal_ref, known_ref, low_token, high_token,
-    out_hbm, pushed_hbm, scratch, back_ref, out_ref, pushed_ref, sems,
+    in_ref, early_ref, get_ref, put_ref, normal_ref, known_ref, mortar_hbm, low_token, high_token,
+    out_hbm, pushed_hbm, scratch, back_ref, out_ref, pushed_ref, later_ref, sems, later_sems,
 ):
-    segs, _, nodes = mortar_ref.shape
+    early, _, nodes = early_ref.shape
+    segs = early + later_ref.shape[0]
+    later = []
+    for k in range(0, segs - early, GROUP):
+        copy = pltpu.make_async_copy(
+            mortar_hbm.at[0, 0, pl.ds(early + k, GROUP)], later_ref.at[pl.ds(k, GROUP)], later_sems.at[k // GROUP]
+        )
+        copy.start()
+        later.append(copy)
     member = lax.rem(iota((3 * GROUP, nodes), 0), GROUP)
     place_in = lax.rem(member, 4)
     block_of = lax.div(member, 4)
@@ -230,8 +243,12 @@
         own = slice(GROUP * g, GROUP * (g + 1))
         um = jnp.concatenate(columns(master[own]), axis=0)
         normal = jnp.concatenate(columns(normal_ref[own, :]), axis=0)
+        mortar_ref, start = early_ref, GROUP * g
+        if start >= early:
+            mortar_ref, start = later_ref, start - early
+            later[start // GROUP].wait()
         weights = []
-        for s in range(GROUP * g, GROUP * (g + 1), 4):
+        for s in range(start, start + GROUP, 4):
             left = mortar_ref[s : s + 2].reshape(2 * nodes, nodes)
             right = mortar_ref[s + 2 : s + 4].reshape(2 * nodes, nodes)
             weights.append(jnp.concatenate([left, right], axis=1))
@@ -268,7 +285,8 @@
 
 
 def bulk_kernel(take, out, give, rounded_ref, product_ref):
-    out_ref, base_ref, *last_refs = out
+    out_ref, base_ref, near_ref, pick_ref, *last_refs = out
+    pick_ref[...] = take(11)[...]
     _, layers, blocks, width = out_ref.shape
     rows = layers * blocks
     step = (rows + 2 * blocks) // PARTS
@@ -304,7 +322,7 @@
         return old + scale_ref[0, l].astype(F32) * (load_ref[0, l].astype(F32) - force)
 
     base_ref[...] = stepped(layer_ref[...], 0, inner(0) + dot(take(10)[...], take(9)[...]))
-    give(1)
+    near_ref[...] = scale_ref[0, 0].astype(F32)
 
     @pl.loop(1, layers)
     def update(l):
@@ -313,44 +331,33 @@
     give(0, (0, pl.ds(1, layers - 1)))
     for last_ref in last_refs:
         last_ref[...] = out_ref[0, layers - 1].astype(BF16)
-        give(2)
-
-
-def summed(in_ref, take, scratch):
-    arrived = gathered(in_ref, scratch)
-    sums = dot(take(0)[...], arrived, ((0,), (0,)))
-    base, scale = take(1)[...], take(2)[...].astype(F32)
-    blocks = base.shape[0]
+        give(4)
+
+
+def summed(in_ref, pick_ref, base_ref, scale_ref, scratch):
+    sums = dot(pick_ref[...], gathered(in_ref, scratch), ((0,), (0,)))
+    blocks = base_ref.shape[0]
     total = sums[:blocks]
     for k in range(1, CAPACITY):
         total = total + sums[k * blocks : (k + 1) * blocks]
-    return base - scale * total
-
-
-def next_kernel(in_ref, take, out, give, scratch):
+    return base_ref[...] - scale_ref[...] * total
+
+
+def next_kernel(in_ref, pick_ref, base_ref, scale_ref, take, out, give, scratch):
     out_ref, layer_ref, high_ref = out
-    first = summed(in_ref, take, scratch)
+    first = summed(in_ref, pick_ref, base_ref, scale_ref, scratch)
     layer_ref[0, 0] = first
     give(1)
     surface = first.astype(BF16)
     high_ref[...] = surface
     give(2)
-    place(dot(take(0)[...], copies(surface)), scratch, out_ref)
+    place(dot(pick_ref[...], copies(surface)), scratch, out_ref)
     give(0)
 
 
-def last_kernel(in_ref, pick_hbm, base_hbm, scale_hbm, field_hbm, out_hbm, pick_ref, base_ref, scale_ref, scratch, layer_ref, sems):
-    pairs = [(pick_hbm, pick_ref), (base_hbm, base_ref), (scale_hbm.at[0, 0], scale_ref)]
-    loads = {i: pltpu.make_async_copy(source, ref, sems.at[i]) for i, (source, ref) in enumerate(pairs)}
-    for load in loads.values():
-        load.start()
-
-    def take(i):
-        loads[i].wait()
-        return pairs[i][1]
-
-    layer_ref[...] = summed(in_ref, take, scratch)
-    store = pltpu.make_async_copy(layer_ref, out_hbm.at[0, 0], sems.at[3])
+def last_kernel(in_ref, pick_ref, base_ref, scale_ref, field_hbm, out_hbm, scratch, layer_ref, sem):
+    layer_ref[...] = summed(in_ref, pick_ref, base_ref, scale_ref, scratch)
+    store = pltpu.make_async_copy(layer_ref, out_hbm.at[0, 0], sem)
     store.start()
     store.wait()
 
@@ -381,7 +388,7 @@
     (asked,) = staged(
         lambda *refs: request_kernel(blocks, *refs), [seg_src, seg_master], [shaped((count, wide), F32)], free_outs=True
     )
-    put, get, pick3, back_sum, normal_rows, low, high = staged(
+    put, get, pick3, back_sum, normal_rows, low, high, surface = staged(
         prep_kernel,
         [seg_src, seg_slave, (normals, (0, 0)), (disp, (0, 0)), (disp, (0, layers - 1))],
         [
@@ -392,17 +399,21 @@
             shaped((segs, width), F32),
             edge,
             edge,
+            shaped((CAPACITY * blocks, width), BF16),
         ],
         tokens=[asked],
+        kept=(7,),
     )
     asked = exchange(asked.reshape(count, 1, wide)).reshape(count, wide)
     pick, sent = staged(
-        first_kernel, [asked, (disp, (0, 0))], [shaped((slots, wide), BF16), message], [rows_scratch], tokens=in_hbm(put), loose=(0,)
-    )
+        first_kernel, [], [shaped((slots, wide), BF16), message], [rows_scratch], direct=(asked, surface)
+    )
+
+    early = max(segs // 2, GROUP)
 
     def stage(token, layer0):
         held = [
-            pltpu.VMEM(mortar.shape[2:], BF16),
+            pltpu.VMEM((early,) + mortar.shape[3:], BF16),
             pltpu.VMEM(get.shape, BF16),
             pltpu.VMEM(put.shape, BF16),
             pltpu.VMEM(normal_rows.shape, F32),
@@ -412,7 +423,7 @@
             stage_kernel,
             out_shape=held,
             in_specs=[ANY] * 8,
-            out_specs=[pl.BlockSpec(memory_space=VMEM)] * 5,
+            out_specs=[IN_VMEM] * 5,
             scratch_shapes=[
                 VMEM(gap0.shape[2:], F32),
                 VMEM(pick3.shape, BF16),
@@ -428,58 +439,57 @@
         return pl.pallas_call(
             contact_kernel,
             out_shape=[pltpu.HBM(message.shape, BF16), pltpu.HBM(pushed.shape, BF16)],
-            in_specs=[pl.BlockSpec(memory_space=VMEM)] * 6 + [ANY] * 2,
+            in_specs=[IN_VMEM] * 6 + [ANY] * 3,
             out_specs=[ANY] * 2,
             scratch_shapes=[
                 rows_scratch,
                 VMEM((segs, width), BF16),
                 VMEM(message.shape, BF16),
                 VMEM(pushed.shape, BF16),
+                VMEM((segs - early,) + mortar.shape[3:], BF16),
                 pltpu.SemaphoreType.DMA((2,)),
+                pltpu.SemaphoreType.DMA(((segs - early) // GROUP,)),
             ],
             compiler_params=pltpu.CompilerParams(vmem_limit_bytes=16 * 2**20),
-        )(*ready, low, high)
+        )(*ready, *in_hbm(mortar), low, high)
 
     def bulk(field, layer0, low, high, pushed, keep_last):
-        outs = [shaped(disp.shape, F32), layer] + ([edge] if keep_last else [])
+        outs = [shaped(disp.shape, F32), layer, layer, shaped(pick.shape, BF16)] + ([edge] if keep_last else [])
         rows = (layers + 2) * blocks
         return staged(
             bulk_kernel,
-            [low, high, field, layer0, k_self, k_layer, k_side, f_ext, inv_diag, pushed, back_sum],
+            [low, high, field, layer0, k_self, k_layer, k_side, f_ext, inv_diag, pushed, back_sum, pick],
             outs,
             [VMEM((rows, width), BF16), VMEM((rows, 3 * width), F32)],
             loose=(0, 1),
+            kept=(1, 2, 3),
         )
 
     arrived = exchange(sent)
     low, high = shift(low, 1), shift(high, -1)
     sent, pushed = contact(arrived, stage(pick, disp), low, high)
     returned = exchange(sent)
-    field, base, last = bulk(disp, (disp, (0, 0)), low, high, pushed, True)
+    field, base, scale, near, last = bulk(disp, (disp, (0, 0)), low, high, pushed, True)
     sent, layer0, high = staged(
-        next_kernel, [pick, base, (inv_diag, (0, 0))], [message, shaped((1, 1, blocks, width), F32), edge], [rows_scratch], direct=returned
+        next_kernel, [], [message, shaped((1, 1, blocks, width), F32), edge], [rows_scratch], direct=(returned, near, base, scale)
     )
     arrived = exchange(sent)
     low, high = shift(last, 1), shift(high, -1)
     sent, pushed = contact(arrived, stage(pick, layer0), low, high)
     returned = exchange(sent)
-    field, base = bulk(field, (layer0, (0, 0)), low, high, pushed, False)
+    field, base, scale, near = bulk(field, (layer0, (0, 0)), low, high, pushed, False)
     return pl.pallas_call(
         last_kernel,
         out_shape=pltpu.HBM(disp.shape, F32),
-        in_specs=[pl.BlockSpec(memory_space=VMEM)] + [HBM] * 4,
+        in_specs=[IN_VMEM] * 4 + [HBM],
         out_specs=HBM,
-        scratch_shapes=[
-            VMEM(pick.shape, BF16),
-            VMEM(base.shape, F32),
-            VMEM(base.shape, BF16),
-            rows_scratch,
-            VMEM(base.shape, F32),
-            pltpu.SemaphoreType.DMA((4,)),
-        ],
+        scratch_shapes=[rows_scratch, VMEM(base.shape, F32), pltpu.SemaphoreType.DMA],
         input_output_aliases={4: 0},
-        compiler_params=pltpu.CompilerParams(vmem_limit_bytes=32 * 2**20),
-    )(pltpu.with_memory_space_constraint(returned, pltpu.VMEM), *in_hbm(pick, base, inv_diag, field))
+        compiler_params=pltpu.CompilerParams(vmem_limit_bytes=16 * 2**20),
+    )(
+        *[pltpu.with_memory_space_constraint(array, pltpu.VMEM) for array in (returned, near, base, scale)],
+        *in_hbm(field),
+    )
 
 
 def solution(mesh):

time: 116 us -> 110 us (0.948)
  local copies, waits for them, and re-layouts: 8.29 us -> 0 us
  waiting for transfers between devices: 26.3 us -> 31.8 us
  starting transfers between devices: 48.5 us -> 46.5 us
  Pallas kernels: 32.1 us -> 30.6 us
    unnamed x14 -> x0, local copies, waits for them, and re-layouts: 8.29 us -> none
    ppermute x4, waiting for transfers between devices: 0.01 us -> 3.83 us  [shift(): return lax.ppermute(block, 'slab', pairs)]
    all_to_all x5, waiting for transfers between devices: 26.3 us -> 28 us  [exchange(): return lax.all_to_all(parts, 'dom', 0, 0, tiled=True)]
    pallas_call x2, Pallas kernels: 7.64 us -> 9.14 us  [contact(): pl.pallas_call(contact_kernel, out_shape=[pltpu.HBM(message.shape, BF16),...]
    pallas_call x2, Pallas kernels: 5.02 us -> 3.69 us  [stage(): pl.pallas_call(stage_kernel, out_shape=held, in_specs=[ANY] * 8, out_spec...]
  transfers between devices with their start and end apart: 9 -> 9, of which waited for: 5 -> 7; matrix products, arithmetic and copies ran while one was open for 0% -> 0% of each run, Pallas kernels for 15% -> 15%
where the time goes in v4:
time: 110 us; the launch traced here: 109 us
  starting transfers between devices  46.5 us (42%)
  waiting for transfers between devices  31.8 us (29%)
  Pallas kernels  30.6 us (28%)
    all_to_all x5, starting transfers between devices, exchange(): return lax.all_to_all(parts, 'dom', 0, 0, tiled=True)  37.5 us
    all_to_all x5, waiting for transfers between devices, exchange(): return lax.all_to_all(parts, 'dom', 0, 0, tiled=True)  28 us
    pallas_call x6, Pallas kernels, staged(): pl.pallas_call(kernel, out_shape=tuple((space(i, out) for i, out in enume...  16.9 us
    pallas_call x2, Pallas kernels, contact(): pl.pallas_call(contact_kernel, out_shape=[pltpu.HBM(message.shape, BF16),...  9.14 us
    ppermute x4, starting transfers between devices, shift(): return lax.ppermute(block, 'slab', pairs)  8.99 us
    ppermute x4, waiting for transfers between devices, shift(): return lax.ppermute(block, 'slab', pairs)  3.83 us
    pallas_call x2, Pallas kernels, stage(): pl.pallas_call(stage_kernel, out_shape=held, in_specs=[ANY] * 8, out_spec...  3.69 us
  transfers between devices with their start and end apart: 9, of which 7 were waited for; matrix products, arithmetic and copies ran while one was open for 0% of the time, Pallas kernels for 15%

profile of v4, /device:TPU:1, one launch (start us, length us, event | category | flops | bytes accessed | tf_op | source)
XLA Modules:
  0.0 109.1 jit_solution(1874612483677734967)
XLA Ops:
  0.0 1.6 %shard_map.118.refs_5_ = f32[64,128]{1,0:T(8,128)} custom-call(s32[1,1,128]{2,1,0:T(1,128)} %refs_0_.3, s32[1,1,128]{2,1,0:T(1,128)} %refs_1_.2), custom_call_target="tpu_custom_call" | custom-call | tf_op jit(solution)/shard_map/pallas_call | solution.py:82
  1.6 13.0 %all-to-all-start = ((f32[64,1,128]{2,1,0:T(1,128)}), f32[64,1,128]{2,1,0:T(1,128)S(1)}, u32[]{:S(2)}, u32[]{:S(2)}) async-start(f32[64,1,128]{2,1,0:T(1,128)} %bitcast.1), calls=%async_computation | async-start | bytes 65536 | tf_op jit(solution)/shard_map/all_to_all | solution.py:372
  14.6 2.0 %shard_map.119 = (bf16[256,128]{1,0:T(8,128)(2,1)}, bf16[128,256]{1,0:T(8,128)(2,1)}, bf16[128,96]{1,0:T(8,128)(2,1)}, bf16[32,256]{1,0:T(8,128)(2,1)}, f32[128,...) custom-call(s32[1,1,128]{2,1,0:T(1,128)} %refs_0_.3, ...), custom_call_target="tpu_custom_call" | custom-call | tf_op jit(solution)/shard_map/pallas_call | solution.py:82
  16.6 7.4 %all-to-all-done = f32[64,1,128]{2,1,0:T(1,128)S(1)} async-done(((f32[64,1,128]{2,1,0:T(1,128)}), f32[64,1,128]{2,1,0:T(1,128)S(1)}, u32[]{:S(2)}, u32[]{:S(2)}) %all-to-all-start) | async-done | bytes 32800 | tf_op jit(solution)/shard_map/all_to_all | solution.py:372
  24.0 1.0 shard_map.120
  25.0 4.7 %all-to-all-start.1 = ((bf16[64,4,384]{2,1,0:T(4,128)(2,1)}), bf16[64,4,384]{2,1,0:T(4,128)(2,1)S(1)}, u32[]{:S(2)}, u32[]{:S(2)}) async-start(bf16[64,4,384]{2,1,0:T(4,128)(2,1)} %get-tuple-element.42), calls=%async_computation.1 | async-start | bytes 393216 | tf_op jit(solution)/shard_map/all_to_all | solution.py:372
  29.8 3.2 %collective-permute-start = (bf16[32,384]{1,0:T(8,128)(2,1)}, bf16[32,384]{1,0:T(8,128)(2,1)S(1)}, u32[]{:S(2)}, u32[]{:S(2)}) collective-permute-start(bf16[32,384]{1,0:T(8,128)(2,1)} %get-tuple-element.53), channel_id=1, source_target_pairs={{0,64},{64,128},{128,192},{1,65},{65,129},{129,193},{2,66},{66,130... | collective-permute-start | bytes 73736 | tf_op jit(solution)/shard_map/ppermute | solution.py:368
  33.0 1.3 %collective-permute-start.1 = (bf16[32,384]{1,0:T(8,128)(2,1)}, bf16[32,384]{1,0:T(8,128)(2,1)S(1)}, u32[]{:S(2)}, u32[]{:S(2)}) collective-permute-start(bf16[32,384]{1,0:T(8,128)(2,1)} %get-tuple-element.54), channel_id=1, source_target_pairs={{64,0},{128,64},{192,128},{65,1},{129,65},{193,129},{66,2},{130,66... | collective-permute-start | bytes 73736 | tf_op jit(solution)/shard_map/ppermute | solution.py:368
  34.3 1.8 %shard_map.121 = (bf16[64,128,128]{2,1,0:T(8,128)(2,1)S(1)}, bf16[128,256]{1,0:T(8,128)(2,1)S(1)}, bf16[256,128]{1,0:T(8,128)(2,1)S(1)}, f32[128,384]{1,0:T(8,128)S(1)}, f32[128,128]{1,0:T(8,128)S(1)}) custom-call(bf16[256,128]{1,0:T(8,128)(2,1)} %get-tuple-element.43.token.refs_11_, bf16[1,1,128,128,128]{4,3,2,1,0:T(8,128)(2,1)} %mortar_hbm.7, ...), custom_call_target="tpu_custom_call" | custom-call | tf_op jit(solution)/shard_map/pallas_call | solution.py:422
  36.1 0.0 collective-permute-done.low_token.refs_0_
  36.2 1.9 %collective-permute-done.1.high_token.refs_1_ = bf16[32,384]{1,0:T(8,128)(2,1)S(1)} collective-permute-done((bf16[32,384]{1,0:T(8,128)(2,1)}, bf16[32,384]{1,0:T(8,128)(2,1)S(1)}, u32[]{:S(2)}, u32[]{:S(2)}) %collective-permute-start.1) | collective-permute-done | bytes 24608 | tf_op jit(solution)/shard_map/ppermute | solution.py:368
  38.1 3.9 %all-to-all-done.1.in_ref = bf16[64,4,384]{2,1,0:T(4,128)(2,1)S(1)} async-done(((bf16[64,4,384]{2,1,0:T(4,128)(2,1)}), bf16[64,4,384]{2,1,0:T(4,128)(2,1)S(1)}, u32[]{:S(2)}, u32[]{:S(2)}) %all-to-all-start.1) | async-done | bytes 196640 | tf_op jit(solution)/shard_map/all_to_all | solution.py:372
  42.0 4.6 %shard_map.122 = (bf16[64,4,384]{2,1,0:T(4,128)(2,1)}, bf16[256,384]{1,0:T(8,128)(2,1)}) custom-call(bf16[64,4,384]{2,1,0:T(4,128)(2,1)S(1)} %all-to-all-done.1.in_ref, bf16[64,128,128]{2,1,0:T(8,128)(2,1)S(1)} %get-tuple-element.48.early_ref, bf16[128,256]{1,0:T(8,128)(2,1)S(1)} %get-tuple-element.49.get_ref, ...), custom_call_target="tpu_custom_call" | custom-call | tf_op jit(solution)/shard_map/pallas_call | solution.py:439
  46.6 7.6 %all-to-all-start.2 = ((bf16[64,4,384]{2,1,0:T(4,128)(2,1)}), bf16[64,4,384]{2,1,0:T(4,128)(2,1)S(1)}, u32[]{:S(2)}, u32[]{:S(2)}) async-start(bf16[64,4,384]{2,1,0:T(4,128)(2,1)} %get-tuple-element.55), calls=%async_computation.2 | async-start | bytes 393216 | tf_op jit(solution)/shard_map/all_to_all | solution.py:372
  54.2 5.6 %shard_map.123 = (f32[1,24,32,384]{3,2,1,0:T(8,128)}, f32[32,384]{1,0:T(8,128)S(1)}, f32[32,384]{1,0:T(8,128)S(1)}, bf16[256,128]{1,0:T(8,128)(2,1)S(1)}, bf16[32,384]{1,0:T(8,128)(2,1)}) custom-call(bf16[32,384]{1,0:T(8,128)(2,1)S(1)} %collective-permute-done.low_token.refs_0_, bf16[32,384]{1,0:T(8,128)(2,1)S(1)} %collective-permute-done.1.high_token.refs_1_, ...), custom_call_target="tpu_custom_call" | custom-call | tf_op jit(solution)/shard_map/pallas_call | solution.py:82
  59.8 6.4 %all-to-all-done.2.refs_0_ = bf16[64,4,384]{2,1,0:T(4,128)(2,1)S(1)} async-done(((bf16[64,4,384]{2,1,0:T(4,128)(2,1)}), bf16[64,4,384]{2,1,0:T(4,128)(2,1)S(1)}, u32[]{:S(2)}, u32[]{:S(2)}) %all-to-all-start.2) | async-done | bytes 196640 | tf_op jit(solution)/shard_map/all_to_all | solution.py:372
  66.2 1.1 %shard_map.124 = (bf16[64,4,384]{2,1,0:T(4,128)(2,1)}, f32[1,1,32,384]{3,2,1,0:T(8,128)}, bf16[32,384]{1,0:T(8,128)(2,1)}) custom-call(bf16[64,4,384]{2,1,0:T(4,128)(2,1)S(1)} %all-to-all-done.2.refs_0_, bf16[256,128]{1,0:T(8,128)(2,1)S(1)} %get-tuple-element.58.refs_1_, f32[32,384]{1,0:T(8,128)S(1)} %get-tuple-element.59.refs_2_, ...), custom_call_target="tpu_custom_call" | custom-call | tf_op jit(solution)/shard_map/pallas_call | solution.py:82
  67.4 4.5 %all-to-all-start.3 = ((bf16[64,4,384]{2,1,0:T(4,128)(2,1)}), bf16[64,4,384]{2,1,0:T(4,128)(2,1)S(1)}, u32[]{:S(2)}, u32[]{:S(2)}) async-start(bf16[64,4,384]{2,1,0:T(4,128)(2,1)} %get-tuple-element.61), calls=%async_computation.3 | async-start | bytes 393216 | tf_op jit(solution)/shard_map/all_to_all | solution.py:372
  71.9 3.2 %collective-permute-start.2 = (bf16[32,384]{1,0:T(8,128)(2,1)}, bf16[32,384]{1,0:T(8,128)(2,1)S(1)}, u32[]{:S(2)}, u32[]{:S(2)}) collective-permute-start(bf16[32,384]{1,0:T(8,128)(2,1)} %get-tuple-element.68), channel_id=1, source_target_pairs={{0,64},{64,128},{128,192},{1,65},{65,129},{129,193},{2,66},{66,130... | collective-permute-start | bytes 73736 | tf_op jit(solution)/shard_map/ppermute | solution.py:368
  75.1 1.3 %collective-permute-start.3 = (bf16[32,384]{1,0:T(8,128)(2,1)}, bf16[32,384]{1,0:T(8,128)(2,1)S(1)}, u32[]{:S(2)}, u32[]{:S(2)}) collective-permute-start(bf16[32,384]{1,0:T(8,128)(2,1)} %get-tuple-element.69), channel_id=1, source_target_pairs={{64,0},{128,64},{192,128},{65,1},{129,65},{193,129},{66,2},{130,66... | collective-permute-start | bytes 73736 | tf_op jit(solution)/shard_map/ppermute | solution.py:368
  76.4 1.8 %shard_map.125 = (bf16[64,128,128]{2,1,0:T(8,128)(2,1)S(1)}, bf16[128,256]{1,0:T(8,128)(2,1)S(1)}, bf16[256,128]{1,0:T(8,128)(2,1)S(1)}, f32[128,384]{1,0:T(8,128)S(1)}, f32[128,128]{1,0:T(8,128)S(1)}) custom-call(bf16[256,128]{1,0:T(8,128)(2,1)} %get-tuple-element.43.token.refs_11_, bf16[1,1,128,128,128]{4,3,2,1,0:T(8,128)(2,1)} %mortar_hbm.7, ...), custom_call_target="tpu_custom_call" | custom-call | tf_op jit(solution)/shard_map/pallas_call | solution.py:422
  78.2 0.0 collective-permute-done.2.low_token.refs_0_
  78.2 1.9 %collective-permute-done.3.high_token.refs_1_ = bf16[32,384]{1,0:T(8,128)(2,1)S(1)} collective-permute-done((bf16[32,384]{1,0:T(8,128)(2,1)}, bf16[32,384]{1,0:T(8,128)(2,1)S(1)}, u32[]{:S(2)}, u32[]{:S(2)}) %collective-permute-start.3) | collective-permute-done | bytes 24608 | tf_op jit(solution)/shard_map/ppermute | solution.py:368
  80.1 3.8 %all-to-all-done.3.in_ref = bf16[64,4,384]{2,1,0:T(4,128)(2,1)S(1)} async-done(((bf16[64,4,384]{2,1,0:T(4,128)(2,1)}), bf16[64,4,384]{2,1,0:T(4,128)(2,1)S(1)}, u32[]{:S(2)}, u32[]{:S(2)}) %all-to-all-start.3) | async-done | bytes 196640 | tf_op jit(solution)/shard_map/all_to_all | solution.py:372
  84.0 4.6 %shard_map.126 = (bf16[64,4,384]{2,1,0:T(4,128)(2,1)}, bf16[256,384]{1,0:T(8,128)(2,1)}) custom-call(bf16[64,4,384]{2,1,0:T(4,128)(2,1)S(1)} %all-to-all-done.3.in_ref, bf16[64,128,128]{2,1,0:T(8,128)(2,1)S(1)} %get-tuple-element.63.early_ref, bf16[128,256]{1,0:T(8,128)(2,1)S(1)} %get-tuple-element.64.get_ref, ...), custom_call_target="tpu_custom_call" | custom-call | tf_op jit(solution)/shard_map/pallas_call | solution.py:439
  88.6 7.7 %all-to-all-start.4 = ((bf16[64,4,384]{2,1,0:T(4,128)(2,1)}), bf16[64,4,384]{2,1,0:T(4,128)(2,1)S(1)}, u32[]{:S(2)}, u32[]{:S(2)}) async-start(bf16[64,4,384]{2,1,0:T(4,128)(2,1)} %get-tuple-element.70), calls=%async_computation.4 | async-start | bytes 393216 | tf_op jit(solution)/shard_map/all_to_all | solution.py:372
  96.2 5.5 %shard_map.127 = (f32[1,24,32,384]{3,2,1,0:T(8,128)}, f32[32,384]{1,0:T(8,128)S(1)}, f32[32,384]{1,0:T(8,128)S(1)}, bf16[256,128]{1,0:T(8,128)(2,1)S(1)}) custom-call(bf16[32,384]{1,0:T(8,128)(2,1)S(1)} %collective-permute-done.2.low_token.refs_0_, bf16[32,384]{1,0:T(8,128)(2,1)S(1)} %collective-permute-done.3.high_token.refs_1_, ...), custom_call_target="tpu_custom_call" | custom-call | tf_op jit(solution)/shard_map/pallas_call | solution.py:82
  101.8 6.5 %all-to-all-done.4.in_ref = bf16[64,4,384]{2,1,0:T(4,128)(2,1)S(1)} async-done(((bf16[64,4,384]{2,1,0:T(4,128)(2,1)}), bf16[64,4,384]{2,1,0:T(4,128)(2,1)S(1)}, u32[]{:S(2)}, u32[]{:S(2)}) %all-to-all-start.4) | async-done | bytes 196640 | tf_op jit(solution)/shard_map/all_to_all | solution.py:372
  108.3 0.8 shard_map.128
Async XLA Ops:
  1.6 22.4 %all-to-all-start = ((f32[64,1,128]{2,1,0:T(1,128)}), f32[64,1,128]{2,1,0:T(1,128)S(1)}, u32[]{:S(2)}, u32[]{:S(2)}) async-start(f32[64,1,128]{2,1,0:T(1,128)} %bitcast.1), calls=%async_computation | async-start | bytes 65536 | tf_op jit(solution)/shard_map/all_to_all | solution.py:372
  25.0 16.9 %all-to-all-start.1 = ((bf16[64,4,384]{2,1,0:T(4,128)(2,1)}), bf16[64,4,384]{2,1,0:T(4,128)(2,1)S(1)}, u32[]{:S(2)}, u32[]{:S(2)}) async-start(bf16[64,4,384]{2,1,0:T(4,128)(2,1)} %get-tuple-element.42), calls=%async_computation.1 | async-start | bytes 393216 | tf_op jit(solution)/shard_map/all_to_all | solution.py:372
  29.8 6.4 %collective-permute-start = (bf16[32,384]{1,0:T(8,128)(2,1)}, bf16[32,384]{1,0:T(8,128)(2,1)S(1)}, u32[]{:S(2)}, u32[]{:S(2)}) collective-permute-start(bf16[32,384]{1,0:T(8,128)(2,1)} %get-tuple-element.53), channel_id=1, source_target_pairs={{0,64},{64,128},{128,192},{1,65},{65,129},{129,193},{2,66},{66,130... | collective-permute-start | bytes 73736 | tf_op jit(solution)/shard_map/ppermute | solution.py:368
  33.0 5.1 %collective-permute-start.1 = (bf16[32,384]{1,0:T(8,128)(2,1)}, bf16[32,384]{1,0:T(8,128)(2,1)S(1)}, u32[]{:S(2)}, u32[]{:S(2)}) collective-permute-start(bf16[32,384]{1,0:T(8,128)(2,1)} %get-tuple-element.54), channel_id=1, source_target_pairs={{64,0},{128,64},{192,128},{65,1},{129,65},{193,129},{66,2},{130,66... | collective-permute-start | bytes 73736 | tf_op jit(solution)/shard_map/ppermute | solution.py:368
  46.6 19.7 %all-to-all-start.2 = ((bf16[64,4,384]{2,1,0:T(4,128)(2,1)}), bf16[64,4,384]{2,1,0:T(4,128)(2,1)S(1)}, u32[]{:S(2)}, u32[]{:S(2)}) async-start(bf16[64,4,384]{2,1,0:T(4,128)(2,1)} %get-tuple-element.55), calls=%async_computation.2 | async-start | bytes 393216 | tf_op jit(solution)/shard_map/all_to_all | solution.py:372
  67.4 16.6 %all-to-all-start.3 = ((bf16[64,4,384]{2,1,0:T(4,128)(2,1)}), bf16[64,4,384]{2,1,0:T(4,128)(2,1)S(1)}, u32[]{:S(2)}, u32[]{:S(2)}) async-start(bf16[64,4,384]{2,1,0:T(4,128)(2,1)} %get-tuple-element.61), calls=%async_computation.3 | async-start | bytes 393216 | tf_op jit(solution)/shard_map/all_to_all | solution.py:372
  71.9 6.4 %collective-permute-start.2 = (bf16[32,384]{1,0:T(8,128)(2,1)}, bf16[32,384]{1,0:T(8,128)(2,1)S(1)}, u32[]{:S(2)}, u32[]{:S(2)}) collective-permute-start(bf16[32,384]{1,0:T(8,128)(2,1)} %get-tuple-element.68), channel_id=1, source_target_pairs={{0,64},{64,128},{128,192},{1,65},{65,129},{129,193},{2,66},{66,130... | collective-permute-start | bytes 73736 | tf_op jit(solution)/shard_map/ppermute | solution.py:368
  75.1 5.1 %collective-permute-start.3 = (bf16[32,384]{1,0:T(8,128)(2,1)}, bf16[32,384]{1,0:T(8,128)(2,1)S(1)}, u32[]{:S(2)}, u32[]{:S(2)}) collective-permute-start(bf16[32,384]{1,0:T(8,128)(2,1)} %get-tuple-element.69), channel_id=1, source_target_pairs={{64,0},{128,64},{192,128},{65,1},{129,65},{193,129},{66,2},{130,66... | collective-permute-start | bytes 73736 | tf_op jit(solution)/shard_map/ppermute | solution.py:368
  88.6 19.7 %all-to-all-start.4 = ((bf16[64,4,384]{2,1,0:T(4,128)(2,1)}), bf16[64,4,384]{2,1,0:T(4,128)(2,1)S(1)}, u32[]{:S(2)}, u32[]{:S(2)}) async-start(bf16[64,4,384]{2,1,0:T(4,128)(2,1)} %get-tuple-element.70), calls=%async_computation.4 | async-start | bytes 393216 | tf_op jit(solution)/shard_map/all_to_all | solution.py:372

commit v5 on v4

--- a/solution.py
+++ b/solution.py
@@ -8,7 +8,7 @@
 PENALTY = 2.0
 CAPACITY = 4
 GROUP = 16
-STREAMS = 4
+PIECES = 4
 PARTS = 2
 VMEM = pltpu.VMEM
 HBM = pl.BlockSpec(memory_space=pltpu.HBM)
@@ -34,7 +34,7 @@
     return [pltpu.with_memory_space_constraint(array, pltpu.HBM) for array in arrays]
 
 
-def staged(body, ins, outs, scratch=(), tokens=(), loose=(), free_outs=False, direct=(), kept=()):
+def staged(body, ins, outs, scratch=(), tokens=(), loose=(), free_outs=False, direct=(), kept=(), fills=()):
     ins = [item if isinstance(item, tuple) else (item, ()) for item in ins]
     operands = [array if i in loose else in_hbm(array)[0] for i, (array, _) in enumerate(ins)]
     held = [VMEM(part_shape(array, index), array.dtype) for array, index in ins]
@@ -49,26 +49,31 @@
             del refs[:count]
             return taken
 
-        landed, sources, _, targets = pop(len(here)), pop(len(ins)), pop(len(tokens)), pop(len(outs))
-        inside, leaving, (in_sems, out_sems), extra = pop(len(ins)), pop(len(given)), pop(2), refs
+        landed, sources, fill_sources = pop(len(here)), pop(len(ins)), pop(len(fills))
+        _, targets = pop(len(tokens)), pop(len(outs))
+        inside, leaving, (in_sems, out_sems, fill_sems), extra = pop(len(ins)), pop(len(given)), pop(3), refs
         leaving = [targets[i] if i in kept else leaving.pop(0) for i in range(len(outs))]
         loads = {}
         for i, (source, ref, (_, index)) in enumerate(zip(sources, inside, ins)):
             loads[i] = pltpu.make_async_copy(source.at[index] if index else source, ref, in_sems.at[i])
             loads[i].start()
 
+        stores = []
+        for i, (source, (_, index, out)) in enumerate(zip(fill_sources, fills)):
+            stores.append(pltpu.make_async_copy(source.at[index] if index else source, targets[out], fill_sems.at[i]))
+            stores[-1].start()
+
         def take(i):
             if i in loads:
                 loads.pop(i).wait()
             return inside[i]
 
-        stores = []
-
-        def give(i, index=None):
+        def give(i, index=None, piece=None):
             source, target = leaving[i], targets[i]
             if index is not None:
                 source, target = source.at[index], target.at[index]
-            stores.append(pltpu.make_async_copy(source, target, out_sems.at[i]))
+            sem = out_sems.at[i if piece is None else len(outs) + piece]
+            stores.append(pltpu.make_async_copy(source, target, sem))
             stores[-1].start()
 
         body(*landed, take, leaving, give, *extra)
@@ -82,14 +87,14 @@
     return pl.pallas_call(
         kernel,
         out_shape=tuple(space(i, out) for i, out in enumerate(outs)),
-        in_specs=[IN_VMEM] * len(here) + [ANY] * (len(ins) + len(tokens)),
+        in_specs=[IN_VMEM] * len(here) + [ANY] * (len(ins) + len(fills) + len(tokens)),
         out_specs=tuple(IN_VMEM if i in kept else ANY for i in range(len(outs))),
         scratch_shapes=held
         + given
-        + [pltpu.SemaphoreType.DMA((max(len(ins), 1),)), pltpu.SemaphoreType.DMA((len(outs),))]
+        + [pltpu.SemaphoreType.DMA((max(count, 1),)) for count in (len(ins), len(outs) + PIECES, len(fills))]
         + list(scratch),
         compiler_params=pltpu.CompilerParams(vmem_limit_bytes=32 * 2**20),
-    )(*here, *operands, *tokens)
+    )(*here, *operands, *in_hbm(*[array for array, _, _ in fills]), *tokens)
 
 
 def part_shape(array, index):
@@ -125,7 +130,7 @@
 
 
 def prep_kernel(take, out, give):
-    put_ref, get_ref, take_ref, sum_ref, normal_rows_ref, low_ref, high_ref, surface_ref = out
+    put_ref, get_ref, take_ref, sum_ref, normal_rows_ref, low_ref, high_ref, surface_ref, _, get_v, put_v, normal_v, known_ref = out
     surface = take(3)[...].astype(BF16)
     surface_ref[...] = copies(surface)
     high_ref[...] = surface
@@ -148,16 +153,40 @@
     once = spread[:blocks].astype(BF16)
     sum_ref[...] = jnp.concatenate([once, once], axis=1)
     give(3)
-    normal_rows_ref[...] = dot(pick, split3(normals))
+    normal_rows = dot(pick, split3(normals))
+    normal_rows_ref[...] = normal_rows
     give(4)
-
-
-def place(rows, scratch, out_ref):
+    put_v[...] = put_ref[...]
+    get_v[...] = get_ref[...]
+    normal_v[...] = normal_rows
+    known_ref[...] = known(take(5)[...], normal_rows, dot(pick, split3(take(3)[...])))
+
+
+def known(gap, normal_rows, slave_rows):
+    x, y, z = columns(normal_rows * slave_rows)
+    return gap - (x + y + z)
+
+
+def columns(rows):
+    nodes = rows.shape[1] // 3
+    return [rows[:, c * nodes : (c + 1) * nodes] for c in range(3)]
+
+
+def known_kernel(take, out, give):
+    slave_rows = dot(take(1)[...], split3(take(0)[...]))
+    out[0][...] = known(take(3)[...], take(2)[...], slave_rows)
+
+
+def place(rows, scratch, out_ref, send):
     scratch[...] = rows
-    for j in range(out_ref.shape[0] // 2):
+    pairs = out_ref.shape[0] // 2
+    part = pairs // PIECES
+    for j in range(pairs):
         both = scratch[2 * CAPACITY * j : 2 * CAPACITY * (j + 1), :].astype(BF16)
         out_ref[2 * j] = both[:CAPACITY]
         out_ref[2 * j + 1] = both[CAPACITY:]
+        if (j + 1) % part == 0:
+            send(j // part, pl.ds(2 * (j + 1 - part), 2 * part))
 
 
 def gathered(in_ref, scratch):
@@ -181,35 +210,7 @@
     pick = jnp.where(mine, rows, 0.0).astype(BF16)
     pick_ref[...] = pick
     give(0)
-    place(dot(pick, surface_ref[...]), scratch, out_ref)
-    give(1)
-
-
-def columns(rows):
-    nodes = rows.shape[1] // 3
-    return [rows[:, c * nodes : (c + 1) * nodes] for c in range(3)]
-
-
-def stage_kernel(
-    token, mortar_hbm, get_hbm, put_hbm, normal_hbm, gap_hbm, pick_hbm, layer_hbm,
-    mortar_ref, get_ref, put_ref, normal_ref, known_ref, gap_ref, pick_ref, layer_ref, sems,
-):
-    pairs = [(layer_hbm.at[0, 0], layer_ref), (pick_hbm, pick_ref), (normal_hbm, normal_ref), (gap_hbm.at[0, 0], gap_ref)]
-    pairs += [(get_hbm, get_ref), (put_hbm, put_ref)]
-    part = mortar_ref.shape[0] // STREAMS
-    for k in range(STREAMS):
-        here = pl.ds(k * part, part)
-        pairs.append((mortar_hbm.at[0, 0, here], mortar_ref.at[here]))
-    loads = [pltpu.make_async_copy(source, target, sems.at[i]) for i, (source, target) in enumerate(pairs)]
-    for load in loads:
-        load.start()
-    for load in loads[:4]:
-        load.wait()
-    slave = dot(pick_ref[...], split3(layer_ref[...]))
-    x, y, z = columns(normal_ref[...] * slave)
-    known_ref[...] = gap_ref[...] - (x + y + z)
-    for load in loads[4:]:
-        load.wait()
+    place(dot(pick, surface_ref[...]), scratch, out_ref, lambda piece, part: give(1, part, piece))
 
 
 def contact_kernel(
@@ -277,15 +278,20 @@
             pushed_ref[segs + GROUP * g : segs + GROUP * (g + 1), cols] = rest[rows]
     store = pltpu.make_async_copy(pushed_ref, pushed_hbm, sems.at[0])
     store.start()
-    place(dot(put_ref[...], back_ref[...]), scratch, out_ref)
-    send = pltpu.make_async_copy(out_ref, out_hbm, sems.at[1])
-    send.start()
-    store.wait()
-    send.wait()
+    stores = [store]
+
+    def send(piece, part):
+        stores.append(pltpu.make_async_copy(out_ref.at[part], out_hbm.at[part], sems.at[1 + piece]))
+        stores[-1].start()
+
+    place(dot(put_ref[...], back_ref[...]), scratch, out_ref, send)
+    for copy in stores:
+        copy.wait()
 
 
 def bulk_kernel(take, out, give, rounded_ref, product_ref):
-    out_ref, base_ref, near_ref, pick_ref, *last_refs = out
+    out_ref, base_ref, near_ref, pick_ref = out[:4]
+    last_refs = out[4:5]
     pick_ref[...] = take(11)[...]
     _, layers, blocks, width = out_ref.shape
     rows = layers * blocks
@@ -351,8 +357,7 @@
     surface = first.astype(BF16)
     high_ref[...] = surface
     give(2)
-    place(dot(pick_ref[...], copies(surface)), scratch, out_ref)
-    give(0)
+    place(dot(pick_ref[...], copies(surface)), scratch, out_ref, lambda piece, part: give(0, part, piece))
 
 
 def last_kernel(in_ref, pick_ref, base_ref, scale_ref, field_hbm, out_hbm, scratch, layer_ref, sem):
@@ -385,12 +390,14 @@
     edge = shaped((blocks, width), BF16)
     layer = shaped((blocks, width), F32)
 
+    early = max(segs // 2, GROUP)
+    early_part = (0, 0, pl.ds(0, early))
     (asked,) = staged(
         lambda *refs: request_kernel(blocks, *refs), [seg_src, seg_master], [shaped((count, wide), F32)], free_outs=True
     )
-    put, get, pick3, back_sum, normal_rows, low, high, surface = staged(
+    put, get, pick3, back_sum, normal_rows, low, high, surface, *ready, gap = staged(
         prep_kernel,
-        [seg_src, seg_slave, (normals, (0, 0)), (disp, (0, 0)), (disp, (0, layers - 1))],
+        [seg_src, seg_slave, (normals, (0, 0)), (disp, (0, 0)), (disp, (0, layers - 1)), (gap0, (0, 0))],
         [
             shaped((slots, segs), BF16),
             shaped((segs, slots), BF16),
@@ -400,41 +407,23 @@
             edge,
             edge,
             shaped((CAPACITY * blocks, width), BF16),
+            shaped((early,) + mortar.shape[3:], BF16),
+            shaped((segs, slots), BF16),
+            shaped((slots, segs), BF16),
+            shaped((segs, width), F32),
+            shaped(gap0.shape[2:], F32),
         ],
         tokens=[asked],
-        kept=(7,),
+        kept=(7, 8, 9, 10, 11, 12),
+        fills=[(mortar, early_part, 8)],
     )
     asked = exchange(asked.reshape(count, 1, wide)).reshape(count, wide)
     pick, sent = staged(
         first_kernel, [], [shaped((slots, wide), BF16), message], [rows_scratch], direct=(asked, surface)
     )
 
-    early = max(segs // 2, GROUP)
-
-    def stage(token, layer0):
-        held = [
-            pltpu.VMEM((early,) + mortar.shape[3:], BF16),
-            pltpu.VMEM(get.shape, BF16),
-            pltpu.VMEM(put.shape, BF16),
-            pltpu.VMEM(normal_rows.shape, F32),
-            pltpu.VMEM(gap0.shape[2:], F32),
-        ]
-        return pl.pallas_call(
-            stage_kernel,
-            out_shape=held,
-            in_specs=[ANY] * 8,
-            out_specs=[IN_VMEM] * 5,
-            scratch_shapes=[
-                VMEM(gap0.shape[2:], F32),
-                VMEM(pick3.shape, BF16),
-                VMEM((blocks, width), F32),
-                pltpu.SemaphoreType.DMA((6 + STREAMS,)),
-            ],
-            compiler_params=pltpu.CompilerParams(vmem_limit_bytes=16 * 2**20),
-        )(*in_hbm(token, mortar, get, put, normal_rows, gap0, pick3, layer0))
-
-    def contact(arrived, staged_arrays, low, high):
-        ready = [pltpu.with_memory_space_constraint(array, pltpu.VMEM) for array in (arrived, *staged_arrays)]
+    def contact(arrived, near_arrays, low, high):
+        here = [pltpu.with_memory_space_constraint(array, pltpu.VMEM) for array in (arrived, *near_arrays)]
         pushed = shaped((2 * segs, width), BF16)
         return pl.pallas_call(
             contact_kernel,
@@ -447,14 +436,16 @@
                 VMEM(message.shape, BF16),
                 VMEM(pushed.shape, BF16),
                 VMEM((segs - early,) + mortar.shape[3:], BF16),
-                pltpu.SemaphoreType.DMA((2,)),
+                pltpu.SemaphoreType.DMA((1 + PIECES,)),
                 pltpu.SemaphoreType.DMA(((segs - early) // GROUP,)),
             ],
             compiler_params=pltpu.CompilerParams(vmem_limit_bytes=16 * 2**20),
-        )(*ready, *in_hbm(mortar), low, high)
-
-    def bulk(field, layer0, low, high, pushed, keep_last):
-        outs = [shaped(disp.shape, F32), layer, layer, shaped(pick.shape, BF16)] + ([edge] if keep_last else [])
+        )(*here, *in_hbm(mortar), low, high)
+
+    def bulk(field, layer0, low, high, pushed, more):
+        outs = [shaped(disp.shape, F32), layer, layer, shaped(pick.shape, BF16)]
+        if more:
+            outs += [edge] + [shaped(array.shape, array.dtype) for array in ready]
         rows = (layers + 2) * blocks
         return staged(
             bulk_kernel,
@@ -462,20 +453,24 @@
             outs,
             [VMEM((rows, width), BF16), VMEM((rows, 3 * width), F32)],
             loose=(0, 1),
-            kept=(1, 2, 3),
+            kept=(1, 2, 3, 5, 6, 7, 8) if more else (1, 2, 3),
+            fills=[(mortar, early_part, 5), (get, (), 6), (put, (), 7), (normal_rows, (), 8)] if more else [],
         )
 
     arrived = exchange(sent)
     low, high = shift(low, 1), shift(high, -1)
-    sent, pushed = contact(arrived, stage(pick, disp), low, high)
+    sent, pushed = contact(arrived, [*ready, gap], low, high)
     returned = exchange(sent)
-    field, base, scale, near, last = bulk(disp, (disp, (0, 0)), low, high, pushed, True)
+    field, base, scale, near, last, *ready = bulk(disp, (disp, (0, 0)), low, high, pushed, True)
     sent, layer0, high = staged(
         next_kernel, [], [message, shaped((1, 1, blocks, width), F32), edge], [rows_scratch], direct=(returned, near, base, scale)
     )
     arrived = exchange(sent)
     low, high = shift(last, 1), shift(high, -1)
-    sent, pushed = contact(arrived, stage(pick, layer0), low, high)
+    (gap,) = staged(
+        known_kernel, [(layer0, (0, 0)), pick3, normal_rows, (gap0, (0, 0))], [shaped(gap0.shape[2:], F32)], kept=(0,)
+    )
+    sent, pushed = contact(arrived, [*ready, gap], low, high)
     returned = exchange(sent)
     field, base, scale, near = bulk(field, (layer0, (0, 0)), low, high, pushed, False)
     return pl.pallas_call(

time: 110 us -> 110 us (level)
  Pallas kernels: 30.6 us -> 28.9 us
  waiting for transfers between devices: 31.8 us -> 33.4 us
    pallas_call x2 -> x0, Pallas kernels: 3.69 us -> none  [stage(): pl.pallas_call(stage_kernel, out_shape=held, in_specs=[ANY] * 8, out_spec...]
    ppermute x4, waiting for transfers between devices: 3.83 us -> 6.43 us  [shift(): return lax.ppermute(block, 'slab', pairs)]
    pallas_call x6 -> x7, Pallas kernels: 16.9 us -> 19 us  [staged(): pl.pallas_call(kernel, out_shape=tuple((space(i, out) for i, out in enume...]
  transfers between devices with their start and end apart: 9 -> 9, of which waited for: 7 -> 7; matrix products, arithmetic and copies ran while one was open for 0% -> 0% of each run, Pallas kernels for 15% -> 14%
where the time goes in v5:
time: 110 us; the launch traced here: 109 us
  starting transfers between devices  46.8 us (43%)
  waiting for transfers between devices  33.4 us (30%)
  Pallas kernels  28.9 us (26%)
    all_to_all x5, starting transfers between devices, exchange(): return lax.all_to_all(parts, 'dom', 0, 0, tiled=True)  37.8 us
    all_to_all x5, waiting for transfers between devices, exchange(): return lax.all_to_all(parts, 'dom', 0, 0, tiled=True)  26.9 us
    pallas_call x7, Pallas kernels, staged(): pl.pallas_call(kernel, out_shape=tuple((space(i, out) for i, out in enume...  19 us
    pallas_call x2, Pallas kernels, contact(): pl.pallas_call(contact_kernel, out_shape=[pltpu.HBM(message.shape, BF16),...  9.08 us
    ppermute x4, starting transfers between devices, shift(): return lax.ppermute(block, 'slab', pairs)  8.99 us
    ppermute x4, waiting for transfers between devices, shift(): return lax.ppermute(block, 'slab', pairs)  6.43 us
  transfers between devices with their start and end apart: 9, of which 7 were waited for; matrix products, arithmetic and copies ran while one was open for 0% of the time, Pallas kernels for 14%

profile of v5, /device:TPU:1, one launch (start us, length us, event | category | flops | bytes accessed | tf_op | source)
XLA Modules:
  0.0 109.3 jit_solution(3548153129315740848)
XLA Ops:
  0.0 1.7 %shard_map.118.refs_7_ = f32[64,128]{1,0:T(8,128)} custom-call(s32[1,1,128]{2,1,0:T(1,128)} %refs_0_.3, s32[1,1,128]{2,1,0:T(1,128)} %refs_1_.2), custom_call_target="tpu_custom_call" | custom-call | tf_op jit(solution)/shard_map/pallas_call | solution.py:87
  1.7 13.0 %all-to-all-start = ((f32[64,1,128]{2,1,0:T(1,128)}), f32[64,1,128]{2,1,0:T(1,128)S(1)}, u32[]{:S(2)}, u32[]{:S(2)}) async-start(f32[64,1,128]{2,1,0:T(1,128)} %bitcast.1), calls=%async_computation | async-start | bytes 65536 | tf_op jit(solution)/shard_map/all_to_all | solution.py:377
  14.7 2.1 %shard_map.119 = (bf16[256,128]{1,0:T(8,128)(2,1)}, bf16[128,256]{1,0:T(8,128)(2,1)}, bf16[128,96]{1,0:T(8,128)(2,1)}, bf16[32,256]{1,0:T(8,128)(2,1)}, f32[128,...) custom-call(s32[1,1,128]{2,1,0:T(1,128)} %refs_0_.3, ...), custom_call_target="tpu_custom_call" | custom-call | tf_op jit(solution)/shard_map/pallas_call | solution.py:87
  16.8 7.3 %all-to-all-done = f32[64,1,128]{2,1,0:T(1,128)S(1)} async-done(((f32[64,1,128]{2,1,0:T(1,128)}), f32[64,1,128]{2,1,0:T(1,128)S(1)}, u32[]{:S(2)}, u32[]{:S(2)}) %all-to-all-start) | async-done | bytes 32800 | tf_op jit(solution)/shard_map/all_to_all | solution.py:377
  24.0 1.0 shard_map.120
  25.1 4.7 %all-to-all-start.1 = ((bf16[64,4,384]{2,1,0:T(4,128)(2,1)}), bf16[64,4,384]{2,1,0:T(4,128)(2,1)S(1)}, u32[]{:S(2)}, u32[]{:S(2)}) async-start(bf16[64,4,384]{2,1,0:T(4,128)(2,1)} %get-tuple-element.41), calls=%async_computation.1 | async-start | bytes 393216 | tf_op jit(solution)/shard_map/all_to_all | solution.py:377
  29.8 3.2 %collective-permute-start = (bf16[32,384]{1,0:T(8,128)(2,1)}, bf16[32,384]{1,0:T(8,128)(2,1)S(1)}, u32[]{:S(2)}, u32[]{:S(2)}) collective-permute-start(bf16[32,384]{1,0:T(8,128)(2,1)} %get-tuple-element.47), channel_id=1, source_target_pairs={{0,64},{64,128},{128,192},{1,65},{65,129},{129,193},{2,66},{66,130... | collective-permute-start | bytes 73736 | tf_op jit(solution)/shard_map/ppermute | solution.py:373
  33.0 1.3 %collective-permute-start.1 = (bf16[32,384]{1,0:T(8,128)(2,1)}, bf16[32,384]{1,0:T(8,128)(2,1)S(1)}, u32[]{:S(2)}, u32[]{:S(2)}) collective-permute-start(bf16[32,384]{1,0:T(8,128)(2,1)} %get-tuple-element.48), channel_id=1, source_target_pairs={{64,0},{128,64},{192,128},{65,1},{129,65},{193,129},{66,2},{130,66... | collective-permute-start | bytes 73736 | tf_op jit(solution)/shard_map/ppermute | solution.py:373
  34.3 0.0 collective-permute-done.low_token.refs_0_
  34.3 3.8 %collective-permute-done.1.high_token.refs_1_ = bf16[32,384]{1,0:T(8,128)(2,1)S(1)} collective-permute-done((bf16[32,384]{1,0:T(8,128)(2,1)}, bf16[32,384]{1,0:T(8,128)(2,1)S(1)}, u32[]{:S(2)}, u32[]{:S(2)}) %collective-permute-start.1) | collective-permute-done | bytes 24608 | tf_op jit(solution)/shard_map/ppermute | solution.py:373
  38.1 3.9 %all-to-all-done.1.in_ref = bf16[64,4,384]{2,1,0:T(4,128)(2,1)S(1)} async-done(((bf16[64,4,384]{2,1,0:T(4,128)(2,1)}), bf16[64,4,384]{2,1,0:T(4,128)(2,1)S(1)}, u32[]{:S(2)}, u32[]{:S(2)}) %all-to-all-start.1) | async-done | bytes 196640 | tf_op jit(solution)/shard_map/all_to_all | solution.py:377
  42.0 4.5 %shard_map.121 = (bf16[64,4,384]{2,1,0:T(4,128)(2,1)}, bf16[256,384]{1,0:T(8,128)(2,1)}) custom-call(bf16[64,4,384]{2,1,0:T(4,128)(2,1)S(1)} %all-to-all-done.1.in_ref, bf16[64,128,128]{2,1,0:T(8,128)(2,1)S(1)} %get-tuple-element.42.early_ref, bf16[128,256]{1,0:T(8,128)(2,1)S(1)} %get-tuple-element.43.get_ref, ...), custom_call_target="tpu_custom_call" | custom-call | tf_op jit(solution)/shard_map/pallas_call | solution.py:428
  46.6 7.7 %all-to-all-start.2 = ((bf16[64,4,384]{2,1,0:T(4,128)(2,1)}), bf16[64,4,384]{2,1,0:T(4,128)(2,1)S(1)}, u32[]{:S(2)}, u32[]{:S(2)}) async-start(bf16[64,4,384]{2,1,0:T(4,128)(2,1)} %get-tuple-element.49), calls=%async_computation.2 | async-start | bytes 393216 | tf_op jit(solution)/shard_map/all_to_all | solution.py:377
  54.2 6.4 %shard_map.122 = (f32[1,24,32,384]{3,2,1,0:T(8,128)}, f32[32,384]{1,0:T(8,128)S(1)}, f32[32,384]{1,0:T(8,128)S(1)}, bf16[256,128]{1,0:T(8,128)(2,1)S(1)}, bf16[3...) custom-call(bf16[32,384]{1,0:T(8,128)(2,1)S(1)} %collective-permute-, ...), custom_call_target="tpu_custom_call" | custom-call | tf_op jit(solution)/shard_map/pallas_call | solution.py:87
  60.6 5.6 %all-to-all-done.2.refs_0_ = bf16[64,4,384]{2,1,0:T(4,128)(2,1)S(1)} async-done(((bf16[64,4,384]{2,1,0:T(4,128)(2,1)}), bf16[64,4,384]{2,1,0:T(4,128)(2,1)S(1)}, u32[]{:S(2)}, u32[]{:S(2)}) %all-to-all-start.2) | async-done | bytes 196640 | tf_op jit(solution)/shard_map/all_to_all | solution.py:377
  66.2 1.1 %shard_map.123 = (bf16[64,4,384]{2,1,0:T(4,128)(2,1)}, f32[1,1,32,384]{3,2,1,0:T(8,128)}, bf16[32,384]{1,0:T(8,128)(2,1)}) custom-call(bf16[64,4,384]{2,1,0:T(4,128)(2,1)S(1)} %all-to-all-done.2.refs_0_, bf16[256,128]{1,0:T(8,128)(2,1)S(1)} %get-tuple-element.56.refs_1_, f32[32,384]{1,0:T(8,128)S(1)} %get-tuple-element.57.refs_2_, ...), custom_call_target="tpu_custom_call" | custom-call | tf_op jit(solution)/shard_map/pallas_call | solution.py:87
  67.4 4.7 %all-to-all-start.3 = ((bf16[64,4,384]{2,1,0:T(4,128)(2,1)}), bf16[64,4,384]{2,1,0:T(4,128)(2,1)S(1)}, u32[]{:S(2)}, u32[]{:S(2)}) async-start(bf16[64,4,384]{2,1,0:T(4,128)(2,1)} %get-tuple-element.59), calls=%async_computation.3 | async-start | bytes 393216 | tf_op jit(solution)/shard_map/all_to_all | solution.py:377
  72.1 3.2 %collective-permute-start.2 = (bf16[32,384]{1,0:T(8,128)(2,1)}, bf16[32,384]{1,0:T(8,128)(2,1)S(1)}, u32[]{:S(2)}, u32[]{:S(2)}) collective-permute-start(bf16[32,384]{1,0:T(8,128)(2,1)} %get-tuple-element.66), channel_id=1, source_target_pairs={{0,64},{64,128},{128,192},{1,65},{65,129},{129,193},{2,66},{66,130... | collective-permute-start | bytes 73736 | tf_op jit(solution)/shard_map/ppermute | solution.py:373
  75.3 1.3 %collective-permute-start.3 = (bf16[32,384]{1,0:T(8,128)(2,1)}, bf16[32,384]{1,0:T(8,128)(2,1)S(1)}, u32[]{:S(2)}, u32[]{:S(2)}) collective-permute-start(bf16[32,384]{1,0:T(8,128)(2,1)} %get-tuple-element.67), channel_id=1, source_target_pairs={{64,0},{128,64},{192,128},{65,1},{129,65},{193,129},{66,2},{130,66... | collective-permute-start | bytes 73736 | tf_op jit(solution)/shard_map/ppermute | solution.py:373
  76.6 1.1 %shard_map.124.known_ref = f32[128,128]{1,0:T(8,128)S(1)} custom-call(f32[1,1,32,384]{3,2,1,0:T(8,128)} %get-tuple-element.64.refs_0_.refs_3_, bf16[128,96]{1,0:T(8,128)(2,1)} %get-tuple-element.65.refs_1_, f32[128,384]{1,0:T(8,128)} %get-tuple-element.55.refs_15_.refs_2_, f32[1,1,128,128]{3,2,1,0:T(8,128)} %refs_3_.5), custom_call_target="tpu_custom_call" | custom-call | tf_op jit(solution)/shard_map/pallas_call | solution.py:87
  77.7 0.0 collective-permute-done.2.low_token.refs_0_
  77.7 2.7 %collective-permute-done.3.high_token.refs_1_ = bf16[32,384]{1,0:T(8,128)(2,1)S(1)} collective-permute-done((bf16[32,384]{1,0:T(8,128)(2,1)}, bf16[32,384]{1,0:T(8,128)(2,1)S(1)}, u32[]{:S(2)}, u32[]{:S(2)}) %collective-permute-start.3) | collective-permute-done | bytes 24608 | tf_op jit(solution)/shard_map/ppermute | solution.py:373
  80.4 3.7 %all-to-all-done.3.in_ref = bf16[64,4,384]{2,1,0:T(4,128)(2,1)S(1)} async-done(((bf16[64,4,384]{2,1,0:T(4,128)(2,1)}), bf16[64,4,384]{2,1,0:T(4,128)(2,1)S(1)}, u32[]{:S(2)}, u32[]{:S(2)}) %all-to-all-start.3) | async-done | bytes 196640 | tf_op jit(solution)/shard_map/all_to_all | solution.py:377
  84.1 4.5 %shard_map.125 = (bf16[64,4,384]{2,1,0:T(4,128)(2,1)}, bf16[256,384]{1,0:T(8,128)(2,1)}) custom-call(bf16[64,4,384]{2,1,0:T(4,128)(2,1)S(1)} %all-to-all-done.3.in_ref, bf16[64,128,128]{2,1,0:T(8,128)(2,1)S(1)} %get-tuple-element.60.early_ref, bf16[128,256]{1,0:T(8,128)(2,1)S(1)} %get-tuple-element.61.get_ref, ...), custom_call_target="tpu_custom_call" | custom-call | tf_op jit(solution)/shard_map/pallas_call | solution.py:428
  88.7 7.7 %all-to-all-start.4 = ((bf16[64,4,384]{2,1,0:T(4,128)(2,1)}), bf16[64,4,384]{2,1,0:T(4,128)(2,1)S(1)}, u32[]{:S(2)}, u32[]{:S(2)}) async-start(bf16[64,4,384]{2,1,0:T(4,128)(2,1)} %get-tuple-element.68), calls=%async_computation.4 | async-start | bytes 393216 | tf_op jit(solution)/shard_map/all_to_all | solution.py:377
  96.4 5.6 %shard_map.126 = (f32[1,24,32,384]{3,2,1,0:T(8,128)}, f32[32,384]{1,0:T(8,128)S(1)}, f32[32,384]{1,0:T(8,128)S(1)}, bf16[256,128]{1,0:T(8,128)(2,1)S(1)}) custom-call(bf16[32,384]{1,0:T(8,128)(2,1)S(1)} %collective-permute-done.2.low_token.refs_0_, bf16[32,384]{1,0:T(8,128)(2,1)S(1)} %collective-permute-done.3.high_token.refs_1_, ...), custom_call_target="tpu_custom_call" | custom-call | tf_op jit(solution)/shard_map/pallas_call | solution.py:87
  102.0 6.4 %all-to-all-done.4.in_ref = bf16[64,4,384]{2,1,0:T(4,128)(2,1)S(1)} async-done(((bf16[64,4,384]{2,1,0:T(4,128)(2,1)}), bf16[64,4,384]{2,1,0:T(4,128)(2,1)S(1)}, u32[]{:S(2)}, u32[]{:S(2)}) %all-to-all-start.4) | async-done | bytes 196640 | tf_op jit(solution)/shard_map/all_to_all | solution.py:377
  108.4 0.8 shard_map.127
Async XLA Ops:
  1.7 22.4 %all-to-all-start = ((f32[64,1,128]{2,1,0:T(1,128)}), f32[64,1,128]{2,1,0:T(1,128)S(1)}, u32[]{:S(2)}, u32[]{:S(2)}) async-start(f32[64,1,128]{2,1,0:T(1,128)} %bitcast.1), calls=%async_computation | async-start | bytes 65536 | tf_op jit(solution)/shard_map/all_to_all | solution.py:377
  25.1 16.9 %all-to-all-start.1 = ((bf16[64,4,384]{2,1,0:T(4,128)(2,1)}), bf16[64,4,384]{2,1,0:T(4,128)(2,1)S(1)}, u32[]{:S(2)}, u32[]{:S(2)}) async-start(bf16[64,4,384]{2,1,0:T(4,128)(2,1)} %get-tuple-element.41), calls=%async_computation.1 | async-start | bytes 393216 | tf_op jit(solution)/shard_map/all_to_all | solution.py:377
  29.8 4.5 %collective-permute-start = (bf16[32,384]{1,0:T(8,128)(2,1)}, bf16[32,384]{1,0:T(8,128)(2,1)S(1)}, u32[]{:S(2)}, u32[]{:S(2)}) collective-permute-start(bf16[32,384]{1,0:T(8,128)(2,1)} %get-tuple-element.47), channel_id=1, source_target_pairs={{0,64},{64,128},{128,192},{1,65},{65,129},{129,193},{2,66},{66,130... | collective-permute-start | bytes 73736 | tf_op jit(solution)/shard_map/ppermute | solution.py:373
  33.0 5.1 %collective-permute-start.1 = (bf16[32,384]{1,0:T(8,128)(2,1)}, bf16[32,384]{1,0:T(8,128)(2,1)S(1)}, u32[]{:S(2)}, u32[]{:S(2)}) collective-permute-start(bf16[32,384]{1,0:T(8,128)(2,1)} %get-tuple-element.48), channel_id=1, source_target_pairs={{64,0},{128,64},{192,128},{65,1},{129,65},{193,129},{66,2},{130,66... | collective-permute-start | bytes 73736 | tf_op jit(solution)/shard_map/ppermute | solution.py:373
  46.6 19.7 %all-to-all-start.2 = ((bf16[64,4,384]{2,1,0:T(4,128)(2,1)}), bf16[64,4,384]{2,1,0:T(4,128)(2,1)S(1)}, u32[]{:S(2)}, u32[]{:S(2)}) async-start(bf16[64,4,384]{2,1,0:T(4,128)(2,1)} %get-tuple-element.49), calls=%async_computation.2 | async-start | bytes 393216 | tf_op jit(solution)/shard_map/all_to_all | solution.py:377
  67.4 16.8 %all-to-all-start.3 = ((bf16[64,4,384]{2,1,0:T(4,128)(2,1)}), bf16[64,4,384]{2,1,0:T(4,128)(2,1)S(1)}, u32[]{:S(2)}, u32[]{:S(2)}) async-start(bf16[64,4,384]{2,1,0:T(4,128)(2,1)} %get-tuple-element.59), calls=%async_computation.3 | async-start | bytes 393216 | tf_op jit(solution)/shard_map/all_to_all | solution.py:377
  72.1 5.6 %collective-permute-start.2 = (bf16[32,384]{1,0:T(8,128)(2,1)}, bf16[32,384]{1,0:T(8,128)(2,1)S(1)}, u32[]{:S(2)}, u32[]{:S(2)}) collective-permute-start(bf16[32,384]{1,0:T(8,128)(2,1)} %get-tuple-element.66), channel_id=1, source_target_pairs={{0,64},{64,128},{128,192},{1,65},{65,129},{129,193},{2,66},{66,130... | collective-permute-start | bytes 73736 | tf_op jit(solution)/shard_map/ppermute | solution.py:373
  75.3 5.1 %collective-permute-start.3 = (bf16[32,384]{1,0:T(8,128)(2,1)}, bf16[32,384]{1,0:T(8,128)(2,1)S(1)}, u32[]{:S(2)}, u32[]{:S(2)}) collective-permute-start(bf16[32,384]{1,0:T(8,128)(2,1)} %get-tuple-element.67), channel_id=1, source_target_pairs={{64,0},{128,64},{192,128},{65,1},{129,65},{193,129},{66,2},{130,66... | collective-permute-start | bytes 73736 | tf_op jit(solution)/shard_map/ppermute | solution.py:373
  88.7 19.7 %all-to-all-start.4 = ((bf16[64,4,384]{2,1,0:T(4,128)(2,1)}), bf16[64,4,384]{2,1,0:T(4,128)(2,1)S(1)}, u32[]{:S(2)}, u32[]{:S(2)}) async-start(bf16[64,4,384]{2,1,0:T(4,128)(2,1)} %get-tuple-element.68), calls=%async_computation.4 | async-start | bytes 393216 | tf_op jit(solution)/shard_map/all_to_all | solution.py:377

commit v6 on v5

--- a/solution.py
+++ b/solution.py
@@ -130,7 +130,7 @@
 
 
 def prep_kernel(take, out, give):
-    put_ref, get_ref, take_ref, sum_ref, normal_rows_ref, low_ref, high_ref, surface_ref, _, get_v, put_v, normal_v, known_ref = out
+    put_ref, get_ref, take_ref, sum_ref, normal_rows_ref, low_ref, high_ref, surface_ref, _, get_v, put_v, known_ref = out
     surface = take(3)[...].astype(BF16)
     surface_ref[...] = copies(surface)
     high_ref[...] = surface
@@ -158,7 +158,6 @@
     give(4)
     put_v[...] = put_ref[...]
     get_v[...] = get_ref[...]
-    normal_v[...] = normal_rows
     known_ref[...] = known(take(5)[...], normal_rows, dot(pick, split3(take(3)[...])))
 
 
@@ -214,18 +213,15 @@
 
 
 def contact_kernel(
-    in_ref, early_ref, get_ref, put_ref, normal_ref, known_ref, mortar_hbm, low_token, high_token,
-    out_hbm, pushed_hbm, scratch, back_ref, out_ref, pushed_ref, later_ref, sems, later_sems,
+    in_ref, early_ref, get_ref, put_ref, known_ref, normal_hbm, mortar_hbm, low_token, high_token,
+    out_hbm, pushed_hbm, scratch, back_ref, out_ref, pushed_ref, normal_ref, later_ref, sems, later_sems,
 ):
     early, _, nodes = early_ref.shape
     segs = early + later_ref.shape[0]
-    later = []
-    for k in range(0, segs - early, GROUP):
-        copy = pltpu.make_async_copy(
-            mortar_hbm.at[0, 0, pl.ds(early + k, GROUP)], later_ref.at[pl.ds(k, GROUP)], later_sems.at[k // GROUP]
-        )
-        copy.start()
-        later.append(copy)
+    normals = pltpu.make_async_copy(normal_hbm, normal_ref, later_sems.at[0])
+    later = pltpu.make_async_copy(mortar_hbm.at[0, 0, pl.ds(early, segs - early)], later_ref, later_sems.at[1])
+    normals.start()
+    later.start()
     member = lax.rem(iota((3 * GROUP, nodes), 0), GROUP)
     place_in = lax.rem(member, 4)
     block_of = lax.div(member, 4)
@@ -240,14 +236,16 @@
             result = jnp.where(block_of == b, parts[b], result)
         return result
 
+    normals.wait()
     for g in range(segs // GROUP):
         own = slice(GROUP * g, GROUP * (g + 1))
+        if GROUP * g == early:
+            later.wait()
         um = jnp.concatenate(columns(master[own]), axis=0)
         normal = jnp.concatenate(columns(normal_ref[own, :]), axis=0)
         mortar_ref, start = early_ref, GROUP * g
         if start >= early:
             mortar_ref, start = later_ref, start - early
-            later[start // GROUP].wait()
         weights = []
         for s in range(start, start + GROUP, 4):
             left = mortar_ref[s : s + 2].reshape(2 * nodes, nodes)
@@ -390,7 +388,7 @@
     edge = shaped((blocks, width), BF16)
     layer = shaped((blocks, width), F32)
 
-    early = max(segs // 2, GROUP)
+    early = max(segs * 5 // 8 // GROUP, 1) * GROUP
     early_part = (0, 0, pl.ds(0, early))
     (asked,) = staged(
         lambda *refs: request_kernel(blocks, *refs), [seg_src, seg_master], [shaped((count, wide), F32)], free_outs=True
@@ -410,11 +408,10 @@
             shaped((early,) + mortar.shape[3:], BF16),
             shaped((segs, slots), BF16),
             shaped((slots, segs), BF16),
-            shaped((segs, width), F32),
             shaped(gap0.shape[2:], F32),
         ],
         tokens=[asked],
-        kept=(7, 8, 9, 10, 11, 12),
+        kept=(7, 8, 9, 10, 11),
         fills=[(mortar, early_part, 8)],
     )
     asked = exchange(asked.reshape(count, 1, wide)).reshape(count, wide)
@@ -428,19 +425,20 @@
         return pl.pallas_call(
             contact_kernel,
             out_shape=[pltpu.HBM(message.shape, BF16), pltpu.HBM(pushed.shape, BF16)],
-            in_specs=[IN_VMEM] * 6 + [ANY] * 3,
+            in_specs=[IN_VMEM] * 5 + [ANY] * 4,
             out_specs=[ANY] * 2,
             scratch_shapes=[
                 rows_scratch,
                 VMEM((segs, width), BF16),
                 VMEM(message.shape, BF16),
                 VMEM(pushed.shape, BF16),
+                VMEM(normal_rows.shape, F32),
                 VMEM((segs - early,) + mortar.shape[3:], BF16),
                 pltpu.SemaphoreType.DMA((1 + PIECES,)),
-                pltpu.SemaphoreType.DMA(((segs - early) // GROUP,)),
+                pltpu.SemaphoreType.DMA((2,)),
             ],
             compiler_params=pltpu.CompilerParams(vmem_limit_bytes=16 * 2**20),
-        )(*here, *in_hbm(mortar), low, high)
+        )(*here, *in_hbm(normal_rows, mortar), low, high)
 
     def bulk(field, layer0, low, high, pushed, more):
         outs = [shaped(disp.shape, F32), layer, layer, shaped(pick.shape, BF16)]
@@ -453,8 +451,8 @@
             outs,
             [VMEM((rows, width), BF16), VMEM((rows, 3 * width), F32)],
             loose=(0, 1),
-            kept=(1, 2, 3, 5, 6, 7, 8) if more else (1, 2, 3),
-            fills=[(mortar, early_part, 5), (get, (), 6), (put, (), 7), (normal_rows, (), 8)] if more else [],
+            kept=(1, 2, 3, 5, 6, 7) if more else (1, 2, 3),
+            fills=[(mortar, early_part, 5), (get, (), 6), (put, (), 7)] if more else [],
         )
 
     arrived = exchange(sent)

time: 110 us -> 110 us (level)
  Pallas kernels: 28.9 us -> 30.2 us
  transfers between devices with their start and end apart: 9 -> 9, of which waited for: 7 -> 7; matrix products, arithmetic and copies ran while one was open for 0% -> 0% of each run, Pallas kernels for 14% -> 15%
where the time goes in v6:
time: 110 us
  starting transfers between devices  46.9 us (43%)
  waiting for transfers between devices  32.5 us (30%)
  Pallas kernels  30.2 us (27%)
    all_to_all x5, starting transfers between devices, exchange(): return lax.all_to_all(parts, 'dom', 0, 0, tiled=True)  37.9 us
    all_to_all x5, waiting for transfers between devices, exchange(): return lax.all_to_all(parts, 'dom', 0, 0, tiled=True)  26.1 us
    pallas_call x7, Pallas kernels, staged(): pl.pallas_call(kernel, out_shape=tuple((space(i, out) for i, out in enume...  19.8 us
    pallas_call x2, Pallas kernels, contact(): pl.pallas_call(contact_kernel, out_shape=[pltpu.HBM(message.shape, BF16),...  9.49 us
    ppermute x4, starting transfers between devices, shift(): return lax.ppermute(block, 'slab', pairs)  8.99 us
    ppermute x4, waiting for transfers between devices, shift(): return lax.ppermute(block, 'slab', pairs)  6.43 us
  transfers between devices with their start and end apart: 9, of which 7 were waited for; matrix products, arithmetic and copies ran while one was open for 0% of the time, Pallas kernels for 15%

profile of v6, /device:TPU:1, one launch (start us, length us, event | category | flops | bytes accessed | tf_op | source)
XLA Modules:
  0.0 109.8 jit_solution(15407323754914857501)
XLA Ops:
  0.0 1.7 %shard_map.118.refs_7_ = f32[64,128]{1,0:T(8,128)} custom-call(s32[1,1,128]{2,1,0:T(1,128)} %refs_0_.3, s32[1,1,128]{2,1,0:T(1,128)} %refs_1_.2), custom_call_target="tpu_custom_call" | custom-call | tf_op jit(solution)/shard_map/pallas_call | solution.py:87
  1.7 13.0 %all-to-all-start = ((f32[64,1,128]{2,1,0:T(1,128)}), f32[64,1,128]{2,1,0:T(1,128)S(1)}, u32[]{:S(2)}, u32[]{:S(2)}) async-start(f32[64,1,128]{2,1,0:T(1,128)} %bitcast.1), calls=%async_computation | async-start | bytes 65536 | tf_op jit(solution)/shard_map/all_to_all | solution.py:375
  14.7 2.9 %shard_map.119 = (bf16[256,128]{1,0:T(8,128)(2,1)}, bf16[128,256]{1,0:T(8,128)(2,1)}, bf16[128,96]{1,0:T(8,128)(2,1)}, bf16[32,256]{1,0:T(8,128)(2,1)}, f32[128,...) custom-call(s32[1,1,128]{2,1,0:T(1,128)} %refs_0_.3, ...), custom_call_target="tpu_custom_call" | custom-call | tf_op jit(solution)/shard_map/pallas_call | solution.py:87
  17.5 6.5 %all-to-all-done = f32[64,1,128]{2,1,0:T(1,128)S(1)} async-done(((f32[64,1,128]{2,1,0:T(1,128)}), f32[64,1,128]{2,1,0:T(1,128)S(1)}, u32[]{:S(2)}, u32[]{:S(2)}) %all-to-all-start) | async-done | bytes 32800 | tf_op jit(solution)/shard_map/all_to_all | solution.py:375
  24.0 1.0 shard_map.120
  25.1 4.7 %all-to-all-start.1 = ((bf16[64,4,384]{2,1,0:T(4,128)(2,1)}), bf16[64,4,384]{2,1,0:T(4,128)(2,1)S(1)}, u32[]{:S(2)}, u32[]{:S(2)}) async-start(bf16[64,4,384]{2,1,0:T(4,128)(2,1)} %get-tuple-element.39), calls=%async_computation.1 | async-start | bytes 393216 | tf_op jit(solution)/shard_map/all_to_all | solution.py:375
  29.8 3.2 %collective-permute-start = (bf16[32,384]{1,0:T(8,128)(2,1)}, bf16[32,384]{1,0:T(8,128)(2,1)S(1)}, u32[]{:S(2)}, u32[]{:S(2)}) collective-permute-start(bf16[32,384]{1,0:T(8,128)(2,1)} %get-tuple-element.45), channel_id=1, source_target_pairs={{0,64},{64,128},{128,192},{1,65},{65,129},{129,193},{2,66},{66,130... | collective-permute-start | bytes 73736 | tf_op jit(solution)/shard_map/ppermute | solution.py:371
  33.0 1.3 %collective-permute-start.1 = (bf16[32,384]{1,0:T(8,128)(2,1)}, bf16[32,384]{1,0:T(8,128)(2,1)S(1)}, u32[]{:S(2)}, u32[]{:S(2)}) collective-permute-start(bf16[32,384]{1,0:T(8,128)(2,1)} %get-tuple-element.46), channel_id=1, source_target_pairs={{64,0},{128,64},{192,128},{65,1},{129,65},{193,129},{66,2},{130,66... | collective-permute-start | bytes 73736 | tf_op jit(solution)/shard_map/ppermute | solution.py:371
  34.3 0.0 collective-permute-done.low_token.refs_0_
  34.3 3.8 %collective-permute-done.1.high_token.refs_1_ = bf16[32,384]{1,0:T(8,128)(2,1)S(1)} collective-permute-done((bf16[32,384]{1,0:T(8,128)(2,1)}, bf16[32,384]{1,0:T(8,128)(2,1)S(1)}, u32[]{:S(2)}, u32[]{:S(2)}) %collective-permute-start.1) | collective-permute-done | bytes 24608 | tf_op jit(solution)/shard_map/ppermute | solution.py:371
  38.1 3.9 %all-to-all-done.1.in_ref = bf16[64,4,384]{2,1,0:T(4,128)(2,1)S(1)} async-done(((bf16[64,4,384]{2,1,0:T(4,128)(2,1)}), bf16[64,4,384]{2,1,0:T(4,128)(2,1)S(1)}, u32[]{:S(2)}, u32[]{:S(2)}) %all-to-all-start.1) | async-done | bytes 196640 | tf_op jit(solution)/shard_map/all_to_all | solution.py:375
  42.0 4.7 %shard_map.121 = (bf16[64,4,384]{2,1,0:T(4,128)(2,1)}, bf16[256,384]{1,0:T(8,128)(2,1)}) custom-call(bf16[64,4,384]{2,1,0:T(4,128)(2,1)S(1)} %all-to-all-done.1.in_ref, bf16[80,128,128]{2,1,0:T(8,128)(2,1)S(1)} %get-tuple-element.40.early_ref, bf16[128,256]{1,0:T(8,128)(2,1)S(1)} %get-tuple-element.41.get_ref, ...), custom_call_target="tpu_custom_call" | custom-call | tf_op jit(solution)/shard_map/pallas_call | solution.py:425
  46.8 7.7 %all-to-all-start.2 = ((bf16[64,4,384]{2,1,0:T(4,128)(2,1)}), bf16[64,4,384]{2,1,0:T(4,128)(2,1)S(1)}, u32[]{:S(2)}, u32[]{:S(2)}) async-start(bf16[64,4,384]{2,1,0:T(4,128)(2,1)} %get-tuple-element.47), calls=%async_computation.2 | async-start | bytes 393216 | tf_op jit(solution)/shard_map/all_to_all | solution.py:375
  54.4 6.5 %shard_map.122 = (f32[1,24,32,384]{3,2,1,0:T(8,128)}, f32[32,384]{1,0:T(8,128)S(1)}, f32[32,384]{1,0:T(8,128)S(1)}, bf16[256,128]{1,0:T(8,128)(2,1)S(1)}, bf16[3...) custom-call(bf16[32,384]{1,0:T(8,128)(2,1)S(1)} %collective-permute-, ...), custom_call_target="tpu_custom_call" | custom-call | tf_op jit(solution)/shard_map/pallas_call | solution.py:87
  60.9 5.5 %all-to-all-done.2.refs_0_ = bf16[64,4,384]{2,1,0:T(4,128)(2,1)S(1)} async-done(((bf16[64,4,384]{2,1,0:T(4,128)(2,1)}), bf16[64,4,384]{2,1,0:T(4,128)(2,1)S(1)}, u32[]{:S(2)}, u32[]{:S(2)}) %all-to-all-start.2) | async-done | bytes 196640 | tf_op jit(solution)/shard_map/all_to_all | solution.py:375
  66.4 1.1 %shard_map.123 = (bf16[64,4,384]{2,1,0:T(4,128)(2,1)}, f32[1,1,32,384]{3,2,1,0:T(8,128)}, bf16[32,384]{1,0:T(8,128)(2,1)}) custom-call(bf16[64,4,384]{2,1,0:T(4,128)(2,1)S(1)} %all-to-all-done.2.refs_0_, bf16[256,128]{1,0:T(8,128)(2,1)S(1)} %get-tuple-element.53.refs_1_, f32[32,384]{1,0:T(8,128)S(1)} %get-tuple-element.54.refs_2_, ...), custom_call_target="tpu_custom_call" | custom-call | tf_op jit(solution)/shard_map/pallas_call | solution.py:87
  67.6 4.8 %all-to-all-start.3 = ((bf16[64,4,384]{2,1,0:T(4,128)(2,1)}), bf16[64,4,384]{2,1,0:T(4,128)(2,1)S(1)}, u32[]{:S(2)}, u32[]{:S(2)}) async-start(bf16[64,4,384]{2,1,0:T(4,128)(2,1)} %get-tuple-element.56), calls=%async_computation.3 | async-start | bytes 393216 | tf_op jit(solution)/shard_map/all_to_all | solution.py:375
  72.4 3.2 %collective-permute-start.2 = (bf16[32,384]{1,0:T(8,128)(2,1)}, bf16[32,384]{1,0:T(8,128)(2,1)S(1)}, u32[]{:S(2)}, u32[]{:S(2)}) collective-permute-start(bf16[32,384]{1,0:T(8,128)(2,1)} %get-tuple-element.62), channel_id=1, source_target_pairs={{0,64},{64,128},{128,192},{1,65},{65,129},{129,193},{2,66},{66,130... | collective-permute-start | bytes 73736 | tf_op jit(solution)/shard_map/ppermute | solution.py:371
  75.6 1.3 %collective-permute-start.3 = (bf16[32,384]{1,0:T(8,128)(2,1)}, bf16[32,384]{1,0:T(8,128)(2,1)S(1)}, u32[]{:S(2)}, u32[]{:S(2)}) collective-permute-start(bf16[32,384]{1,0:T(8,128)(2,1)} %get-tuple-element.63), channel_id=1, source_target_pairs={{64,0},{128,64},{192,128},{65,1},{129,65},{193,129},{66,2},{130,66... | collective-permute-start | bytes 73736 | tf_op jit(solution)/shard_map/ppermute | solution.py:371
  76.9 1.1 shard_map.124.known_ref
  78.0 0.0 collective-permute-done.2.low_token.refs_0_
  78.0 2.7 %collective-permute-done.3.high_token.refs_1_ = bf16[32,384]{1,0:T(8,128)(2,1)S(1)} collective-permute-done((bf16[32,384]{1,0:T(8,128)(2,1)}, bf16[32,384]{1,0:T(8,128)(2,1)S(1)}, u32[]{:S(2)}, u32[]{:S(2)}) %collective-permute-start.3) | collective-permute-done | bytes 24608 | tf_op jit(solution)/shard_map/ppermute | solution.py:371
  80.7 3.7 %all-to-all-done.3.in_ref = bf16[64,4,384]{2,1,0:T(4,128)(2,1)S(1)} async-done(((bf16[64,4,384]{2,1,0:T(4,128)(2,1)}), bf16[64,4,384]{2,1,0:T(4,128)(2,1)S(1)}, u32[]{:S(2)}, u32[]{:S(2)}) %all-to-all-start.3) | async-done | bytes 196640 | tf_op jit(solution)/shard_map/all_to_all | solution.py:375
  84.4 4.7 %shard_map.125 = (bf16[64,4,384]{2,1,0:T(4,128)(2,1)}, bf16[256,384]{1,0:T(8,128)(2,1)}) custom-call(bf16[64,4,384]{2,1,0:T(4,128)(2,1)S(1)} %all-to-all-done.3.in_ref, bf16[80,128,128]{2,1,0:T(8,128)(2,1)S(1)} %get-tuple-element.57.early_ref, bf16[128,256]{1,0:T(8,128)(2,1)S(1)} %get-tuple-element.58.get_ref, ...), custom_call_target="tpu_custom_call" | custom-call | tf_op jit(solution)/shard_map/pallas_call | solution.py:425
  89.2 7.7 %all-to-all-start.4 = ((bf16[64,4,384]{2,1,0:T(4,128)(2,1)}), bf16[64,4,384]{2,1,0:T(4,128)(2,1)S(1)}, u32[]{:S(2)}, u32[]{:S(2)}) async-start(bf16[64,4,384]{2,1,0:T(4,128)(2,1)} %get-tuple-element.64), calls=%async_computation.4 | async-start | bytes 393216 | tf_op jit(solution)/shard_map/all_to_all | solution.py:375
  96.9 5.6 %shard_map.126 = (f32[1,24,32,384]{3,2,1,0:T(8,128)}, f32[32,384]{1,0:T(8,128)S(1)}, f32[32,384]{1,0:T(8,128)S(1)}, bf16[256,128]{1,0:T(8,128)(2,1)S(1)}) custom-call(bf16[32,384]{1,0:T(8,128)(2,1)S(1)} %collective-permute-done.2.low_token.refs_0_, bf16[32,384]{1,0:T(8,128)(2,1)S(1)} %collective-permute-done.3.high_token.refs_1_, ...), custom_call_target="tpu_custom_call" | custom-call | tf_op jit(solution)/shard_map/pallas_call | solution.py:87
  102.5 6.4 %all-to-all-done.4.in_ref = bf16[64,4,384]{2,1,0:T(4,128)(2,1)S(1)} async-done(((bf16[64,4,384]{2,1,0:T(4,128)(2,1)}), bf16[64,4,384]{2,1,0:T(4,128)(2,1)S(1)}, u32[]{:S(2)}, u32[]{:S(2)}) %all-to-all-start.4) | async-done | bytes 196640 | tf_op jit(solution)/shard_map/all_to_all | solution.py:375
  108.9 0.8 shard_map.127
Async XLA Ops:
  1.7 22.4 %all-to-all-start = ((f32[64,1,128]{2,1,0:T(1,128)}), f32[64,1,128]{2,1,0:T(1,128)S(1)}, u32[]{:S(2)}, u32[]{:S(2)}) async-start(f32[64,1,128]{2,1,0:T(1,128)} %bitcast.1), calls=%async_computation | async-start | bytes 65536 | tf_op jit(solution)/shard_map/all_to_all | solution.py:375
  25.1 16.9 %all-to-all-start.1 = ((bf16[64,4,384]{2,1,0:T(4,128)(2,1)}), bf16[64,4,384]{2,1,0:T(4,128)(2,1)S(1)}, u32[]{:S(2)}, u32[]{:S(2)}) async-start(bf16[64,4,384]{2,1,0:T(4,128)(2,1)} %get-tuple-element.39), calls=%async_computation.1 | async-start | bytes 393216 | tf_op jit(solution)/shard_map/all_to_all | solution.py:375
  29.8 4.5 %collective-permute-start = (bf16[32,384]{1,0:T(8,128)(2,1)}, bf16[32,384]{1,0:T(8,128)(2,1)S(1)}, u32[]{:S(2)}, u32[]{:S(2)}) collective-permute-start(bf16[32,384]{1,0:T(8,128)(2,1)} %get-tuple-element.45), channel_id=1, source_target_pairs={{0,64},{64,128},{128,192},{1,65},{65,129},{129,193},{2,66},{66,130... | collective-permute-start | bytes 73736 | tf_op jit(solution)/shard_map/ppermute | solution.py:371
  33.0 5.1 %collective-permute-start.1 = (bf16[32,384]{1,0:T(8,128)(2,1)}, bf16[32,384]{1,0:T(8,128)(2,1)S(1)}, u32[]{:S(2)}, u32[]{:S(2)}) collective-permute-start(bf16[32,384]{1,0:T(8,128)(2,1)} %get-tuple-element.46), channel_id=1, source_target_pairs={{64,0},{128,64},{192,128},{65,1},{129,65},{193,129},{66,2},{130,66... | collective-permute-start | bytes 73736 | tf_op jit(solution)/shard_map/ppermute | solution.py:371
  46.8 19.7 %all-to-all-start.2 = ((bf16[64,4,384]{2,1,0:T(4,128)(2,1)}), bf16[64,4,384]{2,1,0:T(4,128)(2,1)S(1)}, u32[]{:S(2)}, u32[]{:S(2)}) async-start(bf16[64,4,384]{2,1,0:T(4,128)(2,1)} %get-tuple-element.47), calls=%async_computation.2 | async-start | bytes 393216 | tf_op jit(solution)/shard_map/all_to_all | solution.py:375
  67.6 16.8 %all-to-all-start.3 = ((bf16[64,4,384]{2,1,0:T(4,128)(2,1)}), bf16[64,4,384]{2,1,0:T(4,128)(2,1)S(1)}, u32[]{:S(2)}, u32[]{:S(2)}) async-start(bf16[64,4,384]{2,1,0:T(4,128)(2,1)} %get-tuple-element.56), calls=%async_computation.3 | async-start | bytes 393216 | tf_op jit(solution)/shard_map/all_to_all | solution.py:375
  72.4 5.6 %collective-permute-start.2 = (bf16[32,384]{1,0:T(8,128)(2,1)}, bf16[32,384]{1,0:T(8,128)(2,1)S(1)}, u32[]{:S(2)}, u32[]{:S(2)}) collective-permute-start(bf16[32,384]{1,0:T(8,128)(2,1)} %get-tuple-element.62), channel_id=1, source_target_pairs={{0,64},{64,128},{128,192},{1,65},{65,129},{129,193},{2,66},{66,130... | collective-permute-start | bytes 73736 | tf_op jit(solution)/shard_map/ppermute | solution.py:371
  75.6 5.1 %collective-permute-start.3 = (bf16[32,384]{1,0:T(8,128)(2,1)}, bf16[32,384]{1,0:T(8,128)(2,1)S(1)}, u32[]{:S(2)}, u32[]{:S(2)}) collective-permute-start(bf16[32,384]{1,0:T(8,128)(2,1)} %get-tuple-element.63), channel_id=1, source_target_pairs={{64,0},{128,64},{192,128},{65,1},{129,65},{193,129},{66,2},{130,66... | collective-permute-start | bytes 73736 | tf_op jit(solution)/shard_map/ppermute | solution.py:371
  89.2 19.7 %all-to-all-start.4 = ((bf16[64,4,384]{2,1,0:T(4,128)(2,1)}), bf16[64,4,384]{2,1,0:T(4,128)(2,1)S(1)}, u32[]{:S(2)}, u32[]{:S(2)}) async-start(bf16[64,4,384]{2,1,0:T(4,128)(2,1)} %get-tuple-element.64), calls=%async_computation.4 | async-start | bytes 393216 | tf_op jit(solution)/shard_map/all_to_all | solution.py:375

commit v7 on v5

--- a/solution.py
+++ b/solution.py
@@ -214,18 +214,19 @@
 
 
 def contact_kernel(
-    in_ref, early_ref, get_ref, put_ref, normal_ref, known_ref, mortar_hbm, low_token, high_token,
-    out_hbm, pushed_hbm, scratch, back_ref, out_ref, pushed_ref, later_ref, sems, later_sems,
+    in_ref, early_ref, get_ref, put_ref, normal_ref, known_ref, mortar_hbm, low_hbm, high_hbm, token,
+    out_hbm, pushed_hbm, low_out, high_out, scratch, back_ref, out_ref, pushed_ref, later_ref, sems, later_sems,
 ):
     early, _, nodes = early_ref.shape
     segs = early + later_ref.shape[0]
-    later = []
-    for k in range(0, segs - early, GROUP):
-        copy = pltpu.make_async_copy(
-            mortar_hbm.at[0, 0, pl.ds(early + k, GROUP)], later_ref.at[pl.ds(k, GROUP)], later_sems.at[k // GROUP]
-        )
-        copy.start()
-        later.append(copy)
+    later = pltpu.make_async_copy(mortar_hbm.at[0, 0, pl.ds(early, segs - early)], later_ref, later_sems.at[0])
+    later.start()
+    edges = [
+        pltpu.make_async_copy(low_hbm, low_out, later_sems.at[1]),
+        pltpu.make_async_copy(high_hbm, high_out, later_sems.at[2]),
+    ]
+    for edge in edges:
+        edge.start()
     member = lax.rem(iota((3 * GROUP, nodes), 0), GROUP)
     place_in = lax.rem(member, 4)
     block_of = lax.div(member, 4)
@@ -242,12 +243,13 @@
 
     for g in range(segs // GROUP):
         own = slice(GROUP * g, GROUP * (g + 1))
+        if GROUP * g == early:
+            later.wait()
         um = jnp.concatenate(columns(master[own]), axis=0)
         normal = jnp.concatenate(columns(normal_ref[own, :]), axis=0)
         mortar_ref, start = early_ref, GROUP * g
         if start >= early:
             mortar_ref, start = later_ref, start - early
-            later[start // GROUP].wait()
         weights = []
         for s in range(start, start + GROUP, 4):
             left = mortar_ref[s : s + 2].reshape(2 * nodes, nodes)
@@ -278,7 +280,7 @@
             pushed_ref[segs + GROUP * g : segs + GROUP * (g + 1), cols] = rest[rows]
     store = pltpu.make_async_copy(pushed_ref, pushed_hbm, sems.at[0])
     store.start()
-    stores = [store]
+    stores = edges + [store]
 
     def send(piece, part):
         stores.append(pltpu.make_async_copy(out_ref.at[part], out_hbm.at[part], sems.at[1 + piece]))
@@ -289,20 +291,19 @@
         copy.wait()
 
 
-def bulk_kernel(take, out, give, rounded_ref, product_ref):
-    out_ref, base_ref, near_ref, pick_ref = out[:4]
-    last_refs = out[4:5]
-    pick_ref[...] = take(11)[...]
+def bulk_kernel(whole, take, out, give, rounded_ref, product_ref):
+    out_ref = out[0]
     _, layers, blocks, width = out_ref.shape
     rows = layers * blocks
     step = (rows + 2 * blocks) // PARTS
-    low_ref, high_ref, field_ref, layer_ref = take(0), take(1), take(2), take(3)
-    rounded_ref[:blocks] = low_ref[...]
+    field_ref, layer_ref = take(0), take(1)
+    zero = jnp.zeros((blocks, width), BF16)
+    rounded_ref[:blocks] = take(7)[...] if whole else zero
     rounded_ref[blocks : 2 * blocks] = layer_ref[...].astype(BF16)
     for l in range(1, layers):
         rounded_ref[(l + 1) * blocks : (l + 2) * blocks] = field_ref[0, l].astype(BF16)
-    rounded_ref[rows + blocks :] = high_ref[...]
-    weight_refs = [take(i) for i in (4, 5, 6)]
+    rounded_ref[rows + blocks :] = take(8)[...] if whole else zero
+    weight_refs = [take(i) for i in (2, 3, 4)]
 
     @pl.loop(0, PARTS)
     def multiply(p):
@@ -322,22 +323,39 @@
         right = jnp.where(block == blocks - 1, 0.0, pltpu.roll(side, blocks - 1, 0))
         return product(l + 1, 0) + (product(l, 1) + product(l + 2, 1)) + (left + right)
 
-    load_ref, scale_ref = take(7), take(8)
+    load_ref, scale_ref = take(5), take(6)
 
     def stepped(old, l, force):
         return old + scale_ref[0, l].astype(F32) * (load_ref[0, l].astype(F32) - force)
 
-    base_ref[...] = stepped(layer_ref[...], 0, inner(0) + dot(take(10)[...], take(9)[...]))
-    near_ref[...] = scale_ref[0, 0].astype(F32)
+    first = inner(0)
+    if whole:
+        base_ref, near_ref, pick_ref, last_ref = out[1:5]
+        pick_ref[...] = take(11)[...]
+        near_ref[...] = scale_ref[0, 0].astype(F32)
+        first = first + dot(take(10)[...], take(9)[...])
+        base_ref[...] = stepped(layer_ref[...], 0, first)
+    out_ref[0, 0] = stepped(layer_ref[...], 0, first)
 
     @pl.loop(1, layers)
     def update(l):
         out_ref[0, l] = stepped(field_ref[0, l], l, inner(l))
 
-    give(0, (0, pl.ds(1, layers - 1)))
-    for last_ref in last_refs:
+    give(0)
+    if whole:
         last_ref[...] = out_ref[0, layers - 1].astype(BF16)
         give(4)
+
+
+def tail_kernel(take, out, give):
+    first, last, first_scale, last_scale = [take(i)[...].astype(F32) for i in range(4)]
+    base_ref, row_ref, scale0_ref, scale1_ref, pick_ref, weight_ref = out
+    base_ref[...] = first - first_scale * dot(take(5)[...], take(4)[...])
+    row_ref[...] = last
+    scale0_ref[...] = first_scale
+    scale1_ref[...] = last_scale
+    pick_ref[...] = take(6)[...]
+    weight_ref[...] = take(7)[...]
 
 
 def summed(in_ref, pick_ref, base_ref, scale_ref, scratch):
@@ -360,11 +378,20 @@
     place(dot(pick_ref[...], copies(surface)), scratch, out_ref, lambda piece, part: give(0, part, piece))
 
 
-def last_kernel(in_ref, pick_ref, base_ref, scale_ref, field_hbm, out_hbm, scratch, layer_ref, sem):
-    layer_ref[...] = summed(in_ref, pick_ref, base_ref, scale_ref, scratch)
-    store = pltpu.make_async_copy(layer_ref, out_hbm.at[0, 0], sem)
-    store.start()
-    store.wait()
+def last_kernel(
+    in_ref, base_ref, row_ref, scale0_ref, scale1_ref, pick_ref, weight_ref, low_ref, high_ref, field_hbm,
+    out_hbm, scratch, first_ref, last_ref, sems,
+):
+    end = out_hbm.shape[1] - 1
+    last_ref[...] = row_ref[...] - scale1_ref[...] * dot(high_ref[...], weight_ref[...])
+    stores = [pltpu.make_async_copy(last_ref, out_hbm.at[0, end], sems.at[0])]
+    stores[0].start()
+    below = scale0_ref[...] * dot(low_ref[...], weight_ref[...])
+    first_ref[...] = summed(in_ref, pick_ref, base_ref, scale0_ref, scratch) - below
+    stores.append(pltpu.make_async_copy(first_ref, out_hbm.at[0, 0], sems.at[1]))
+    stores[1].start()
+    for store in stores:
+        store.wait()
 
 
 def shift(block, step):
@@ -422,14 +449,14 @@
         first_kernel, [], [shaped((slots, wide), BF16), message], [rows_scratch], direct=(asked, surface)
     )
 
-    def contact(arrived, near_arrays, low, high):
+    def contact(arrived, near_arrays, low, high, token):
         here = [pltpu.with_memory_space_constraint(array, pltpu.VMEM) for array in (arrived, *near_arrays)]
         pushed = shaped((2 * segs, width), BF16)
         return pl.pallas_call(
             contact_kernel,
-            out_shape=[pltpu.HBM(message.shape, BF16), pltpu.HBM(pushed.shape, BF16)],
-            in_specs=[IN_VMEM] * 6 + [ANY] * 3,
-            out_specs=[ANY] * 2,
+            out_shape=[pltpu.HBM(out.shape, BF16) for out in (message, pushed, edge, edge)],
+            in_specs=[IN_VMEM] * 6 + [ANY] * 4,
+            out_specs=[ANY] * 4,
             scratch_shapes=[
                 rows_scratch,
                 VMEM((segs, width), BF16),
@@ -437,52 +464,67 @@
                 VMEM(pushed.shape, BF16),
                 VMEM((segs - early,) + mortar.shape[3:], BF16),
                 pltpu.SemaphoreType.DMA((1 + PIECES,)),
-                pltpu.SemaphoreType.DMA(((segs - early) // GROUP,)),
+                pltpu.SemaphoreType.DMA((3,)),
             ],
             compiler_params=pltpu.CompilerParams(vmem_limit_bytes=16 * 2**20),
-        )(*here, *in_hbm(mortar), low, high)
-
-    def bulk(field, layer0, low, high, pushed, more):
-        outs = [shaped(disp.shape, F32), layer, layer, shaped(pick.shape, BF16)]
-        if more:
-            outs += [edge] + [shaped(array.shape, array.dtype) for array in ready]
-        rows = (layers + 2) * blocks
-        return staged(
-            bulk_kernel,
-            [low, high, field, layer0, k_self, k_layer, k_side, f_ext, inv_diag, pushed, back_sum, pick],
-            outs,
-            [VMEM((rows, width), BF16), VMEM((rows, 3 * width), F32)],
-            loose=(0, 1),
-            kept=(1, 2, 3, 5, 6, 7, 8) if more else (1, 2, 3),
-            fills=[(mortar, early_part, 5), (get, (), 6), (put, (), 7), (normal_rows, (), 8)] if more else [],
-        )
+        )(*here, *in_hbm(mortar), low, high, *in_hbm(token))
+
+    rows = (layers + 2) * blocks
+    bulk_scratch = [VMEM((rows, width), BF16), VMEM((rows, 3 * width), F32)]
+    steady = [k_self, k_layer, k_side, f_ext, inv_diag]
+    near_shape = shaped((slots, wide), BF16)
 
     arrived = exchange(sent)
     low, high = shift(low, 1), shift(high, -1)
-    sent, pushed = contact(arrived, [*ready, gap], low, high)
+    sent, pushed, low, high = contact(arrived, [*ready, gap], low, high, pick)
     returned = exchange(sent)
-    field, base, scale, near, last, *ready = bulk(disp, (disp, (0, 0)), low, high, pushed, True)
+    field, base, scale, near, last, *ready = staged(
+        lambda *refs: bulk_kernel(True, *refs),
+        [disp, (disp, (0, 0)), *steady, low, high, pushed, back_sum, pick],
+        [shaped(disp.shape, F32), layer, layer, near_shape, edge] + [shaped(array.shape, array.dtype) for array in ready],
+        bulk_scratch,
+        kept=(1, 2, 3, 5, 6, 7, 8),
+        fills=[(mortar, early_part, 5), (get, (), 6), (put, (), 7), (normal_rows, (), 8)],
+    )
     sent, layer0, high = staged(
-        next_kernel, [], [message, shaped((1, 1, blocks, width), F32), edge], [rows_scratch], direct=(returned, near, base, scale)
+        next_kernel,
+        [],
+        [message, shaped((1, 1, blocks, width), F32), edge],
+        [rows_scratch],
+        direct=(returned, near, base, scale),
     )
     arrived = exchange(sent)
-    low, high = shift(last, 1), shift(high, -1)
+    (field,) = staged(
+        lambda *refs: bulk_kernel(False, *refs),
+        [field, (layer0, (0, 0)), *steady],
+        [shaped(disp.shape, F32)],
+        bulk_scratch,
+    )
     (gap,) = staged(
         known_kernel, [(layer0, (0, 0)), pick3, normal_rows, (gap0, (0, 0))], [shaped(gap0.shape[2:], F32)], kept=(0,)
     )
-    sent, pushed = contact(arrived, [*ready, gap], low, high)
+    sent, pushed, low, high = contact(arrived, [*ready, gap], *in_hbm(last, high), field)
     returned = exchange(sent)
-    field, base, scale, near = bulk(field, (layer0, (0, 0)), low, high, pushed, False)
+    low, high = shift(low, 1), shift(high, -1)
+    ends = [(array, (0, l)) for array in (field, inv_diag) for l in (0, layers - 1)]
+    held = staged(
+        tail_kernel,
+        ends + [pushed, back_sum, pick, k_layer],
+        [layer, layer, layer, layer, near_shape, shaped(k_layer.shape, BF16)],
+        kept=range(6),
+    )
     return pl.pallas_call(
         last_kernel,
         out_shape=pltpu.HBM(disp.shape, F32),
-        in_specs=[IN_VMEM] * 4 + [HBM],
+        in_specs=[IN_VMEM] * 9 + [HBM],
         out_specs=HBM,
-        scratch_shapes=[rows_scratch, VMEM(base.shape, F32), pltpu.SemaphoreType.DMA],
-        input_output_aliases={4: 0},
+        scratch_shapes=[
+            rows_scratch, VMEM(base.shape, F32), VMEM(base.shape, F32), pltpu.SemaphoreType.DMA((2,))
+        ],
+        input_output_aliases={9: 0},
         compiler_params=pltpu.CompilerParams(vmem_limit_bytes=16 * 2**20),
     )(
-        *[pltpu.with_memory_space_constraint(array, pltpu.VMEM) for array in (returned, near, base, scale)],
+        *[pltpu.with_memory_space_constraint(array, pltpu.VMEM) for array in (returned, *held, low, high)],
         *in_hbm(field),
     )
 

time: 110 us -> 106 us (0.964)
  starting transfers between devices: 46.8 us -> 43.2 us
  Pallas kernels: 28.9 us -> 27.6 us
    all_to_all x5, starting transfers between devices: 37.8 us -> 34.2 us  [exchange(): return lax.all_to_all(parts, 'dom', 0, 0, tiled=True)]
    pallas_call x2, Pallas kernels: 9.08 us -> 7.9 us  [contact(): pl.pallas_call(contact_kernel, out_shape=[pltpu.HBM(out.shape, BF16) for...]
    pallas_call x7 -> x8, Pallas kernels: 19 us -> 18.8 us  [staged(): pl.pallas_call(kernel, out_shape=tuple((space(i, out) for i, out in enume...]
where the time goes in v7:
time: 106 us; the launch traced here: 105 us
  starting transfers between devices  43.2 us (41%)
  waiting for transfers between devices  33.9 us (32%)
  Pallas kernels  27.6 us (26%)
    all_to_all x5, starting transfers between devices, exchange(): return lax.all_to_all(parts, 'dom', 0, 0, tiled=True)  34.2 us
    all_to_all x5, waiting for transfers between devices, exchange(): return lax.all_to_all(parts, 'dom', 0, 0, tiled=True)  27.8 us
    pallas_call x8, Pallas kernels, staged(): pl.pallas_call(kernel, out_shape=tuple((space(i, out) for i, out in enume...  18.8 us
    ppermute x4, starting transfers between devices, shift(): return lax.ppermute(block, 'slab', pairs)  9 us
    pallas_call x2, Pallas kernels, contact(): pl.pallas_call(contact_kernel, out_shape=[pltpu.HBM(out.shape, BF16) for...  7.9 us
    ppermute x4, waiting for transfers between devices, shift(): return lax.ppermute(block, 'slab', pairs)  6.13 us
  transfers between devices with their start and end apart: 9, of which 7 were waited for; matrix products, arithmetic and copies ran while one was open for 0% of the time, Pallas kernels for 14%

profile of v7, /device:TPU:1, one launch (start us, length us, event | category | flops | bytes accessed | tf_op | source)
XLA Modules:
  0.0 104.9 jit_solution(13031175405835988112)
XLA Ops:
  0.0 1.7 %shard_map.118.refs_7_ = f32[64,128]{1,0:T(8,128)} custom-call(s32[1,1,128]{2,1,0:T(1,128)} %refs_0_.4, s32[1,1,128]{2,1,0:T(1,128)} %refs_1_.3), custom_call_target="tpu_custom_call" | custom-call | tf_op jit(solution)/shard_map/pallas_call | solution.py:87
  1.7 13.0 %all-to-all-start = ((f32[64,1,128]{2,1,0:T(1,128)}), f32[64,1,128]{2,1,0:T(1,128)S(1)}, u32[]{:S(2)}, u32[]{:S(2)}) async-start(f32[64,1,128]{2,1,0:T(1,128)} %bitcast.1), calls=%async_computation | async-start | bytes 65536 | tf_op jit(solution)/shard_map/all_to_all | solution.py:404
  14.7 2.1 %shard_map.119 = (bf16[256,128]{1,0:T(8,128)(2,1)}, bf16[128,256]{1,0:T(8,128)(2,1)}, bf16[128,96]{1,0:T(8,128)(2,1)}, bf16[32,256]{1,0:T(8,128)(2,1)}, f32[128,...) custom-call(s32[1,1,128]{2,1,0:T(1,128)} %refs_0_.4, ...), custom_call_target="tpu_custom_call" | custom-call | tf_op jit(solution)/shard_map/pallas_call | solution.py:87
  16.8 7.3 %all-to-all-done = f32[64,1,128]{2,1,0:T(1,128)S(1)} async-done(((f32[64,1,128]{2,1,0:T(1,128)}), f32[64,1,128]{2,1,0:T(1,128)S(1)}, u32[]{:S(2)}, u32[]{:S(2)}) %all-to-all-start) | async-done | bytes 32800 | tf_op jit(solution)/shard_map/all_to_all | solution.py:404
  24.1 1.0 shard_map.120
  25.1 4.7 %all-to-all-start.1 = ((bf16[64,4,384]{2,1,0:T(4,128)(2,1)}), bf16[64,4,384]{2,1,0:T(4,128)(2,1)S(1)}, u32[]{:S(2)}, u32[]{:S(2)}) async-start(bf16[64,4,384]{2,1,0:T(4,128)(2,1)} %get-tuple-element.47), calls=%async_computation.1 | async-start | bytes 393216 | tf_op jit(solution)/shard_map/all_to_all | solution.py:404
  29.8 3.2 %collective-permute-start = (bf16[32,384]{1,0:T(8,128)(2,1)}, bf16[32,384]{1,0:T(8,128)(2,1)S(1)}, u32[]{:S(2)}, u32[]{:S(2)}) collective-permute-start(bf16[32,384]{1,0:T(8,128)(2,1)} %get-tuple-element.53), channel_id=1, source_target_pairs={{0,64},{64,128},{128,192},{1,65},{65,129},{129,193},{2,66},{66,130... | collective-permute-start | bytes 73736 | tf_op jit(solution)/shard_map/ppermute | solution.py:400
  33.0 1.3 %collective-permute-start.1 = (bf16[32,384]{1,0:T(8,128)(2,1)}, bf16[32,384]{1,0:T(8,128)(2,1)S(1)}, u32[]{:S(2)}, u32[]{:S(2)}) collective-permute-start(bf16[32,384]{1,0:T(8,128)(2,1)} %get-tuple-element.54), channel_id=1, source_target_pairs={{64,0},{128,64},{192,128},{65,1},{129,65},{193,129},{66,2},{130,66... | collective-permute-start | bytes 73736 | tf_op jit(solution)/shard_map/ppermute | solution.py:400
  34.3 0.0 collective-permute-done.low_hbm
  34.3 3.8 %collective-permute-done.1.high_hbm = bf16[32,384]{1,0:T(8,128)(2,1)S(1)} collective-permute-done((bf16[32,384]{1,0:T(8,128)(2,1)}, bf16[32,384]{1,0:T(8,128)(2,1)S(1)}, u32[]{:S(2)}, u32[]{:S(2)}) %collective-permute-start.1) | collective-permute-done | bytes 24608 | tf_op jit(solution)/shard_map/ppermute | solution.py:400
  38.1 3.9 %all-to-all-done.1.in_ref = bf16[64,4,384]{2,1,0:T(4,128)(2,1)S(1)} async-done(((bf16[64,4,384]{2,1,0:T(4,128)(2,1)}), bf16[64,4,384]{2,1,0:T(4,128)(2,1)S(1)}, u32[]{:S(2)}, u32[]{:S(2)}) %all-to-all-start.1) | async-done | bytes 196640 | tf_op jit(solution)/shard_map/all_to_all | solution.py:404
  42.0 4.0 %shard_map.121 = (bf16[64,4,384]{2,1,0:T(4,128)(2,1)}, bf16[256,384]{1,0:T(8,128)(2,1)}, bf16[32,384]{1,0:T(8,128)(2,1)}, bf16[32,384]{1,0:T(8,128)(2,1)}) custom-call(bf16[64,4,384]{2,1,0:T(4,128)(2,1)S(1)} %all-to-all-done.1.in_ref, bf16[64,128,128]{2,1,0:T(8,128)(2,1)S(1)} %get-tuple-element.48.early_ref, bf16[128,256]{1,0:T(8,128)(2,1)S(1)} %get-tuple-element.49.get_ref, ...), custom_call_target="tpu_custom_call" | custom-call | tf_op jit(solution)/shard_map/pallas_call | solution.py:455
  45.9 7.7 %all-to-all-start.2 = ((bf16[64,4,384]{2,1,0:T(4,128)(2,1)}), bf16[64,4,384]{2,1,0:T(4,128)(2,1)S(1)}, u32[]{:S(2)}, u32[]{:S(2)}) async-start(bf16[64,4,384]{2,1,0:T(4,128)(2,1)} %get-tuple-element.56), calls=%async_computation.2 | async-start | bytes 393216 | tf_op jit(solution)/shard_map/all_to_all | solution.py:404
  53.6 5.6 %shard_map.122 = (f32[1,24,32,384]{3,2,1,0:T(8,128)}, f32[32,384]{1,0:T(8,128)S(1)}, f32[32,384]{1,0:T(8,128)S(1)}, bf16[256,128]{1,0:T(8,128)(2,1)S(1)}, bf16[3...) custom-call(f32[1,24,32,384]{3,2,1,0:T(8,128)} %refs_1_.5, ...), custom_call_target="tpu_custom_call" | custom-call | tf_op jit(solution)/shard_map/pallas_call | solution.py:87
  59.2 6.5 %all-to-all-done.2.refs_0_ = bf16[64,4,384]{2,1,0:T(4,128)(2,1)S(1)} async-done(((bf16[64,4,384]{2,1,0:T(4,128)(2,1)}), bf16[64,4,384]{2,1,0:T(4,128)(2,1)S(1)}, u32[]{:S(2)}, u32[]{:S(2)}) %all-to-all-start.2) | async-done | bytes 196640 | tf_op jit(solution)/shard_map/all_to_all | solution.py:404
  65.6 1.1 %shard_map.123 = (bf16[64,4,384]{2,1,0:T(4,128)(2,1)}, f32[1,1,32,384]{3,2,1,0:T(8,128)}, bf16[32,384]{1,0:T(8,128)(2,1)}) custom-call(bf16[64,4,384]{2,1,0:T(4,128)(2,1)S(1)} %all-to-all-done.2.refs_0_, bf16[256,128]{1,0:T(8,128)(2,1)S(1)} %get-tuple-element.64.refs_1_, f32[32,384]{1,0:T(8,128)S(1)} %get-tuple-element.65.refs_2_, ...), custom_call_target="tpu_custom_call" | custom-call | tf_op jit(solution)/shard_map/pallas_call | solution.py:87
  66.8 4.5 %all-to-all-start.3 = ((bf16[64,4,384]{2,1,0:T(4,128)(2,1)}), bf16[64,4,384]{2,1,0:T(4,128)(2,1)S(1)}, u32[]{:S(2)}, u32[]{:S(2)}) async-start(bf16[64,4,384]{2,1,0:T(4,128)(2,1)} %get-tuple-element.67), calls=%async_computation.3 | async-start | bytes 393216 | tf_op jit(solution)/shard_map/all_to_all | solution.py:404
  71.2 1.1 %shard_map.124.known_ref = f32[128,128]{1,0:T(8,128)S(1)} custom-call(f32[1,1,32,384]{3,2,1,0:T(8,128)} %get-tuple-element.72.refs_0_.refs_1_, bf16[128,96]{1,0:T(8,128)(2,1)} %get-tuple-element.73.refs_1_, f32[128,384]{1,0:T(8,128)} %get-tuple-element.63.refs_15_.refs_2_, f32[1,1,128,128]{3,2,1,0:T(8,128)} %refs_3_.7), custom_call_target="tpu_custom_call" | custom-call | tf_op jit(solution)/shard_map/pallas_call | solution.py:87
  72.4 4.8 %shard_map.125.token.refs_0_.refs_1_.field_hbm = f32[1,24,32,384]{3,2,1,0:T(8,128)} custom-call(f32[1,24,32,384]{3,2,1,0:T(8,128)} %get-tuple-element.76.refs_0_, f32[1,1,32,384]{3,2,1,0:T(8,128)} %get-tuple-element.72.refs_0_.refs_1_, bf16[384,384]{1,0:T(8,128)(2,1)} %refs_2_.6, bf16[384,384]{1,0:T(8,128)(2,1)} %refs_7_.1, bf16[384,384]{1,0:T(8,128)(2,1)} %refs_4_.5, ...), custom_call_target="tpu_custom_call" | custom-call | tf_op jit(solution)/shard_map/pallas_call | solution.py:87
  77.2 6.3 %all-to-all-done.3.in_ref = bf16[64,4,384]{2,1,0:T(4,128)(2,1)S(1)} async-done(((bf16[64,4,384]{2,1,0:T(4,128)(2,1)}), bf16[64,4,384]{2,1,0:T(4,128)(2,1)S(1)}, u32[]{:S(2)}, u32[]{:S(2)}) %all-to-all-start.3) | async-done | bytes 196640 | tf_op jit(solution)/shard_map/all_to_all | solution.py:404
  83.5 3.9 %shard_map.126 = (bf16[64,4,384]{2,1,0:T(4,128)(2,1)}, bf16[256,384]{1,0:T(8,128)(2,1)}, bf16[32,384]{1,0:T(8,128)(2,1)}, bf16[32,384]{1,0:T(8,128)(2,1)}) custom-call(bf16[64,4,384]{2,1,0:T(4,128)(2,1)S(1)} %all-to-all-done.3.in_ref, bf16[64,128,128]{2,1,0:T(8,128)(2,1)S(1)} %get-tuple-element.68.early_ref, bf16[128,256]{1,0:T(8,128)(2,1)S(1)} %get-tuple-element.69.get_ref, ...), custom_call_target="tpu_custom_call" | custom-call | tf_op jit(solution)/shard_map/pallas_call | solution.py:455
  87.4 4.4 %all-to-all-start.4 = ((bf16[64,4,384]{2,1,0:T(4,128)(2,1)}), bf16[64,4,384]{2,1,0:T(4,128)(2,1)S(1)}, u32[]{:S(2)}, u32[]{:S(2)}) async-start(bf16[64,4,384]{2,1,0:T(4,128)(2,1)} %get-tuple-element.77), calls=%async_computation.4 | async-start | bytes 393216 | tf_op jit(solution)/shard_map/all_to_all | solution.py:404
  91.8 3.2 %collective-permute-start.2 = (bf16[32,384]{1,0:T(8,128)(2,1)}, bf16[32,384]{1,0:T(8,128)(2,1)S(1)}, u32[]{:S(2)}, u32[]{:S(2)}) collective-permute-start(bf16[32,384]{1,0:T(8,128)(2,1)} %get-tuple-element.85), channel_id=1, source_target_pairs={{0,64},{64,128},{128,192},{1,65},{65,129},{129,193},{2,66},{66,130... | collective-permute-start | bytes 73736 | tf_op jit(solution)/shard_map/ppermute | solution.py:400
  95.0 1.3 %collective-permute-start.3 = (bf16[32,384]{1,0:T(8,128)(2,1)}, bf16[32,384]{1,0:T(8,128)(2,1)S(1)}, u32[]{:S(2)}, u32[]{:S(2)}) collective-permute-start(bf16[32,384]{1,0:T(8,128)(2,1)} %get-tuple-element.86), channel_id=1, source_target_pairs={{64,0},{128,64},{192,128},{65,1},{129,65},{193,129},{66,2},{130,66... | collective-permute-start | bytes 73736 | tf_op jit(solution)/shard_map/ppermute | solution.py:400
  96.3 1.4 %shard_map.127 = (f32[32,384]{1,0:T(8,128)S(1)}, f32[32,384]{1,0:T(8,128)S(1)}, f32[32,384]{1,0:T(8,128)S(1)}, f32[32,384]{1,0:T(8,128)S(1)}, bf16[256,128]{1,0:...) custom-call(f32[1,24,32,384]{3,2,1,0:T(8,128)} %shard_map.125.token.refs_0_.refs_1_.field_hbm, ...), custom_call_target="tpu_custom_call" | custom-call | tf_op jit(solution)/shard_map/pallas_call | solution.py:87
  97.7 0.0 collective-permute-done.2.low_ref
  97.7 2.4 %collective-permute-done.3.high_ref = bf16[32,384]{1,0:T(8,128)(2,1)S(1)} collective-permute-done((bf16[32,384]{1,0:T(8,128)(2,1)}, bf16[32,384]{1,0:T(8,128)(2,1)S(1)}, u32[]{:S(2)}, u32[]{:S(2)}) %collective-permute-start.3) | collective-permute-done | bytes 24608 | tf_op jit(solution)/shard_map/ppermute | solution.py:400
  100.1 3.9 %all-to-all-done.4.in_ref = bf16[64,4,384]{2,1,0:T(4,128)(2,1)S(1)} async-done(((bf16[64,4,384]{2,1,0:T(4,128)(2,1)}), bf16[64,4,384]{2,1,0:T(4,128)(2,1)S(1)}, u32[]{:S(2)}, u32[]{:S(2)}) %all-to-all-start.4) | async-done | bytes 196640 | tf_op jit(solution)/shard_map/all_to_all | solution.py:404
  104.0 0.9 shard_map.128
Async XLA Ops:
  1.7 22.4 %all-to-all-start = ((f32[64,1,128]{2,1,0:T(1,128)}), f32[64,1,128]{2,1,0:T(1,128)S(1)}, u32[]{:S(2)}, u32[]{:S(2)}) async-start(f32[64,1,128]{2,1,0:T(1,128)} %bitcast.1), calls=%async_computation | async-start | bytes 65536 | tf_op jit(solution)/shard_map/all_to_all | solution.py:404
  25.1 16.9 %all-to-all-start.1 = ((bf16[64,4,384]{2,1,0:T(4,128)(2,1)}), bf16[64,4,384]{2,1,0:T(4,128)(2,1)S(1)}, u32[]{:S(2)}, u32[]{:S(2)}) async-start(bf16[64,4,384]{2,1,0:T(4,128)(2,1)} %get-tuple-element.47), calls=%async_computation.1 | async-start | bytes 393216 | tf_op jit(solution)/shard_map/all_to_all | solution.py:404
  29.8 4.5 %collective-permute-start = (bf16[32,384]{1,0:T(8,128)(2,1)}, bf16[32,384]{1,0:T(8,128)(2,1)S(1)}, u32[]{:S(2)}, u32[]{:S(2)}) collective-permute-start(bf16[32,384]{1,0:T(8,128)(2,1)} %get-tuple-element.53), channel_id=1, source_target_pairs={{0,64},{64,128},{128,192},{1,65},{65,129},{129,193},{2,66},{66,130... | collective-permute-start | bytes 73736 | tf_op jit(solution)/shard_map/ppermute | solution.py:400
  33.0 5.1 %collective-permute-start.1 = (bf16[32,384]{1,0:T(8,128)(2,1)}, bf16[32,384]{1,0:T(8,128)(2,1)S(1)}, u32[]{:S(2)}, u32[]{:S(2)}) collective-permute-start(bf16[32,384]{1,0:T(8,128)(2,1)} %get-tuple-element.54), channel_id=1, source_target_pairs={{64,0},{128,64},{192,128},{65,1},{129,65},{193,129},{66,2},{130,66... | collective-permute-start | bytes 73736 | tf_op jit(solution)/shard_map/ppermute | solution.py:400
  45.9 19.7 %all-to-all-start.2 = ((bf16[64,4,384]{2,1,0:T(4,128)(2,1)}), bf16[64,4,384]{2,1,0:T(4,128)(2,1)S(1)}, u32[]{:S(2)}, u32[]{:S(2)}) async-start(bf16[64,4,384]{2,1,0:T(4,128)(2,1)} %get-tuple-element.56), calls=%async_computation.2 | async-start | bytes 393216 | tf_op jit(solution)/shard_map/all_to_all | solution.py:404
  66.8 16.7 %all-to-all-start.3 = ((bf16[64,4,384]{2,1,0:T(4,128)(2,1)}), bf16[64,4,384]{2,1,0:T(4,128)(2,1)S(1)}, u32[]{:S(2)}, u32[]{:S(2)}) async-start(bf16[64,4,384]{2,1,0:T(4,128)(2,1)} %get-tuple-element.67), calls=%async_computation.3 | async-start | bytes 393216 | tf_op jit(solution)/shard_map/all_to_all | solution.py:404
  87.4 16.6 %all-to-all-start.4 = ((bf16[64,4,384]{2,1,0:T(4,128)(2,1)}), bf16[64,4,384]{2,1,0:T(4,128)(2,1)S(1)}, u32[]{:S(2)}, u32[]{:S(2)}) async-start(bf16[64,4,384]{2,1,0:T(4,128)(2,1)} %get-tuple-element.77), calls=%async_computation.4 | async-start | bytes 393216 | tf_op jit(solution)/shard_map/all_to_all | solution.py:404
  91.8 5.9 %collective-permute-start.2 = (bf16[32,384]{1,0:T(8,128)(2,1)}, bf16[32,384]{1,0:T(8,128)(2,1)S(1)}, u32[]{:S(2)}, u32[]{:S(2)}) collective-permute-start(bf16[32,384]{1,0:T(8,128)(2,1)} %get-tuple-element.85), channel_id=1, source_target_pairs={{0,64},{64,128},{128,192},{1,65},{65,129},{129,193},{2,66},{66,130... | collective-permute-start | bytes 73736 | tf_op jit(solution)/shard_map/ppermute | solution.py:400
  95.0 5.1 %collective-permute-start.3 = (bf16[32,384]{1,0:T(8,128)(2,1)}, bf16[32,384]{1,0:T(8,128)(2,1)S(1)}, u32[]{:S(2)}, u32[]{:S(2)}) collective-permute-start(bf16[32,384]{1,0:T(8,128)(2,1)} %get-tuple-element.86), channel_id=1, source_target_pairs={{64,0},{128,64},{192,128},{65,1},{129,65},{193,129},{66,2},{130,66... | collective-permute-start | bytes 73736 | tf_op jit(solution)/shard_map/ppermute | solution.py:400

commit v8 on v7

--- a/solution.py
+++ b/solution.py
@@ -182,9 +182,9 @@
     pairs = out_ref.shape[0] // 2
     part = pairs // PIECES
     for j in range(pairs):
-        both = scratch[2 * CAPACITY * j : 2 * CAPACITY * (j + 1), :].astype(BF16)
-        out_ref[2 * j] = both[:CAPACITY]
-        out_ref[2 * j + 1] = both[CAPACITY:]
+        both = scratch[2 * CAPACITY * j : 2 * CAPACITY * (j + 1), :]
+        out_ref[2 * j] = both[:CAPACITY].astype(BF16)
+        out_ref[2 * j + 1] = both[CAPACITY:].astype(BF16)
         if (j + 1) % part == 0:
             send(j // part, pl.ds(2 * (j + 1 - part), 2 * part))
 
@@ -417,7 +417,7 @@
     edge = shaped((blocks, width), BF16)
     layer = shaped((blocks, width), F32)
 
-    early = max(segs // 2, GROUP)
+    early = max(segs * 5 // 8 // GROUP, 1) * GROUP
     early_part = (0, 0, pl.ds(0, early))
     (asked,) = staged(
         lambda *refs: request_kernel(blocks, *refs), [seg_src, seg_master], [shaped((count, wide), F32)], free_outs=True

time: 106 us -> 105 us (level)
  no operation moved by 1% of the time
where the time goes in v8:
time: 105 us
  starting transfers between devices  43.2 us (41%)
  waiting for transfers between devices  33.9 us (32%)
  Pallas kernels  27.6 us (26%)
    all_to_all x5, starting transfers between devices, exchange(): return lax.all_to_all(parts, 'dom', 0, 0, tiled=True)  34.2 us
    all_to_all x5, waiting for transfers between devices, exchange(): return lax.all_to_all(parts, 'dom', 0, 0, tiled=True)  27.7 us
    pallas_call x8, Pallas kernels, staged(): pl.pallas_call(kernel, out_shape=tuple((space(i, out) for i, out in enume...  18.8 us
    ppermute x4, starting transfers between devices, shift(): return lax.ppermute(block, 'slab', pairs)  8.99 us
    pallas_call x2, Pallas kernels, contact(): pl.pallas_call(contact_kernel, out_shape=[pltpu.HBM(out.shape, BF16) for...  7.84 us
    ppermute x4, waiting for transfers between devices, shift(): return lax.ppermute(block, 'slab', pairs)  6.13 us
  transfers between devices with their start and end apart: 9, of which 7 were waited for; matrix products, arithmetic and copies ran while one was open for 0% of the time, Pallas kernels for 14%

profile of v8, /device:TPU:1, one launch (start us, length us, event | category | flops | bytes accessed | tf_op | source)
XLA Modules:
  0.0 104.8 jit_solution(11978725227518013640)
XLA Ops:
  0.0 1.7 %shard_map.118.refs_7_ = f32[64,128]{1,0:T(8,128)} custom-call(s32[1,1,128]{2,1,0:T(1,128)} %refs_0_.4, s32[1,1,128]{2,1,0:T(1,128)} %refs_1_.3), custom_call_target="tpu_custom_call" | custom-call | tf_op jit(solution)/shard_map/pallas_call | solution.py:87
  1.7 13.0 %all-to-all-start = ((f32[64,1,128]{2,1,0:T(1,128)}), f32[64,1,128]{2,1,0:T(1,128)S(1)}, u32[]{:S(2)}, u32[]{:S(2)}) async-start(f32[64,1,128]{2,1,0:T(1,128)} %bitcast.1), calls=%async_computation | async-start | bytes 65536 | tf_op jit(solution)/shard_map/all_to_all | solution.py:404
  14.7 2.2 %shard_map.119 = (bf16[256,128]{1,0:T(8,128)(2,1)}, bf16[128,256]{1,0:T(8,128)(2,1)}, bf16[128,96]{1,0:T(8,128)(2,1)}, bf16[32,256]{1,0:T(8,128)(2,1)}, f32[128,...) custom-call(s32[1,1,128]{2,1,0:T(1,128)} %refs_0_.4, ...), custom_call_target="tpu_custom_call" | custom-call | tf_op jit(solution)/shard_map/pallas_call | solution.py:87
  16.8 7.2 %all-to-all-done = f32[64,1,128]{2,1,0:T(1,128)S(1)} async-done(((f32[64,1,128]{2,1,0:T(1,128)}), f32[64,1,128]{2,1,0:T(1,128)S(1)}, u32[]{:S(2)}, u32[]{:S(2)}) %all-to-all-start) | async-done | bytes 32800 | tf_op jit(solution)/shard_map/all_to_all | solution.py:404
  24.1 1.0 shard_map.120
  25.1 4.7 %all-to-all-start.1 = ((bf16[64,4,384]{2,1,0:T(4,128)(2,1)}), bf16[64,4,384]{2,1,0:T(4,128)(2,1)S(1)}, u32[]{:S(2)}, u32[]{:S(2)}) async-start(bf16[64,4,384]{2,1,0:T(4,128)(2,1)} %get-tuple-element.47), calls=%async_computation.1 | async-start | bytes 393216 | tf_op jit(solution)/shard_map/all_to_all | solution.py:404
  29.8 3.2 %collective-permute-start = (bf16[32,384]{1,0:T(8,128)(2,1)}, bf16[32,384]{1,0:T(8,128)(2,1)S(1)}, u32[]{:S(2)}, u32[]{:S(2)}) collective-permute-start(bf16[32,384]{1,0:T(8,128)(2,1)} %get-tuple-element.53), channel_id=1, source_target_pairs={{0,64},{64,128},{128,192},{1,65},{65,129},{129,193},{2,66},{66,130... | collective-permute-start | bytes 73736 | tf_op jit(solution)/shard_map/ppermute | solution.py:400
  33.0 1.3 %collective-permute-start.1 = (bf16[32,384]{1,0:T(8,128)(2,1)}, bf16[32,384]{1,0:T(8,128)(2,1)S(1)}, u32[]{:S(2)}, u32[]{:S(2)}) collective-permute-start(bf16[32,384]{1,0:T(8,128)(2,1)} %get-tuple-element.54), channel_id=1, source_target_pairs={{64,0},{128,64},{192,128},{65,1},{129,65},{193,129},{66,2},{130,66... | collective-permute-start | bytes 73736 | tf_op jit(solution)/shard_map/ppermute | solution.py:400
  34.3 0.0 collective-permute-done.low_hbm
  34.3 3.8 %collective-permute-done.1.high_hbm = bf16[32,384]{1,0:T(8,128)(2,1)S(1)} collective-permute-done((bf16[32,384]{1,0:T(8,128)(2,1)}, bf16[32,384]{1,0:T(8,128)(2,1)S(1)}, u32[]{:S(2)}, u32[]{:S(2)}) %collective-permute-start.1) | collective-permute-done | bytes 24608 | tf_op jit(solution)/shard_map/ppermute | solution.py:400
  38.1 3.9 %all-to-all-done.1.in_ref = bf16[64,4,384]{2,1,0:T(4,128)(2,1)S(1)} async-done(((bf16[64,4,384]{2,1,0:T(4,128)(2,1)}), bf16[64,4,384]{2,1,0:T(4,128)(2,1)S(1)}, u32[]{:S(2)}, u32[]{:S(2)}) %all-to-all-start.1) | async-done | bytes 196640 | tf_op jit(solution)/shard_map/all_to_all | solution.py:404
  42.0 3.9 %shard_map.121 = (bf16[64,4,384]{2,1,0:T(4,128)(2,1)}, bf16[256,384]{1,0:T(8,128)(2,1)}, bf16[32,384]{1,0:T(8,128)(2,1)}, bf16[32,384]{1,0:T(8,128)(2,1)}) custom-call(bf16[64,4,384]{2,1,0:T(4,128)(2,1)S(1)} %all-to-all-done.1.in_ref, bf16[80,128,128]{2,1,0:T(8,128)(2,1)S(1)} %get-tuple-element.48.early_ref, bf16[128,256]{1,0:T(8,128)(2,1)S(1)} %get-tuple-element.49.get_ref, ...), custom_call_target="tpu_custom_call" | custom-call | tf_op jit(solution)/shard_map/pallas_call | solution.py:455
  45.9 7.7 %all-to-all-start.2 = ((bf16[64,4,384]{2,1,0:T(4,128)(2,1)}), bf16[64,4,384]{2,1,0:T(4,128)(2,1)S(1)}, u32[]{:S(2)}, u32[]{:S(2)}) async-start(bf16[64,4,384]{2,1,0:T(4,128)(2,1)} %get-tuple-element.56), calls=%async_computation.2 | async-start | bytes 393216 | tf_op jit(solution)/shard_map/all_to_all | solution.py:404
  53.6 5.6 %shard_map.122 = (f32[1,24,32,384]{3,2,1,0:T(8,128)}, f32[32,384]{1,0:T(8,128)S(1)}, f32[32,384]{1,0:T(8,128)S(1)}, bf16[256,128]{1,0:T(8,128)(2,1)S(1)}, bf16[3...) custom-call(f32[1,24,32,384]{3,2,1,0:T(8,128)} %refs_1_.5, ...), custom_call_target="tpu_custom_call" | custom-call | tf_op jit(solution)/shard_map/pallas_call | solution.py:87
  59.1 6.5 %all-to-all-done.2.refs_0_ = bf16[64,4,384]{2,1,0:T(4,128)(2,1)S(1)} async-done(((bf16[64,4,384]{2,1,0:T(4,128)(2,1)}), bf16[64,4,384]{2,1,0:T(4,128)(2,1)S(1)}, u32[]{:S(2)}, u32[]{:S(2)}) %all-to-all-start.2) | async-done | bytes 196640 | tf_op jit(solution)/shard_map/all_to_all | solution.py:404
  65.6 1.1 %shard_map.123 = (bf16[64,4,384]{2,1,0:T(4,128)(2,1)}, f32[1,1,32,384]{3,2,1,0:T(8,128)}, bf16[32,384]{1,0:T(8,128)(2,1)}) custom-call(bf16[64,4,384]{2,1,0:T(4,128)(2,1)S(1)} %all-to-all-done.2.refs_0_, bf16[256,128]{1,0:T(8,128)(2,1)S(1)} %get-tuple-element.64.refs_1_, f32[32,384]{1,0:T(8,128)S(1)} %get-tuple-element.65.refs_2_, ...), custom_call_target="tpu_custom_call" | custom-call | tf_op jit(solution)/shard_map/pallas_call | solution.py:87
  66.7 4.5 %all-to-all-start.3 = ((bf16[64,4,384]{2,1,0:T(4,128)(2,1)}), bf16[64,4,384]{2,1,0:T(4,128)(2,1)S(1)}, u32[]{:S(2)}, u32[]{:S(2)}) async-start(bf16[64,4,384]{2,1,0:T(4,128)(2,1)} %get-tuple-element.67), calls=%async_computation.3 | async-start | bytes 393216 | tf_op jit(solution)/shard_map/all_to_all | solution.py:404
  71.2 1.1 %shard_map.124.known_ref = f32[128,128]{1,0:T(8,128)S(1)} custom-call(f32[1,1,32,384]{3,2,1,0:T(8,128)} %get-tuple-element.72.refs_0_.refs_1_, bf16[128,96]{1,0:T(8,128)(2,1)} %get-tuple-element.73.refs_1_, f32[128,384]{1,0:T(8,128)} %get-tuple-element.63.refs_15_.refs_2_, f32[1,1,128,128]{3,2,1,0:T(8,128)} %refs_3_.7), custom_call_target="tpu_custom_call" | custom-call | tf_op jit(solution)/shard_map/pallas_call | solution.py:87
  72.3 4.8 %shard_map.125.token.refs_0_.refs_1_.field_hbm = f32[1,24,32,384]{3,2,1,0:T(8,128)} custom-call(f32[1,24,32,384]{3,2,1,0:T(8,128)} %get-tuple-element.76.refs_0_, f32[1,1,32,384]{3,2,1,0:T(8,128)} %get-tuple-element.72.refs_0_.refs_1_, bf16[384,384]{1,0:T(8,128)(2,1)} %refs_2_.6, bf16[384,384]{1,0:T(8,128)(2,1)} %refs_7_.1, bf16[384,384]{1,0:T(8,128)(2,1)} %refs_4_.5, ...), custom_call_target="tpu_custom_call" | custom-call | tf_op jit(solution)/shard_map/pallas_call | solution.py:87
  77.2 6.3 %all-to-all-done.3.in_ref = bf16[64,4,384]{2,1,0:T(4,128)(2,1)S(1)} async-done(((bf16[64,4,384]{2,1,0:T(4,128)(2,1)}), bf16[64,4,384]{2,1,0:T(4,128)(2,1)S(1)}, u32[]{:S(2)}, u32[]{:S(2)}) %all-to-all-start.3) | async-done | bytes 196640 | tf_op jit(solution)/shard_map/all_to_all | solution.py:404
  83.4 3.9 %shard_map.126 = (bf16[64,4,384]{2,1,0:T(4,128)(2,1)}, bf16[256,384]{1,0:T(8,128)(2,1)}, bf16[32,384]{1,0:T(8,128)(2,1)}, bf16[32,384]{1,0:T(8,128)(2,1)}) custom-call(bf16[64,4,384]{2,1,0:T(4,128)(2,1)S(1)} %all-to-all-done.3.in_ref, bf16[80,128,128]{2,1,0:T(8,128)(2,1)S(1)} %get-tuple-element.68.early_ref, bf16[128,256]{1,0:T(8,128)(2,1)S(1)} %get-tuple-element.69.get_ref, ...), custom_call_target="tpu_custom_call" | custom-call | tf_op jit(solution)/shard_map/pallas_call | solution.py:455
  87.3 4.4 %all-to-all-start.4 = ((bf16[64,4,384]{2,1,0:T(4,128)(2,1)}), bf16[64,4,384]{2,1,0:T(4,128)(2,1)S(1)}, u32[]{:S(2)}, u32[]{:S(2)}) async-start(bf16[64,4,384]{2,1,0:T(4,128)(2,1)} %get-tuple-element.77), calls=%async_computation.4 | async-start | bytes 393216 | tf_op jit(solution)/shard_map/all_to_all | solution.py:404
  91.7 3.2 %collective-permute-start.2 = (bf16[32,384]{1,0:T(8,128)(2,1)}, bf16[32,384]{1,0:T(8,128)(2,1)S(1)}, u32[]{:S(2)}, u32[]{:S(2)}) collective-permute-start(bf16[32,384]{1,0:T(8,128)(2,1)} %get-tuple-element.85), channel_id=1, source_target_pairs={{0,64},{64,128},{128,192},{1,65},{65,129},{129,193},{2,66},{66,130... | collective-permute-start | bytes 73736 | tf_op jit(solution)/shard_map/ppermute | solution.py:400
  94.9 1.3 %collective-permute-start.3 = (bf16[32,384]{1,0:T(8,128)(2,1)}, bf16[32,384]{1,0:T(8,128)(2,1)S(1)}, u32[]{:S(2)}, u32[]{:S(2)}) collective-permute-start(bf16[32,384]{1,0:T(8,128)(2,1)} %get-tuple-element.86), channel_id=1, source_target_pairs={{64,0},{128,64},{192,128},{65,1},{129,65},{193,129},{66,2},{130,66... | collective-permute-start | bytes 73736 | tf_op jit(solution)/shard_map/ppermute | solution.py:400
  96.2 1.4 %shard_map.127 = (f32[32,384]{1,0:T(8,128)S(1)}, f32[32,384]{1,0:T(8,128)S(1)}, f32[32,384]{1,0:T(8,128)S(1)}, f32[32,384]{1,0:T(8,128)S(1)}, bf16[256,128]{1,0:...) custom-call(f32[1,24,32,384]{3,2,1,0:T(8,128)} %shard_map.125.token.refs_0_.refs_1_.field_hbm, ...), custom_call_target="tpu_custom_call" | custom-call | tf_op jit(solution)/shard_map/pallas_call | solution.py:87
  97.6 0.0 collective-permute-done.2.low_ref
  97.7 2.4 %collective-permute-done.3.high_ref = bf16[32,384]{1,0:T(8,128)(2,1)S(1)} collective-permute-done((bf16[32,384]{1,0:T(8,128)(2,1)}, bf16[32,384]{1,0:T(8,128)(2,1)S(1)}, u32[]{:S(2)}, u32[]{:S(2)}) %collective-permute-start.3) | collective-permute-done | bytes 24608 | tf_op jit(solution)/shard_map/ppermute | solution.py:400
  100.0 3.9 %all-to-all-done.4.in_ref = bf16[64,4,384]{2,1,0:T(4,128)(2,1)S(1)} async-done(((bf16[64,4,384]{2,1,0:T(4,128)(2,1)}), bf16[64,4,384]{2,1,0:T(4,128)(2,1)S(1)}, u32[]{:S(2)}, u32[]{:S(2)}) %all-to-all-start.4) | async-done | bytes 196640 | tf_op jit(solution)/shard_map/all_to_all | solution.py:404
  103.9 0.9 shard_map.128
Async XLA Ops:
  1.7 22.4 %all-to-all-start = ((f32[64,1,128]{2,1,0:T(1,128)}), f32[64,1,128]{2,1,0:T(1,128)S(1)}, u32[]{:S(2)}, u32[]{:S(2)}) async-start(f32[64,1,128]{2,1,0:T(1,128)} %bitcast.1), calls=%async_computation | async-start | bytes 65536 | tf_op jit(solution)/shard_map/all_to_all | solution.py:404
  25.1 16.9 %all-to-all-start.1 = ((bf16[64,4,384]{2,1,0:T(4,128)(2,1)}), bf16[64,4,384]{2,1,0:T(4,128)(2,1)S(1)}, u32[]{:S(2)}, u32[]{:S(2)}) async-start(bf16[64,4,384]{2,1,0:T(4,128)(2,1)} %get-tuple-element.47), calls=%async_computation.1 | async-start | bytes 393216 | tf_op jit(solution)/shard_map/all_to_all | solution.py:404
  29.8 4.5 %collective-permute-start = (bf16[32,384]{1,0:T(8,128)(2,1)}, bf16[32,384]{1,0:T(8,128)(2,1)S(1)}, u32[]{:S(2)}, u32[]{:S(2)}) collective-permute-start(bf16[32,384]{1,0:T(8,128)(2,1)} %get-tuple-element.53), channel_id=1, source_target_pairs={{0,64},{64,128},{128,192},{1,65},{65,129},{129,193},{2,66},{66,130... | collective-permute-start | bytes 73736 | tf_op jit(solution)/shard_map/ppermute | solution.py:400
  33.0 5.1 %collective-permute-start.1 = (bf16[32,384]{1,0:T(8,128)(2,1)}, bf16[32,384]{1,0:T(8,128)(2,1)S(1)}, u32[]{:S(2)}, u32[]{:S(2)}) collective-permute-start(bf16[32,384]{1,0:T(8,128)(2,1)} %get-tuple-element.54), channel_id=1, source_target_pairs={{64,0},{128,64},{192,128},{65,1},{129,65},{193,129},{66,2},{130,66... | collective-permute-start | bytes 73736 | tf_op jit(solution)/shard_map/ppermute | solution.py:400
  45.9 19.7 %all-to-all-start.2 = ((bf16[64,4,384]{2,1,0:T(4,128)(2,1)}), bf16[64,4,384]{2,1,0:T(4,128)(2,1)S(1)}, u32[]{:S(2)}, u32[]{:S(2)}) async-start(bf16[64,4,384]{2,1,0:T(4,128)(2,1)} %get-tuple-element.56), calls=%async_computation.2 | async-start | bytes 393216 | tf_op jit(solution)/shard_map/all_to_all | solution.py:404
  66.7 16.7 %all-to-all-start.3 = ((bf16[64,4,384]{2,1,0:T(4,128)(2,1)}), bf16[64,4,384]{2,1,0:T(4,128)(2,1)S(1)}, u32[]{:S(2)}, u32[]{:S(2)}) async-start(bf16[64,4,384]{2,1,0:T(4,128)(2,1)} %get-tuple-element.67), calls=%async_computation.3 | async-start | bytes 393216 | tf_op jit(solution)/shard_map/all_to_all | solution.py:404
  87.3 16.6 %all-to-all-start.4 = ((bf16[64,4,384]{2,1,0:T(4,128)(2,1)}), bf16[64,4,384]{2,1,0:T(4,128)(2,1)S(1)}, u32[]{:S(2)}, u32[]{:S(2)}) async-start(bf16[64,4,384]{2,1,0:T(4,128)(2,1)} %get-tuple-element.77), calls=%async_computation.4 | async-start | bytes 393216 | tf_op jit(solution)/shard_map/all_to_all | solution.py:404
  91.7 5.9 %collective-permute-start.2 = (bf16[32,384]{1,0:T(8,128)(2,1)}, bf16[32,384]{1,0:T(8,128)(2,1)S(1)}, u32[]{:S(2)}, u32[]{:S(2)}) collective-permute-start(bf16[32,384]{1,0:T(8,128)(2,1)} %get-tuple-element.85), channel_id=1, source_target_pairs={{0,64},{64,128},{128,192},{1,65},{65,129},{129,193},{2,66},{66,130... | collective-permute-start | bytes 73736 | tf_op jit(solution)/shard_map/ppermute | solution.py:400
  94.9 5.1 %collective-permute-start.3 = (bf16[32,384]{1,0:T(8,128)(2,1)}, bf16[32,384]{1,0:T(8,128)(2,1)S(1)}, u32[]{:S(2)}, u32[]{:S(2)}) collective-permute-start(bf16[32,384]{1,0:T(8,128)(2,1)} %get-tuple-element.86), channel_id=1, source_target_pairs={{64,0},{128,64},{192,128},{65,1},{129,65},{193,129},{66,2},{130,66... | collective-permute-start | bytes 73736 | tf_op jit(solution)/shard_map/ppermute | solution.py:400

commit v9 on v8

--- a/solution.py
+++ b/solution.py
@@ -8,6 +8,7 @@
 PENALTY = 2.0
 CAPACITY = 4
 GROUP = 16
+HALF = 8
 PIECES = 4
 PARTS = 2
 VMEM = pltpu.VMEM
@@ -227,57 +228,57 @@
     ]
     for edge in edges:
         edge.start()
-    member = lax.rem(iota((3 * GROUP, nodes), 0), GROUP)
+    member = lax.rem(iota((3 * HALF, nodes), 0), HALF)
     place_in = lax.rem(member, 4)
-    block_of = lax.div(member, 4)
+    second = member >= 4
     odd = lax.rem(place_in, 2) == 1
     late = place_in >= 2
-    zero = jnp.zeros((3 * GROUP, nodes), BF16)
-    master = dot(get_ref[...], gathered(in_ref, scratch)).astype(BF16)
-
-    def choose(parts):
-        result = parts[0]
-        for b in range(1, GROUP // 4):
-            result = jnp.where(block_of == b, parts[b], result)
-        return result
+    master = dot(get_ref[...], gathered(in_ref, scratch))
+
+    def apart(chosen, rows):
+        return jnp.concatenate([jnp.where(chosen, 0.0, rows), jnp.where(chosen, rows, 0.0)], axis=1).astype(BF16)
+
+    def joined(halves, c):
+        return jnp.concatenate([half[HALF * c : HALF * (c + 1)] for half in halves], axis=0)
 
     for g in range(segs // GROUP):
-        own = slice(GROUP * g, GROUP * (g + 1))
         if GROUP * g == early:
             later.wait()
-        um = jnp.concatenate(columns(master[own]), axis=0)
-        normal = jnp.concatenate(columns(normal_ref[own, :]), axis=0)
-        mortar_ref, start = early_ref, GROUP * g
-        if start >= early:
-            mortar_ref, start = later_ref, start - early
-        weights = []
-        for s in range(start, start + GROUP, 4):
-            left = mortar_ref[s : s + 2].reshape(2 * nodes, nodes)
-            right = mortar_ref[s + 2 : s + 4].reshape(2 * nodes, nodes)
-            weights.append(jnp.concatenate([left, right], axis=1))
-        lhs = jnp.concatenate([jnp.where(late, zero, um), jnp.where(late, um, zero)], axis=1)
-        parts = []
-        for w in weights:
-            r = dot(lhs, w, ((1,), (1,)))
-            parts.append(jnp.where(odd, r[:, nodes:], r[:, :nodes]))
-        terms = normal * choose(parts)
-        gap = known_ref[own, :] + (terms[:GROUP] + terms[GROUP : 2 * GROUP] + terms[2 * GROUP :])
-        pressure = PENALTY * jnp.maximum(-gap, 0.0)
-        pushed = jnp.concatenate([pressure] * 3, axis=0) * normal
-        high = pushed.astype(BF16)
-        rest = (pushed - high.astype(F32)).astype(BF16)
-        lhs = jnp.concatenate([jnp.where(odd, zero, high), jnp.where(odd, high, zero)], axis=1)
-        parts = []
-        for w in weights:
-            r = dot(lhs, w)
-            parts.append(jnp.where(late, r[:, nodes:], r[:, :nodes]))
-        back = (-choose(parts)).astype(BF16)
+        backs, pushes = [], []
+        for start in range(GROUP * g, GROUP * (g + 1), HALF):
+            own = slice(start, start + HALF)
+            um = jnp.concatenate(columns(master[own]), axis=0)
+            normal = jnp.concatenate(columns(normal_ref[own, :]), axis=0)
+            mortar_ref, s = (early_ref, start) if start < early else (later_ref, start - early)
+            weights = []
+            for k in (s, s + 4):
+                left = mortar_ref[k : k + 2].reshape(2 * nodes, nodes)
+                right = mortar_ref[k + 2 : k + 4].reshape(2 * nodes, nodes)
+                weights.append(jnp.concatenate([left, right], axis=1))
+            lhs = apart(late, um)
+            parts = []
+            for w in weights:
+                r = dot(lhs, w, ((1,), (1,)))
+                parts.append(jnp.where(odd, r[:, nodes:], r[:, :nodes]))
+            terms = normal * jnp.where(second, parts[1], parts[0])
+            gap = known_ref[own, :] + (terms[:HALF] + terms[HALF : 2 * HALF] + terms[2 * HALF :])
+            pressure = PENALTY * jnp.maximum(-gap, 0.0)
+            pushed = jnp.concatenate([pressure] * 3, axis=0) * normal
+            lhs = apart(odd, pushed)
+            parts = []
+            for w in weights:
+                r = dot(lhs, w)
+                parts.append(jnp.where(late, r[:, nodes:], r[:, :nodes]))
+            backs.append(-jnp.where(second, parts[1], parts[0]))
+            pushes.append(pushed)
+        own = slice(GROUP * g, GROUP * (g + 1))
         for c in range(3):
-            rows = slice(GROUP * c, GROUP * (c + 1))
             cols = slice(nodes * c, nodes * (c + 1))
-            back_ref[own, cols] = back[rows]
-            pushed_ref[own, cols] = high[rows]
-            pushed_ref[segs + GROUP * g : segs + GROUP * (g + 1), cols] = rest[rows]
+            back_ref[own, cols] = joined(backs, c).astype(BF16)
+            pushed = joined(pushes, c)
+            high = pushed.astype(BF16)
+            pushed_ref[own, cols] = high
+            pushed_ref[segs + GROUP * g : segs + GROUP * (g + 1), cols] = (pushed - high.astype(F32)).astype(BF16)
     store = pltpu.make_async_copy(pushed_ref, pushed_hbm, sems.at[0])
     store.start()
     stores = edges + [store]

time: 105 us -> 107 us (1.019)
  Pallas kernels: 27.6 us -> 28.7 us
    pallas_call x2, Pallas kernels: 7.84 us -> 8.96 us  [contact(): pl.pallas_call(contact_kernel, out_shape=[pltpu.HBM(out.shape, BF16) for...]
where the time goes in v9:
time: 107 us; the launch traced here: 106 us
  starting transfers between devices  43.2 us (40%)
  waiting for transfers between devices  33.9 us (32%)
  Pallas kernels  28.7 us (27%)
    all_to_all x5, starting transfers between devices, exchange(): return lax.all_to_all(parts, 'dom', 0, 0, tiled=True)  34.2 us
    all_to_all x5, waiting for transfers between devices, exchange(): return lax.all_to_all(parts, 'dom', 0, 0, tiled=True)  27.7 us
    pallas_call x8, Pallas kernels, staged(): pl.pallas_call(kernel, out_shape=tuple((space(i, out) for i, out in enume...  18.8 us
    ppermute x4, starting transfers between devices, shift(): return lax.ppermute(block, 'slab', pairs)  8.99 us
    pallas_call x2, Pallas kernels, contact(): pl.pallas_call(contact_kernel, out_shape=[pltpu.HBM(out.shape, BF16) for...  8.96 us
    ppermute x4, waiting for transfers between devices, shift(): return lax.ppermute(block, 'slab', pairs)  6.13 us
  transfers between devices with their start and end apart: 9, of which 7 were waited for; matrix products, arithmetic and copies ran while one was open for 0% of the time, Pallas kernels for 14%

profile of v9, /device:TPU:1, one launch (start us, length us, event | category | flops | bytes accessed | tf_op | source)
XLA Modules:
  0.0 106.0 jit_solution(7241645660147718757)
XLA Ops:
  0.0 1.7 %shard_map.118.refs_7_ = f32[64,128]{1,0:T(8,128)} custom-call(s32[1,1,128]{2,1,0:T(1,128)} %refs_0_.4, s32[1,1,128]{2,1,0:T(1,128)} %refs_1_.3), custom_call_target="tpu_custom_call" | custom-call | tf_op jit(solution)/shard_map/pallas_call | solution.py:88
  1.7 13.0 %all-to-all-start = ((f32[64,1,128]{2,1,0:T(1,128)}), f32[64,1,128]{2,1,0:T(1,128)S(1)}, u32[]{:S(2)}, u32[]{:S(2)}) async-start(f32[64,1,128]{2,1,0:T(1,128)} %bitcast.1), calls=%async_computation | async-start | bytes 65536 | tf_op jit(solution)/shard_map/all_to_all | solution.py:405
  14.7 2.2 %shard_map.119 = (bf16[256,128]{1,0:T(8,128)(2,1)}, bf16[128,256]{1,0:T(8,128)(2,1)}, bf16[128,96]{1,0:T(8,128)(2,1)}, bf16[32,256]{1,0:T(8,128)(2,1)}, f32[128,...) custom-call(s32[1,1,128]{2,1,0:T(1,128)} %refs_0_.4, ...), custom_call_target="tpu_custom_call" | custom-call | tf_op jit(solution)/shard_map/pallas_call | solution.py:88
  16.8 7.2 %all-to-all-done = f32[64,1,128]{2,1,0:T(1,128)S(1)} async-done(((f32[64,1,128]{2,1,0:T(1,128)}), f32[64,1,128]{2,1,0:T(1,128)S(1)}, u32[]{:S(2)}, u32[]{:S(2)}) %all-to-all-start) | async-done | bytes 32800 | tf_op jit(solution)/shard_map/all_to_all | solution.py:405
  24.1 1.0 shard_map.120
  25.1 4.7 %all-to-all-start.1 = ((bf16[64,4,384]{2,1,0:T(4,128)(2,1)}), bf16[64,4,384]{2,1,0:T(4,128)(2,1)S(1)}, u32[]{:S(2)}, u32[]{:S(2)}) async-start(bf16[64,4,384]{2,1,0:T(4,128)(2,1)} %get-tuple-element.47), calls=%async_computation.1 | async-start | bytes 393216 | tf_op jit(solution)/shard_map/all_to_all | solution.py:405
  29.8 3.2 %collective-permute-start = (bf16[32,384]{1,0:T(8,128)(2,1)}, bf16[32,384]{1,0:T(8,128)(2,1)S(1)}, u32[]{:S(2)}, u32[]{:S(2)}) collective-permute-start(bf16[32,384]{1,0:T(8,128)(2,1)} %get-tuple-element.53), channel_id=1, source_target_pairs={{0,64},{64,128},{128,192},{1,65},{65,129},{129,193},{2,66},{66,130... | collective-permute-start | bytes 73736 | tf_op jit(solution)/shard_map/ppermute | solution.py:401
  33.0 1.3 %collective-permute-start.1 = (bf16[32,384]{1,0:T(8,128)(2,1)}, bf16[32,384]{1,0:T(8,128)(2,1)S(1)}, u32[]{:S(2)}, u32[]{:S(2)}) collective-permute-start(bf16[32,384]{1,0:T(8,128)(2,1)} %get-tuple-element.54), channel_id=1, source_target_pairs={{64,0},{128,64},{192,128},{65,1},{129,65},{193,129},{66,2},{130,66... | collective-permute-start | bytes 73736 | tf_op jit(solution)/shard_map/ppermute | solution.py:401
  34.3 0.0 collective-permute-done.low_hbm
  34.3 3.8 %collective-permute-done.1.high_hbm = bf16[32,384]{1,0:T(8,128)(2,1)S(1)} collective-permute-done((bf16[32,384]{1,0:T(8,128)(2,1)}, bf16[32,384]{1,0:T(8,128)(2,1)S(1)}, u32[]{:S(2)}, u32[]{:S(2)}) %collective-permute-start.1) | collective-permute-done | bytes 24608 | tf_op jit(solution)/shard_map/ppermute | solution.py:401
  38.1 3.9 %all-to-all-done.1.in_ref = bf16[64,4,384]{2,1,0:T(4,128)(2,1)S(1)} async-done(((bf16[64,4,384]{2,1,0:T(4,128)(2,1)}), bf16[64,4,384]{2,1,0:T(4,128)(2,1)S(1)}, u32[]{:S(2)}, u32[]{:S(2)}) %all-to-all-start.1) | async-done | bytes 196640 | tf_op jit(solution)/shard_map/all_to_all | solution.py:405
  42.0 4.5 %shard_map.121 = (bf16[64,4,384]{2,1,0:T(4,128)(2,1)}, bf16[256,384]{1,0:T(8,128)(2,1)}, bf16[32,384]{1,0:T(8,128)(2,1)}, bf16[32,384]{1,0:T(8,128)(2,1)}) custom-call(bf16[64,4,384]{2,1,0:T(4,128)(2,1)S(1)} %all-to-all-done.1.in_ref, bf16[80,128,128]{2,1,0:T(8,128)(2,1)S(1)} %get-tuple-element.48.early_ref, bf16[128,256]{1,0:T(8,128)(2,1)S(1)} %get-tuple-element.49.get_ref, ...), custom_call_target="tpu_custom_call" | custom-call | tf_op jit(solution)/shard_map/pallas_call | solution.py:456
  46.5 7.7 %all-to-all-start.2 = ((bf16[64,4,384]{2,1,0:T(4,128)(2,1)}), bf16[64,4,384]{2,1,0:T(4,128)(2,1)S(1)}, u32[]{:S(2)}, u32[]{:S(2)}) async-start(bf16[64,4,384]{2,1,0:T(4,128)(2,1)} %get-tuple-element.56), calls=%async_computation.2 | async-start | bytes 393216 | tf_op jit(solution)/shard_map/all_to_all | solution.py:405
  54.1 5.6 %shard_map.122 = (f32[1,24,32,384]{3,2,1,0:T(8,128)}, f32[32,384]{1,0:T(8,128)S(1)}, f32[32,384]{1,0:T(8,128)S(1)}, bf16[256,128]{1,0:T(8,128)(2,1)S(1)}, bf16[3...) custom-call(f32[1,24,32,384]{3,2,1,0:T(8,128)} %refs_1_.5, ...), custom_call_target="tpu_custom_call" | custom-call | tf_op jit(solution)/shard_map/pallas_call | solution.py:88
  59.7 6.5 %all-to-all-done.2.refs_0_ = bf16[64,4,384]{2,1,0:T(4,128)(2,1)S(1)} async-done(((bf16[64,4,384]{2,1,0:T(4,128)(2,1)}), bf16[64,4,384]{2,1,0:T(4,128)(2,1)S(1)}, u32[]{:S(2)}, u32[]{:S(2)}) %all-to-all-start.2) | async-done | bytes 196640 | tf_op jit(solution)/shard_map/all_to_all | solution.py:405
  66.2 1.1 %shard_map.123 = (bf16[64,4,384]{2,1,0:T(4,128)(2,1)}, f32[1,1,32,384]{3,2,1,0:T(8,128)}, bf16[32,384]{1,0:T(8,128)(2,1)}) custom-call(bf16[64,4,384]{2,1,0:T(4,128)(2,1)S(1)} %all-to-all-done.2.refs_0_, bf16[256,128]{1,0:T(8,128)(2,1)S(1)} %get-tuple-element.64.refs_1_, f32[32,384]{1,0:T(8,128)S(1)} %get-tuple-element.65.refs_2_, ...), custom_call_target="tpu_custom_call" | custom-call | tf_op jit(solution)/shard_map/pallas_call | solution.py:88
  67.3 4.5 %all-to-all-start.3 = ((bf16[64,4,384]{2,1,0:T(4,128)(2,1)}), bf16[64,4,384]{2,1,0:T(4,128)(2,1)S(1)}, u32[]{:S(2)}, u32[]{:S(2)}) async-start(bf16[64,4,384]{2,1,0:T(4,128)(2,1)} %get-tuple-element.67), calls=%async_computation.3 | async-start | bytes 393216 | tf_op jit(solution)/shard_map/all_to_all | solution.py:405
  71.8 1.1 %shard_map.124.known_ref = f32[128,128]{1,0:T(8,128)S(1)} custom-call(f32[1,1,32,384]{3,2,1,0:T(8,128)} %get-tuple-element.72.refs_0_.refs_1_, bf16[128,96]{1,0:T(8,128)(2,1)} %get-tuple-element.73.refs_1_, f32[128,384]{1,0:T(8,128)} %get-tuple-element.63.refs_15_.refs_2_, f32[1,1,128,128]{3,2,1,0:T(8,128)} %refs_3_.7), custom_call_target="tpu_custom_call" | custom-call | tf_op jit(solution)/shard_map/pallas_call | solution.py:88
  72.9 4.8 %shard_map.125.token.refs_0_.refs_1_.field_hbm = f32[1,24,32,384]{3,2,1,0:T(8,128)} custom-call(f32[1,24,32,384]{3,2,1,0:T(8,128)} %get-tuple-element.76.refs_0_, f32[1,1,32,384]{3,2,1,0:T(8,128)} %get-tuple-element.72.refs_0_.refs_1_, bf16[384,384]{1,0:T(8,128)(2,1)} %refs_2_.6, bf16[384,384]{1,0:T(8,128)(2,1)} %refs_7_.1, bf16[384,384]{1,0:T(8,128)(2,1)} %refs_4_.5, ...), custom_call_target="tpu_custom_call" | custom-call | tf_op jit(solution)/shard_map/pallas_call | solution.py:88
  77.7 6.2 %all-to-all-done.3.in_ref = bf16[64,4,384]{2,1,0:T(4,128)(2,1)S(1)} async-done(((bf16[64,4,384]{2,1,0:T(4,128)(2,1)}), bf16[64,4,384]{2,1,0:T(4,128)(2,1)S(1)}, u32[]{:S(2)}, u32[]{:S(2)}) %all-to-all-start.3) | async-done | bytes 196640 | tf_op jit(solution)/shard_map/all_to_all | solution.py:405
  84.0 4.5 %shard_map.126 = (bf16[64,4,384]{2,1,0:T(4,128)(2,1)}, bf16[256,384]{1,0:T(8,128)(2,1)}, bf16[32,384]{1,0:T(8,128)(2,1)}, bf16[32,384]{1,0:T(8,128)(2,1)}) custom-call(bf16[64,4,384]{2,1,0:T(4,128)(2,1)S(1)} %all-to-all-done.3.in_ref, bf16[80,128,128]{2,1,0:T(8,128)(2,1)S(1)} %get-tuple-element.68.early_ref, bf16[128,256]{1,0:T(8,128)(2,1)S(1)} %get-tuple-element.69.get_ref, ...), custom_call_target="tpu_custom_call" | custom-call | tf_op jit(solution)/shard_map/pallas_call | solution.py:456
  88.5 4.4 %all-to-all-start.4 = ((bf16[64,4,384]{2,1,0:T(4,128)(2,1)}), bf16[64,4,384]{2,1,0:T(4,128)(2,1)S(1)}, u32[]{:S(2)}, u32[]{:S(2)}) async-start(bf16[64,4,384]{2,1,0:T(4,128)(2,1)} %get-tuple-element.77), calls=%async_computation.4 | async-start | bytes 393216 | tf_op jit(solution)/shard_map/all_to_all | solution.py:405
  92.8 3.2 %collective-permute-start.2 = (bf16[32,384]{1,0:T(8,128)(2,1)}, bf16[32,384]{1,0:T(8,128)(2,1)S(1)}, u32[]{:S(2)}, u32[]{:S(2)}) collective-permute-start(bf16[32,384]{1,0:T(8,128)(2,1)} %get-tuple-element.85), channel_id=1, source_target_pairs={{0,64},{64,128},{128,192},{1,65},{65,129},{129,193},{2,66},{66,130... | collective-permute-start | bytes 73736 | tf_op jit(solution)/shard_map/ppermute | solution.py:401
  96.1 1.3 %collective-permute-start.3 = (bf16[32,384]{1,0:T(8,128)(2,1)}, bf16[32,384]{1,0:T(8,128)(2,1)S(1)}, u32[]{:S(2)}, u32[]{:S(2)}) collective-permute-start(bf16[32,384]{1,0:T(8,128)(2,1)} %get-tuple-element.86), channel_id=1, source_target_pairs={{64,0},{128,64},{192,128},{65,1},{129,65},{193,129},{66,2},{130,66... | collective-permute-start | bytes 73736 | tf_op jit(solution)/shard_map/ppermute | solution.py:401
  97.4 1.4 %shard_map.127 = (f32[32,384]{1,0:T(8,128)S(1)}, f32[32,384]{1,0:T(8,128)S(1)}, f32[32,384]{1,0:T(8,128)S(1)}, f32[32,384]{1,0:T(8,128)S(1)}, bf16[256,128]{1,0:...) custom-call(f32[1,24,32,384]{3,2,1,0:T(8,128)} %shard_map.125.token.refs_0_.refs_1_.field_hbm, ...), custom_call_target="tpu_custom_call" | custom-call | tf_op jit(solution)/shard_map/pallas_call | solution.py:88
  98.8 0.0 collective-permute-done.2.low_ref
  98.8 2.4 %collective-permute-done.3.high_ref = bf16[32,384]{1,0:T(8,128)(2,1)S(1)} collective-permute-done((bf16[32,384]{1,0:T(8,128)(2,1)}, bf16[32,384]{1,0:T(8,128)(2,1)S(1)}, u32[]{:S(2)}, u32[]{:S(2)}) %collective-permute-start.3) | collective-permute-done | bytes 24608 | tf_op jit(solution)/shard_map/ppermute | solution.py:401
  101.1 3.9 %all-to-all-done.4.in_ref = bf16[64,4,384]{2,1,0:T(4,128)(2,1)S(1)} async-done(((bf16[64,4,384]{2,1,0:T(4,128)(2,1)}), bf16[64,4,384]{2,1,0:T(4,128)(2,1)S(1)}, u32[]{:S(2)}, u32[]{:S(2)}) %all-to-all-start.4) | async-done | bytes 196640 | tf_op jit(solution)/shard_map/all_to_all | solution.py:405
  105.0 0.9 shard_map.128
Async XLA Ops:
  1.7 22.4 %all-to-all-start = ((f32[64,1,128]{2,1,0:T(1,128)}), f32[64,1,128]{2,1,0:T(1,128)S(1)}, u32[]{:S(2)}, u32[]{:S(2)}) async-start(f32[64,1,128]{2,1,0:T(1,128)} %bitcast.1), calls=%async_computation | async-start | bytes 65536 | tf_op jit(solution)/shard_map/all_to_all | solution.py:405
  25.1 16.9 %all-to-all-start.1 = ((bf16[64,4,384]{2,1,0:T(4,128)(2,1)}), bf16[64,4,384]{2,1,0:T(4,128)(2,1)S(1)}, u32[]{:S(2)}, u32[]{:S(2)}) async-start(bf16[64,4,384]{2,1,0:T(4,128)(2,1)} %get-tuple-element.47), calls=%async_computation.1 | async-start | bytes 393216 | tf_op jit(solution)/shard_map/all_to_all | solution.py:405
  29.8 4.5 %collective-permute-start = (bf16[32,384]{1,0:T(8,128)(2,1)}, bf16[32,384]{1,0:T(8,128)(2,1)S(1)}, u32[]{:S(2)}, u32[]{:S(2)}) collective-permute-start(bf16[32,384]{1,0:T(8,128)(2,1)} %get-tuple-element.53), channel_id=1, source_target_pairs={{0,64},{64,128},{128,192},{1,65},{65,129},{129,193},{2,66},{66,130... | collective-permute-start | bytes 73736 | tf_op jit(solution)/shard_map/ppermute | solution.py:401
  33.0 5.1 %collective-permute-start.1 = (bf16[32,384]{1,0:T(8,128)(2,1)}, bf16[32,384]{1,0:T(8,128)(2,1)S(1)}, u32[]{:S(2)}, u32[]{:S(2)}) collective-permute-start(bf16[32,384]{1,0:T(8,128)(2,1)} %get-tuple-element.54), channel_id=1, source_target_pairs={{64,0},{128,64},{192,128},{65,1},{129,65},{193,129},{66,2},{130,66... | collective-permute-start | bytes 73736 | tf_op jit(solution)/shard_map/ppermute | solution.py:401
  46.5 19.7 %all-to-all-start.2 = ((bf16[64,4,384]{2,1,0:T(4,128)(2,1)}), bf16[64,4,384]{2,1,0:T(4,128)(2,1)S(1)}, u32[]{:S(2)}, u32[]{:S(2)}) async-start(bf16[64,4,384]{2,1,0:T(4,128)(2,1)} %get-tuple-element.56), calls=%async_computation.2 | async-start | bytes 393216 | tf_op jit(solution)/shard_map/all_to_all | solution.py:405
  67.3 16.7 %all-to-all-start.3 = ((bf16[64,4,384]{2,1,0:T(4,128)(2,1)}), bf16[64,4,384]{2,1,0:T(4,128)(2,1)S(1)}, u32[]{:S(2)}, u32[]{:S(2)}) async-start(bf16[64,4,384]{2,1,0:T(4,128)(2,1)} %get-tuple-element.67), calls=%async_computation.3 | async-start | bytes 393216 | tf_op jit(solution)/shard_map/all_to_all | solution.py:405
  88.5 16.6 %all-to-all-start.4 = ((bf16[64,4,384]{2,1,0:T(4,128)(2,1)}), bf16[64,4,384]{2,1,0:T(4,128)(2,1)S(1)}, u32[]{:S(2)}, u32[]{:S(2)}) async-start(bf16[64,4,384]{2,1,0:T(4,128)(2,1)} %get-tuple-element.77), calls=%async_computation.4 | async-start | bytes 393216 | tf_op jit(solution)/shard_map/all_to_all | solution.py:405
  92.8 5.9 %collective-permute-start.2 = (bf16[32,384]{1,0:T(8,128)(2,1)}, bf16[32,384]{1,0:T(8,128)(2,1)S(1)}, u32[]{:S(2)}, u32[]{:S(2)}) collective-permute-start(bf16[32,384]{1,0:T(8,128)(2,1)} %get-tuple-element.85), channel_id=1, source_target_pairs={{0,64},{64,128},{128,192},{1,65},{65,129},{129,193},{2,66},{66,130... | collective-permute-start | bytes 73736 | tf_op jit(solution)/shard_map/ppermute | solution.py:401
  96.1 5.1 %collective-permute-start.3 = (bf16[32,384]{1,0:T(8,128)(2,1)}, bf16[32,384]{1,0:T(8,128)(2,1)S(1)}, u32[]{:S(2)}, u32[]{:S(2)}) collective-permute-start(bf16[32,384]{1,0:T(8,128)(2,1)} %get-tuple-element.86), channel_id=1, source_target_pairs={{64,0},{128,64},{192,128},{65,1},{129,65},{193,129},{66,2},{130,66... | collective-permute-start | bytes 73736 | tf_op jit(solution)/shard_map/ppermute | solution.py:401

commit v10 on v8

--- a/solution.py
+++ b/solution.py
@@ -241,45 +241,46 @@
             result = jnp.where(block_of == b, parts[b], result)
         return result
 
+    def weights(g):
+        ref, start = (early_ref, GROUP * g) if GROUP * g < early else (later_ref, GROUP * g - early)
+        for k in range(start, start + GROUP, 4):
+            left = ref[k : k + 2].reshape(2 * nodes, nodes)
+            right = ref[k + 2 : k + 4].reshape(2 * nodes, nodes)
+            yield jnp.concatenate([left, right], axis=1)
+
     for g in range(segs // GROUP):
         own = slice(GROUP * g, GROUP * (g + 1))
         if GROUP * g == early:
             later.wait()
         um = jnp.concatenate(columns(master[own]), axis=0)
         normal = jnp.concatenate(columns(normal_ref[own, :]), axis=0)
-        mortar_ref, start = early_ref, GROUP * g
-        if start >= early:
-            mortar_ref, start = later_ref, start - early
-        weights = []
-        for s in range(start, start + GROUP, 4):
-            left = mortar_ref[s : s + 2].reshape(2 * nodes, nodes)
-            right = mortar_ref[s + 2 : s + 4].reshape(2 * nodes, nodes)
-            weights.append(jnp.concatenate([left, right], axis=1))
         lhs = jnp.concatenate([jnp.where(late, zero, um), jnp.where(late, um, zero)], axis=1)
         parts = []
-        for w in weights:
+        for w in weights(g):
             r = dot(lhs, w, ((1,), (1,)))
             parts.append(jnp.where(odd, r[:, nodes:], r[:, :nodes]))
         terms = normal * choose(parts)
         gap = known_ref[own, :] + (terms[:GROUP] + terms[GROUP : 2 * GROUP] + terms[2 * GROUP :])
         pressure = PENALTY * jnp.maximum(-gap, 0.0)
-        pushed = jnp.concatenate([pressure] * 3, axis=0) * normal
-        high = pushed.astype(BF16)
-        rest = (pushed - high.astype(F32)).astype(BF16)
+        for c, part in enumerate(columns(normal_ref[own, :])):
+            cols = slice(nodes * c, nodes * (c + 1))
+            pushed = pressure * part
+            high = pushed.astype(BF16)
+            pushed_ref[own, cols] = high
+            pushed_ref[segs + GROUP * g : segs + GROUP * (g + 1), cols] = (pushed - high.astype(F32)).astype(BF16)
+    store = pltpu.make_async_copy(pushed_ref, pushed_hbm, sems.at[0])
+    store.start()
+    for g in range(segs // GROUP):
+        own = slice(GROUP * g, GROUP * (g + 1))
+        high = jnp.concatenate(columns(pushed_ref[own, :]), axis=0)
         lhs = jnp.concatenate([jnp.where(odd, zero, high), jnp.where(odd, high, zero)], axis=1)
         parts = []
-        for w in weights:
+        for w in weights(g):
             r = dot(lhs, w)
             parts.append(jnp.where(late, r[:, nodes:], r[:, :nodes]))
         back = (-choose(parts)).astype(BF16)
         for c in range(3):
-            rows = slice(GROUP * c, GROUP * (c + 1))
-            cols = slice(nodes * c, nodes * (c + 1))
-            back_ref[own, cols] = back[rows]
-            pushed_ref[own, cols] = high[rows]
-            pushed_ref[segs + GROUP * g : segs + GROUP * (g + 1), cols] = rest[rows]
-    store = pltpu.make_async_copy(pushed_ref, pushed_hbm, sems.at[0])
-    store.start()
+            back_ref[own, nodes * c : nodes * (c + 1)] = back[GROUP * c : GROUP * (c + 1)]
     stores = edges + [store]
 
     def send(piece, part):

time: 105 us -> 105 us (level)
  no operation moved by 1% of the time
where the time goes in v10:
time: 105 us; the launch traced here: 104 us
  starting transfers between devices  43.2 us (41%)
  waiting for transfers between devices  33.9 us (32%)
  Pallas kernels  27 us (26%)
    all_to_all x5, starting transfers between devices, exchange(): return lax.all_to_all(parts, 'dom', 0, 0, tiled=True)  34.2 us
    all_to_all x5, waiting for transfers between devices, exchange(): return lax.all_to_all(parts, 'dom', 0, 0, tiled=True)  27.7 us
    pallas_call x8, Pallas kernels, staged(): pl.pallas_call(kernel, out_shape=tuple((space(i, out) for i, out in enume...  18.8 us
    ppermute x4, starting transfers between devices, shift(): return lax.ppermute(block, 'slab', pairs)  9 us
    pallas_call x2, Pallas kernels, contact(): pl.pallas_call(contact_kernel, out_shape=[pltpu.HBM(out.shape, BF16) for...  7.26 us
    ppermute x4, waiting for transfers between devices, shift(): return lax.ppermute(block, 'slab', pairs)  6.13 us
  transfers between devices with their start and end apart: 9, of which 7 were waited for; matrix products, arithmetic and copies ran while one was open for 0% of the time, Pallas kernels for 14%

profile of v10, /device:TPU:1, one launch (start us, length us, event | category | flops | bytes accessed | tf_op | source)
XLA Modules:
  0.0 104.2 jit_solution(5770629814334853195)
XLA Ops:
  0.0 1.7 %shard_map.118.refs_7_ = f32[64,128]{1,0:T(8,128)} custom-call(s32[1,1,128]{2,1,0:T(1,128)} %refs_0_.4, s32[1,1,128]{2,1,0:T(1,128)} %refs_1_.3), custom_call_target="tpu_custom_call" | custom-call | tf_op jit(solution)/shard_map/pallas_call | solution.py:87
  1.7 13.0 %all-to-all-start = ((f32[64,1,128]{2,1,0:T(1,128)}), f32[64,1,128]{2,1,0:T(1,128)S(1)}, u32[]{:S(2)}, u32[]{:S(2)}) async-start(f32[64,1,128]{2,1,0:T(1,128)} %bitcast.1), calls=%async_computation | async-start | bytes 65536 | tf_op jit(solution)/shard_map/all_to_all | solution.py:405
  14.7 2.2 %shard_map.119 = (bf16[256,128]{1,0:T(8,128)(2,1)}, bf16[128,256]{1,0:T(8,128)(2,1)}, bf16[128,96]{1,0:T(8,128)(2,1)}, bf16[32,256]{1,0:T(8,128)(2,1)}, f32[128,...) custom-call(s32[1,1,128]{2,1,0:T(1,128)} %refs_0_.4, ...), custom_call_target="tpu_custom_call" | custom-call | tf_op jit(solution)/shard_map/pallas_call | solution.py:87
  16.8 7.2 %all-to-all-done = f32[64,1,128]{2,1,0:T(1,128)S(1)} async-done(((f32[64,1,128]{2,1,0:T(1,128)}), f32[64,1,128]{2,1,0:T(1,128)S(1)}, u32[]{:S(2)}, u32[]{:S(2)}) %all-to-all-start) | async-done | bytes 32800 | tf_op jit(solution)/shard_map/all_to_all | solution.py:405
  24.1 1.0 shard_map.120
  25.1 4.7 %all-to-all-start.1 = ((bf16[64,4,384]{2,1,0:T(4,128)(2,1)}), bf16[64,4,384]{2,1,0:T(4,128)(2,1)S(1)}, u32[]{:S(2)}, u32[]{:S(2)}) async-start(bf16[64,4,384]{2,1,0:T(4,128)(2,1)} %get-tuple-element.47), calls=%async_computation.1 | async-start | bytes 393216 | tf_op jit(solution)/shard_map/all_to_all | solution.py:405
  29.8 3.2 %collective-permute-start = (bf16[32,384]{1,0:T(8,128)(2,1)}, bf16[32,384]{1,0:T(8,128)(2,1)S(1)}, u32[]{:S(2)}, u32[]{:S(2)}) collective-permute-start(bf16[32,384]{1,0:T(8,128)(2,1)} %get-tuple-element.53), channel_id=1, source_target_pairs={{0,64},{64,128},{128,192},{1,65},{65,129},{129,193},{2,66},{66,130... | collective-permute-start | bytes 73736 | tf_op jit(solution)/shard_map/ppermute | solution.py:401
  33.0 1.3 %collective-permute-start.1 = (bf16[32,384]{1,0:T(8,128)(2,1)}, bf16[32,384]{1,0:T(8,128)(2,1)S(1)}, u32[]{:S(2)}, u32[]{:S(2)}) collective-permute-start(bf16[32,384]{1,0:T(8,128)(2,1)} %get-tuple-element.54), channel_id=1, source_target_pairs={{64,0},{128,64},{192,128},{65,1},{129,65},{193,129},{66,2},{130,66... | collective-permute-start | bytes 73736 | tf_op jit(solution)/shard_map/ppermute | solution.py:401
  34.3 0.0 collective-permute-done.low_hbm
  34.3 3.8 %collective-permute-done.1.high_hbm = bf16[32,384]{1,0:T(8,128)(2,1)S(1)} collective-permute-done((bf16[32,384]{1,0:T(8,128)(2,1)}, bf16[32,384]{1,0:T(8,128)(2,1)S(1)}, u32[]{:S(2)}, u32[]{:S(2)}) %collective-permute-start.1) | collective-permute-done | bytes 24608 | tf_op jit(solution)/shard_map/ppermute | solution.py:401
  38.1 3.9 %all-to-all-done.1.in_ref = bf16[64,4,384]{2,1,0:T(4,128)(2,1)S(1)} async-done(((bf16[64,4,384]{2,1,0:T(4,128)(2,1)}), bf16[64,4,384]{2,1,0:T(4,128)(2,1)S(1)}, u32[]{:S(2)}, u32[]{:S(2)}) %all-to-all-start.1) | async-done | bytes 196640 | tf_op jit(solution)/shard_map/all_to_all | solution.py:405
  42.0 3.6 %shard_map.121 = (bf16[64,4,384]{2,1,0:T(4,128)(2,1)}, bf16[256,384]{1,0:T(8,128)(2,1)}, bf16[32,384]{1,0:T(8,128)(2,1)}, bf16[32,384]{1,0:T(8,128)(2,1)}) custom-call(bf16[64,4,384]{2,1,0:T(4,128)(2,1)S(1)} %all-to-all-done.1.in_ref, bf16[80,128,128]{2,1,0:T(8,128)(2,1)S(1)} %get-tuple-element.48.early_ref, bf16[128,256]{1,0:T(8,128)(2,1)S(1)} %get-tuple-element.49.get_ref, ...), custom_call_target="tpu_custom_call" | custom-call | tf_op jit(solution)/shard_map/pallas_call | solution.py:456
  45.6 7.6 %all-to-all-start.2 = ((bf16[64,4,384]{2,1,0:T(4,128)(2,1)}), bf16[64,4,384]{2,1,0:T(4,128)(2,1)S(1)}, u32[]{:S(2)}, u32[]{:S(2)}) async-start(bf16[64,4,384]{2,1,0:T(4,128)(2,1)} %get-tuple-element.56), calls=%async_computation.2 | async-start | bytes 393216 | tf_op jit(solution)/shard_map/all_to_all | solution.py:405
  53.3 5.6 %shard_map.122 = (f32[1,24,32,384]{3,2,1,0:T(8,128)}, f32[32,384]{1,0:T(8,128)S(1)}, f32[32,384]{1,0:T(8,128)S(1)}, bf16[256,128]{1,0:T(8,128)(2,1)S(1)}, bf16[3...) custom-call(f32[1,24,32,384]{3,2,1,0:T(8,128)} %refs_1_.5, ...), custom_call_target="tpu_custom_call" | custom-call | tf_op jit(solution)/shard_map/pallas_call | solution.py:87
  58.9 6.5 %all-to-all-done.2.refs_0_ = bf16[64,4,384]{2,1,0:T(4,128)(2,1)S(1)} async-done(((bf16[64,4,384]{2,1,0:T(4,128)(2,1)}), bf16[64,4,384]{2,1,0:T(4,128)(2,1)S(1)}, u32[]{:S(2)}, u32[]{:S(2)}) %all-to-all-start.2) | async-done | bytes 196640 | tf_op jit(solution)/shard_map/all_to_all | solution.py:405
  65.3 1.1 %shard_map.123 = (bf16[64,4,384]{2,1,0:T(4,128)(2,1)}, f32[1,1,32,384]{3,2,1,0:T(8,128)}, bf16[32,384]{1,0:T(8,128)(2,1)}) custom-call(bf16[64,4,384]{2,1,0:T(4,128)(2,1)S(1)} %all-to-all-done.2.refs_0_, bf16[256,128]{1,0:T(8,128)(2,1)S(1)} %get-tuple-element.64.refs_1_, f32[32,384]{1,0:T(8,128)S(1)} %get-tuple-element.65.refs_2_, ...), custom_call_target="tpu_custom_call" | custom-call | tf_op jit(solution)/shard_map/pallas_call | solution.py:87
  66.4 4.5 %all-to-all-start.3 = ((bf16[64,4,384]{2,1,0:T(4,128)(2,1)}), bf16[64,4,384]{2,1,0:T(4,128)(2,1)S(1)}, u32[]{:S(2)}, u32[]{:S(2)}) async-start(bf16[64,4,384]{2,1,0:T(4,128)(2,1)} %get-tuple-element.67), calls=%async_computation.3 | async-start | bytes 393216 | tf_op jit(solution)/shard_map/all_to_all | solution.py:405
  70.9 1.1 %shard_map.124.known_ref = f32[128,128]{1,0:T(8,128)S(1)} custom-call(f32[1,1,32,384]{3,2,1,0:T(8,128)} %get-tuple-element.72.refs_0_.refs_1_, bf16[128,96]{1,0:T(8,128)(2,1)} %get-tuple-element.73.refs_1_, f32[128,384]{1,0:T(8,128)} %get-tuple-element.63.refs_15_.refs_2_, f32[1,1,128,128]{3,2,1,0:T(8,128)} %refs_3_.7), custom_call_target="tpu_custom_call" | custom-call | tf_op jit(solution)/shard_map/pallas_call | solution.py:87
  72.0 4.8 %shard_map.125.token.refs_0_.refs_1_.field_hbm = f32[1,24,32,384]{3,2,1,0:T(8,128)} custom-call(f32[1,24,32,384]{3,2,1,0:T(8,128)} %get-tuple-element.76.refs_0_, f32[1,1,32,384]{3,2,1,0:T(8,128)} %get-tuple-element.72.refs_0_.refs_1_, bf16[384,384]{1,0:T(8,128)(2,1)} %refs_2_.6, bf16[384,384]{1,0:T(8,128)(2,1)} %refs_7_.1, bf16[384,384]{1,0:T(8,128)(2,1)} %refs_4_.5, ...), custom_call_target="tpu_custom_call" | custom-call | tf_op jit(solution)/shard_map/pallas_call | solution.py:87
  76.9 6.3 %all-to-all-done.3.in_ref = bf16[64,4,384]{2,1,0:T(4,128)(2,1)S(1)} async-done(((bf16[64,4,384]{2,1,0:T(4,128)(2,1)}), bf16[64,4,384]{2,1,0:T(4,128)(2,1)S(1)}, u32[]{:S(2)}, u32[]{:S(2)}) %all-to-all-start.3) | async-done | bytes 196640 | tf_op jit(solution)/shard_map/all_to_all | solution.py:405
  83.1 3.6 %shard_map.126 = (bf16[64,4,384]{2,1,0:T(4,128)(2,1)}, bf16[256,384]{1,0:T(8,128)(2,1)}, bf16[32,384]{1,0:T(8,128)(2,1)}, bf16[32,384]{1,0:T(8,128)(2,1)}) custom-call(bf16[64,4,384]{2,1,0:T(4,128)(2,1)S(1)} %all-to-all-done.3.in_ref, bf16[80,128,128]{2,1,0:T(8,128)(2,1)S(1)} %get-tuple-element.68.early_ref, bf16[128,256]{1,0:T(8,128)(2,1)S(1)} %get-tuple-element.69.get_ref, ...), custom_call_target="tpu_custom_call" | custom-call | tf_op jit(solution)/shard_map/pallas_call | solution.py:456
  86.8 4.4 %all-to-all-start.4 = ((bf16[64,4,384]{2,1,0:T(4,128)(2,1)}), bf16[64,4,384]{2,1,0:T(4,128)(2,1)S(1)}, u32[]{:S(2)}, u32[]{:S(2)}) async-start(bf16[64,4,384]{2,1,0:T(4,128)(2,1)} %get-tuple-element.77), calls=%async_computation.4 | async-start | bytes 393216 | tf_op jit(solution)/shard_map/all_to_all | solution.py:405
  91.1 3.2 %collective-permute-start.2 = (bf16[32,384]{1,0:T(8,128)(2,1)}, bf16[32,384]{1,0:T(8,128)(2,1)S(1)}, u32[]{:S(2)}, u32[]{:S(2)}) collective-permute-start(bf16[32,384]{1,0:T(8,128)(2,1)} %get-tuple-element.85), channel_id=1, source_target_pairs={{0,64},{64,128},{128,192},{1,65},{65,129},{129,193},{2,66},{66,130... | collective-permute-start | bytes 73736 | tf_op jit(solution)/shard_map/ppermute | solution.py:401
  94.4 1.3 %collective-permute-start.3 = (bf16[32,384]{1,0:T(8,128)(2,1)}, bf16[32,384]{1,0:T(8,128)(2,1)S(1)}, u32[]{:S(2)}, u32[]{:S(2)}) collective-permute-start(bf16[32,384]{1,0:T(8,128)(2,1)} %get-tuple-element.86), channel_id=1, source_target_pairs={{64,0},{128,64},{192,128},{65,1},{129,65},{193,129},{66,2},{130,66... | collective-permute-start | bytes 73736 | tf_op jit(solution)/shard_map/ppermute | solution.py:401
  95.7 1.4 %shard_map.127 = (f32[32,384]{1,0:T(8,128)S(1)}, f32[32,384]{1,0:T(8,128)S(1)}, f32[32,384]{1,0:T(8,128)S(1)}, f32[32,384]{1,0:T(8,128)S(1)}, bf16[256,128]{1,0:...) custom-call(f32[1,24,32,384]{3,2,1,0:T(8,128)} %shard_map.125.token.refs_0_.refs_1_.field_hbm, ...), custom_call_target="tpu_custom_call" | custom-call | tf_op jit(solution)/shard_map/pallas_call | solution.py:87
  97.1 0.0 collective-permute-done.2.low_ref
  97.1 2.4 %collective-permute-done.3.high_ref = bf16[32,384]{1,0:T(8,128)(2,1)S(1)} collective-permute-done((bf16[32,384]{1,0:T(8,128)(2,1)}, bf16[32,384]{1,0:T(8,128)(2,1)S(1)}, u32[]{:S(2)}, u32[]{:S(2)}) %collective-permute-start.3) | collective-permute-done | bytes 24608 | tf_op jit(solution)/shard_map/ppermute | solution.py:401
  99.4 3.9 %all-to-all-done.4.in_ref = bf16[64,4,384]{2,1,0:T(4,128)(2,1)S(1)} async-done(((bf16[64,4,384]{2,1,0:T(4,128)(2,1)}), bf16[64,4,384]{2,1,0:T(4,128)(2,1)S(1)}, u32[]{:S(2)}, u32[]{:S(2)}) %all-to-all-start.4) | async-done | bytes 196640 | tf_op jit(solution)/shard_map/all_to_all | solution.py:405
  103.3 0.9 shard_map.128
Async XLA Ops:
  1.7 22.4 %all-to-all-start = ((f32[64,1,128]{2,1,0:T(1,128)}), f32[64,1,128]{2,1,0:T(1,128)S(1)}, u32[]{:S(2)}, u32[]{:S(2)}) async-start(f32[64,1,128]{2,1,0:T(1,128)} %bitcast.1), calls=%async_computation | async-start | bytes 65536 | tf_op jit(solution)/shard_map/all_to_all | solution.py:405
  25.1 16.9 %all-to-all-start.1 = ((bf16[64,4,384]{2,1,0:T(4,128)(2,1)}), bf16[64,4,384]{2,1,0:T(4,128)(2,1)S(1)}, u32[]{:S(2)}, u32[]{:S(2)}) async-start(bf16[64,4,384]{2,1,0:T(4,128)(2,1)} %get-tuple-element.47), calls=%async_computation.1 | async-start | bytes 393216 | tf_op jit(solution)/shard_map/all_to_all | solution.py:405
  29.8 4.5 %collective-permute-start = (bf16[32,384]{1,0:T(8,128)(2,1)}, bf16[32,384]{1,0:T(8,128)(2,1)S(1)}, u32[]{:S(2)}, u32[]{:S(2)}) collective-permute-start(bf16[32,384]{1,0:T(8,128)(2,1)} %get-tuple-element.53), channel_id=1, source_target_pairs={{0,64},{64,128},{128,192},{1,65},{65,129},{129,193},{2,66},{66,130... | collective-permute-start | bytes 73736 | tf_op jit(solution)/shard_map/ppermute | solution.py:401
  33.0 5.1 %collective-permute-start.1 = (bf16[32,384]{1,0:T(8,128)(2,1)}, bf16[32,384]{1,0:T(8,128)(2,1)S(1)}, u32[]{:S(2)}, u32[]{:S(2)}) collective-permute-start(bf16[32,384]{1,0:T(8,128)(2,1)} %get-tuple-element.54), channel_id=1, source_target_pairs={{64,0},{128,64},{192,128},{65,1},{129,65},{193,129},{66,2},{130,66... | collective-permute-start | bytes 73736 | tf_op jit(solution)/shard_map/ppermute | solution.py:401
  45.6 19.7 %all-to-all-start.2 = ((bf16[64,4,384]{2,1,0:T(4,128)(2,1)}), bf16[64,4,384]{2,1,0:T(4,128)(2,1)S(1)}, u32[]{:S(2)}, u32[]{:S(2)}) async-start(bf16[64,4,384]{2,1,0:T(4,128)(2,1)} %get-tuple-element.56), calls=%async_computation.2 | async-start | bytes 393216 | tf_op jit(solution)/shard_map/all_to_all | solution.py:405
  66.4 16.7 %all-to-all-start.3 = ((bf16[64,4,384]{2,1,0:T(4,128)(2,1)}), bf16[64,4,384]{2,1,0:T(4,128)(2,1)S(1)}, u32[]{:S(2)}, u32[]{:S(2)}) async-start(bf16[64,4,384]{2,1,0:T(4,128)(2,1)} %get-tuple-element.67), calls=%async_computation.3 | async-start | bytes 393216 | tf_op jit(solution)/shard_map/all_to_all | solution.py:405
  86.8 16.6 %all-to-all-start.4 = ((bf16[64,4,384]{2,1,0:T(4,128)(2,1)}), bf16[64,4,384]{2,1,0:T(4,128)(2,1)S(1)}, u32[]{:S(2)}, u32[]{:S(2)}) async-start(bf16[64,4,384]{2,1,0:T(4,128)(2,1)} %get-tuple-element.77), calls=%async_computation.4 | async-start | bytes 393216 | tf_op jit(solution)/shard_map/all_to_all | solution.py:405
  91.1 5.9 %collective-permute-start.2 = (bf16[32,384]{1,0:T(8,128)(2,1)}, bf16[32,384]{1,0:T(8,128)(2,1)S(1)}, u32[]{:S(2)}, u32[]{:S(2)}) collective-permute-start(bf16[32,384]{1,0:T(8,128)(2,1)} %get-tuple-element.85), channel_id=1, source_target_pairs={{0,64},{64,128},{128,192},{1,65},{65,129},{129,193},{2,66},{66,130... | collective-permute-start | bytes 73736 | tf_op jit(solution)/shard_map/ppermute | solution.py:401
  94.4 5.1 %collective-permute-start.3 = (bf16[32,384]{1,0:T(8,128)(2,1)}, bf16[32,384]{1,0:T(8,128)(2,1)S(1)}, u32[]{:S(2)}, u32[]{:S(2)}) collective-permute-start(bf16[32,384]{1,0:T(8,128)(2,1)} %get-tuple-element.86), channel_id=1, source_target_pairs={{64,0},{128,64},{192,128},{65,1},{129,65},{193,129},{66,2},{130,66... | collective-permute-start | bytes 73736 | tf_op jit(solution)/shard_map/ppermute | solution.py:401

commit v11 on v10

--- a/solution.py
+++ b/solution.py
@@ -7,7 +7,7 @@
 
 PENALTY = 2.0
 CAPACITY = 4
-GROUP = 16
+GROUP = 32
 PIECES = 4
 PARTS = 2
 VMEM = pltpu.VMEM

time: 105 us -> 105 us (level)
  no operation moved by 1% of the time
where the time goes in v11:
time: 105 us
  starting transfers between devices  43.2 us (41%)
  waiting for transfers between devices  33.9 us (32%)
  Pallas kernels  27.6 us (26%)
    all_to_all x5, starting transfers between devices, exchange(): return lax.all_to_all(parts, 'dom', 0, 0, tiled=True)  34.2 us
    all_to_all x5, waiting for transfers between devices, exchange(): return lax.all_to_all(parts, 'dom', 0, 0, tiled=True)  27.8 us
    pallas_call x8, Pallas kernels, staged(): pl.pallas_call(kernel, out_shape=tuple((space(i, out) for i, out in enume...  18.8 us
    ppermute x4, starting transfers between devices, shift(): return lax.ppermute(block, 'slab', pairs)  8.99 us
    pallas_call x2, Pallas kernels, contact(): pl.pallas_call(contact_kernel, out_shape=[pltpu.HBM(out.shape, BF16) for...  7.86 us
    ppermute x4, waiting for transfers between devices, shift(): return lax.ppermute(block, 'slab', pairs)  6.13 us
  transfers between devices with their start and end apart: 9, of which 7 were waited for; matrix products, arithmetic and copies ran while one was open for 0% of the time, Pallas kernels for 14%

profile of v11, /device:TPU:1, one launch (start us, length us, event | category | flops | bytes accessed | tf_op | source)
XLA Modules:
  0.0 104.9 jit_solution(2013241888375736472)
XLA Ops:
  0.0 1.7 %shard_map.118.refs_7_ = f32[64,128]{1,0:T(8,128)} custom-call(s32[1,1,128]{2,1,0:T(1,128)} %refs_0_.4, s32[1,1,128]{2,1,0:T(1,128)} %refs_1_.3), custom_call_target="tpu_custom_call" | custom-call | tf_op jit(solution)/shard_map/pallas_call | solution.py:87
  1.7 13.0 %all-to-all-start = ((f32[64,1,128]{2,1,0:T(1,128)}), f32[64,1,128]{2,1,0:T(1,128)S(1)}, u32[]{:S(2)}, u32[]{:S(2)}) async-start(f32[64,1,128]{2,1,0:T(1,128)} %bitcast.1), calls=%async_computation | async-start | bytes 65536 | tf_op jit(solution)/shard_map/all_to_all | solution.py:405
  14.7 2.1 %shard_map.119 = (bf16[256,128]{1,0:T(8,128)(2,1)}, bf16[128,256]{1,0:T(8,128)(2,1)}, bf16[128,96]{1,0:T(8,128)(2,1)}, bf16[32,256]{1,0:T(8,128)(2,1)}, f32[128,...) custom-call(s32[1,1,128]{2,1,0:T(1,128)} %refs_0_.4, ...), custom_call_target="tpu_custom_call" | custom-call | tf_op jit(solution)/shard_map/pallas_call | solution.py:87
  16.8 7.3 %all-to-all-done = f32[64,1,128]{2,1,0:T(1,128)S(1)} async-done(((f32[64,1,128]{2,1,0:T(1,128)}), f32[64,1,128]{2,1,0:T(1,128)S(1)}, u32[]{:S(2)}, u32[]{:S(2)}) %all-to-all-start) | async-done | bytes 32800 | tf_op jit(solution)/shard_map/all_to_all | solution.py:405
  24.1 1.0 shard_map.120
  25.1 4.7 %all-to-all-start.1 = ((bf16[64,4,384]{2,1,0:T(4,128)(2,1)}), bf16[64,4,384]{2,1,0:T(4,128)(2,1)S(1)}, u32[]{:S(2)}, u32[]{:S(2)}) async-start(bf16[64,4,384]{2,1,0:T(4,128)(2,1)} %get-tuple-element.47), calls=%async_computation.1 | async-start | bytes 393216 | tf_op jit(solution)/shard_map/all_to_all | solution.py:405
  29.8 3.2 %collective-permute-start = (bf16[32,384]{1,0:T(8,128)(2,1)}, bf16[32,384]{1,0:T(8,128)(2,1)S(1)}, u32[]{:S(2)}, u32[]{:S(2)}) collective-permute-start(bf16[32,384]{1,0:T(8,128)(2,1)} %get-tuple-element.53), channel_id=1, source_target_pairs={{0,64},{64,128},{128,192},{1,65},{65,129},{129,193},{2,66},{66,130... | collective-permute-start | bytes 73736 | tf_op jit(solution)/shard_map/ppermute | solution.py:401
  33.0 1.3 %collective-permute-start.1 = (bf16[32,384]{1,0:T(8,128)(2,1)}, bf16[32,384]{1,0:T(8,128)(2,1)S(1)}, u32[]{:S(2)}, u32[]{:S(2)}) collective-permute-start(bf16[32,384]{1,0:T(8,128)(2,1)} %get-tuple-element.54), channel_id=1, source_target_pairs={{64,0},{128,64},{192,128},{65,1},{129,65},{193,129},{66,2},{130,66... | collective-permute-start | bytes 73736 | tf_op jit(solution)/shard_map/ppermute | solution.py:401
  34.3 0.0 collective-permute-done.low_hbm
  34.3 3.8 %collective-permute-done.1.high_hbm = bf16[32,384]{1,0:T(8,128)(2,1)S(1)} collective-permute-done((bf16[32,384]{1,0:T(8,128)(2,1)}, bf16[32,384]{1,0:T(8,128)(2,1)S(1)}, u32[]{:S(2)}, u32[]{:S(2)}) %collective-permute-start.1) | collective-permute-done | bytes 24608 | tf_op jit(solution)/shard_map/ppermute | solution.py:401
  38.1 3.9 %all-to-all-done.1.in_ref = bf16[64,4,384]{2,1,0:T(4,128)(2,1)S(1)} async-done(((bf16[64,4,384]{2,1,0:T(4,128)(2,1)}), bf16[64,4,384]{2,1,0:T(4,128)(2,1)S(1)}, u32[]{:S(2)}, u32[]{:S(2)}) %all-to-all-start.1) | async-done | bytes 196640 | tf_op jit(solution)/shard_map/all_to_all | solution.py:405
  42.0 3.9 %shard_map.121 = (bf16[64,4,384]{2,1,0:T(4,128)(2,1)}, bf16[256,384]{1,0:T(8,128)(2,1)}, bf16[32,384]{1,0:T(8,128)(2,1)}, bf16[32,384]{1,0:T(8,128)(2,1)}) custom-call(bf16[64,4,384]{2,1,0:T(4,128)(2,1)S(1)} %all-to-all-done.1.in_ref, bf16[64,128,128]{2,1,0:T(8,128)(2,1)S(1)} %get-tuple-element.48.early_ref, bf16[128,256]{1,0:T(8,128)(2,1)S(1)} %get-tuple-element.49.get_ref, ...), custom_call_target="tpu_custom_call" | custom-call | tf_op jit(solution)/shard_map/pallas_call | solution.py:456
  45.9 7.7 %all-to-all-start.2 = ((bf16[64,4,384]{2,1,0:T(4,128)(2,1)}), bf16[64,4,384]{2,1,0:T(4,128)(2,1)S(1)}, u32[]{:S(2)}, u32[]{:S(2)}) async-start(bf16[64,4,384]{2,1,0:T(4,128)(2,1)} %get-tuple-element.56), calls=%async_computation.2 | async-start | bytes 393216 | tf_op jit(solution)/shard_map/all_to_all | solution.py:405
  53.6 5.6 %shard_map.122 = (f32[1,24,32,384]{3,2,1,0:T(8,128)}, f32[32,384]{1,0:T(8,128)S(1)}, f32[32,384]{1,0:T(8,128)S(1)}, bf16[256,128]{1,0:T(8,128)(2,1)S(1)}, bf16[3...) custom-call(f32[1,24,32,384]{3,2,1,0:T(8,128)} %refs_1_.5, ...), custom_call_target="tpu_custom_call" | custom-call | tf_op jit(solution)/shard_map/pallas_call | solution.py:87
  59.2 6.5 %all-to-all-done.2.refs_0_ = bf16[64,4,384]{2,1,0:T(4,128)(2,1)S(1)} async-done(((bf16[64,4,384]{2,1,0:T(4,128)(2,1)}), bf16[64,4,384]{2,1,0:T(4,128)(2,1)S(1)}, u32[]{:S(2)}, u32[]{:S(2)}) %all-to-all-start.2) | async-done | bytes 196640 | tf_op jit(solution)/shard_map/all_to_all | solution.py:405
  65.6 1.1 %shard_map.123 = (bf16[64,4,384]{2,1,0:T(4,128)(2,1)}, f32[1,1,32,384]{3,2,1,0:T(8,128)}, bf16[32,384]{1,0:T(8,128)(2,1)}) custom-call(bf16[64,4,384]{2,1,0:T(4,128)(2,1)S(1)} %all-to-all-done.2.refs_0_, bf16[256,128]{1,0:T(8,128)(2,1)S(1)} %get-tuple-element.64.refs_1_, f32[32,384]{1,0:T(8,128)S(1)} %get-tuple-element.65.refs_2_, ...), custom_call_target="tpu_custom_call" | custom-call | tf_op jit(solution)/shard_map/pallas_call | solution.py:87
  66.7 4.5 %all-to-all-start.3 = ((bf16[64,4,384]{2,1,0:T(4,128)(2,1)}), bf16[64,4,384]{2,1,0:T(4,128)(2,1)S(1)}, u32[]{:S(2)}, u32[]{:S(2)}) async-start(bf16[64,4,384]{2,1,0:T(4,128)(2,1)} %get-tuple-element.67), calls=%async_computation.3 | async-start | bytes 393216 | tf_op jit(solution)/shard_map/all_to_all | solution.py:405
  71.2 1.1 %shard_map.124.known_ref = f32[128,128]{1,0:T(8,128)S(1)} custom-call(f32[1,1,32,384]{3,2,1,0:T(8,128)} %get-tuple-element.72.refs_0_.refs_1_, bf16[128,96]{1,0:T(8,128)(2,1)} %get-tuple-element.73.refs_1_, f32[128,384]{1,0:T(8,128)} %get-tuple-element.63.refs_15_.refs_2_, f32[1,1,128,128]{3,2,1,0:T(8,128)} %refs_3_.7), custom_call_target="tpu_custom_call" | custom-call | tf_op jit(solution)/shard_map/pallas_call | solution.py:87
  72.3 4.8 %shard_map.125.token.refs_0_.refs_1_.field_hbm = f32[1,24,32,384]{3,2,1,0:T(8,128)} custom-call(f32[1,24,32,384]{3,2,1,0:T(8,128)} %get-tuple-element.76.refs_0_, f32[1,1,32,384]{3,2,1,0:T(8,128)} %get-tuple-element.72.refs_0_.refs_1_, bf16[384,384]{1,0:T(8,128)(2,1)} %refs_2_.6, bf16[384,384]{1,0:T(8,128)(2,1)} %refs_7_.1, bf16[384,384]{1,0:T(8,128)(2,1)} %refs_4_.5, ...), custom_call_target="tpu_custom_call" | custom-call | tf_op jit(solution)/shard_map/pallas_call | solution.py:87
  77.2 6.3 %all-to-all-done.3.in_ref = bf16[64,4,384]{2,1,0:T(4,128)(2,1)S(1)} async-done(((bf16[64,4,384]{2,1,0:T(4,128)(2,1)}), bf16[64,4,384]{2,1,0:T(4,128)(2,1)S(1)}, u32[]{:S(2)}, u32[]{:S(2)}) %all-to-all-start.3) | async-done | bytes 196640 | tf_op jit(solution)/shard_map/all_to_all | solution.py:405
  83.4 3.9 %shard_map.126 = (bf16[64,4,384]{2,1,0:T(4,128)(2,1)}, bf16[256,384]{1,0:T(8,128)(2,1)}, bf16[32,384]{1,0:T(8,128)(2,1)}, bf16[32,384]{1,0:T(8,128)(2,1)}) custom-call(bf16[64,4,384]{2,1,0:T(4,128)(2,1)S(1)} %all-to-all-done.3.in_ref, bf16[64,128,128]{2,1,0:T(8,128)(2,1)S(1)} %get-tuple-element.68.early_ref, bf16[128,256]{1,0:T(8,128)(2,1)S(1)} %get-tuple-element.69.get_ref, ...), custom_call_target="tpu_custom_call" | custom-call | tf_op jit(solution)/shard_map/pallas_call | solution.py:456
  87.4 4.4 %all-to-all-start.4 = ((bf16[64,4,384]{2,1,0:T(4,128)(2,1)}), bf16[64,4,384]{2,1,0:T(4,128)(2,1)S(1)}, u32[]{:S(2)}, u32[]{:S(2)}) async-start(bf16[64,4,384]{2,1,0:T(4,128)(2,1)} %get-tuple-element.77), calls=%async_computation.4 | async-start | bytes 393216 | tf_op jit(solution)/shard_map/all_to_all | solution.py:405
  91.7 3.2 %collective-permute-start.2 = (bf16[32,384]{1,0:T(8,128)(2,1)}, bf16[32,384]{1,0:T(8,128)(2,1)S(1)}, u32[]{:S(2)}, u32[]{:S(2)}) collective-permute-start(bf16[32,384]{1,0:T(8,128)(2,1)} %get-tuple-element.85), channel_id=1, source_target_pairs={{0,64},{64,128},{128,192},{1,65},{65,129},{129,193},{2,66},{66,130... | collective-permute-start | bytes 73736 | tf_op jit(solution)/shard_map/ppermute | solution.py:401
  95.0 1.3 %collective-permute-start.3 = (bf16[32,384]{1,0:T(8,128)(2,1)}, bf16[32,384]{1,0:T(8,128)(2,1)S(1)}, u32[]{:S(2)}, u32[]{:S(2)}) collective-permute-start(bf16[32,384]{1,0:T(8,128)(2,1)} %get-tuple-element.86), channel_id=1, source_target_pairs={{64,0},{128,64},{192,128},{65,1},{129,65},{193,129},{66,2},{130,66... | collective-permute-start | bytes 73736 | tf_op jit(solution)/shard_map/ppermute | solution.py:401
  96.3 1.4 %shard_map.127 = (f32[32,384]{1,0:T(8,128)S(1)}, f32[32,384]{1,0:T(8,128)S(1)}, f32[32,384]{1,0:T(8,128)S(1)}, f32[32,384]{1,0:T(8,128)S(1)}, bf16[256,128]{1,0:...) custom-call(f32[1,24,32,384]{3,2,1,0:T(8,128)} %shard_map.125.token.refs_0_.refs_1_.field_hbm, ...), custom_call_target="tpu_custom_call" | custom-call | tf_op jit(solution)/shard_map/pallas_call | solution.py:87
  97.7 0.0 collective-permute-done.2.low_ref
  97.7 2.4 %collective-permute-done.3.high_ref = bf16[32,384]{1,0:T(8,128)(2,1)S(1)} collective-permute-done((bf16[32,384]{1,0:T(8,128)(2,1)}, bf16[32,384]{1,0:T(8,128)(2,1)S(1)}, u32[]{:S(2)}, u32[]{:S(2)}) %collective-permute-start.3) | collective-permute-done | bytes 24608 | tf_op jit(solution)/shard_map/ppermute | solution.py:401
  100.0 3.9 %all-to-all-done.4.in_ref = bf16[64,4,384]{2,1,0:T(4,128)(2,1)S(1)} async-done(((bf16[64,4,384]{2,1,0:T(4,128)(2,1)}), bf16[64,4,384]{2,1,0:T(4,128)(2,1)S(1)}, u32[]{:S(2)}, u32[]{:S(2)}) %all-to-all-start.4) | async-done | bytes 196640 | tf_op jit(solution)/shard_map/all_to_all | solution.py:405
  103.9 0.9 shard_map.128
Async XLA Ops:
  1.7 22.4 %all-to-all-start = ((f32[64,1,128]{2,1,0:T(1,128)}), f32[64,1,128]{2,1,0:T(1,128)S(1)}, u32[]{:S(2)}, u32[]{:S(2)}) async-start(f32[64,1,128]{2,1,0:T(1,128)} %bitcast.1), calls=%async_computation | async-start | bytes 65536 | tf_op jit(solution)/shard_map/all_to_all | solution.py:405
  25.1 16.9 %all-to-all-start.1 = ((bf16[64,4,384]{2,1,0:T(4,128)(2,1)}), bf16[64,4,384]{2,1,0:T(4,128)(2,1)S(1)}, u32[]{:S(2)}, u32[]{:S(2)}) async-start(bf16[64,4,384]{2,1,0:T(4,128)(2,1)} %get-tuple-element.47), calls=%async_computation.1 | async-start | bytes 393216 | tf_op jit(solution)/shard_map/all_to_all | solution.py:405
  29.8 4.5 %collective-permute-start = (bf16[32,384]{1,0:T(8,128)(2,1)}, bf16[32,384]{1,0:T(8,128)(2,1)S(1)}, u32[]{:S(2)}, u32[]{:S(2)}) collective-permute-start(bf16[32,384]{1,0:T(8,128)(2,1)} %get-tuple-element.53), channel_id=1, source_target_pairs={{0,64},{64,128},{128,192},{1,65},{65,129},{129,193},{2,66},{66,130... | collective-permute-start | bytes 73736 | tf_op jit(solution)/shard_map/ppermute | solution.py:401
  33.0 5.1 %collective-permute-start.1 = (bf16[32,384]{1,0:T(8,128)(2,1)}, bf16[32,384]{1,0:T(8,128)(2,1)S(1)}, u32[]{:S(2)}, u32[]{:S(2)}) collective-permute-start(bf16[32,384]{1,0:T(8,128)(2,1)} %get-tuple-element.54), channel_id=1, source_target_pairs={{64,0},{128,64},{192,128},{65,1},{129,65},{193,129},{66,2},{130,66... | collective-permute-start | bytes 73736 | tf_op jit(solution)/shard_map/ppermute | solution.py:401
  45.9 19.7 %all-to-all-start.2 = ((bf16[64,4,384]{2,1,0:T(4,128)(2,1)}), bf16[64,4,384]{2,1,0:T(4,128)(2,1)S(1)}, u32[]{:S(2)}, u32[]{:S(2)}) async-start(bf16[64,4,384]{2,1,0:T(4,128)(2,1)} %get-tuple-element.56), calls=%async_computation.2 | async-start | bytes 393216 | tf_op jit(solution)/shard_map/all_to_all | solution.py:405
  66.7 16.7 %all-to-all-start.3 = ((bf16[64,4,384]{2,1,0:T(4,128)(2,1)}), bf16[64,4,384]{2,1,0:T(4,128)(2,1)S(1)}, u32[]{:S(2)}, u32[]{:S(2)}) async-start(bf16[64,4,384]{2,1,0:T(4,128)(2,1)} %get-tuple-element.67), calls=%async_computation.3 | async-start | bytes 393216 | tf_op jit(solution)/shard_map/all_to_all | solution.py:405
  87.4 16.6 %all-to-all-start.4 = ((bf16[64,4,384]{2,1,0:T(4,128)(2,1)}), bf16[64,4,384]{2,1,0:T(4,128)(2,1)S(1)}, u32[]{:S(2)}, u32[]{:S(2)}) async-start(bf16[64,4,384]{2,1,0:T(4,128)(2,1)} %get-tuple-element.77), calls=%async_computation.4 | async-start | bytes 393216 | tf_op jit(solution)/shard_map/all_to_all | solution.py:405
  91.7 5.9 %collective-permute-start.2 = (bf16[32,384]{1,0:T(8,128)(2,1)}, bf16[32,384]{1,0:T(8,128)(2,1)S(1)}, u32[]{:S(2)}, u32[]{:S(2)}) collective-permute-start(bf16[32,384]{1,0:T(8,128)(2,1)} %get-tuple-element.85), channel_id=1, source_target_pairs={{0,64},{64,128},{128,192},{1,65},{65,129},{129,193},{2,66},{66,130... | collective-permute-start | bytes 73736 | tf_op jit(solution)/shard_map/ppermute | solution.py:401
  95.0 5.1 %collective-permute-start.3 = (bf16[32,384]{1,0:T(8,128)(2,1)}, bf16[32,384]{1,0:T(8,128)(2,1)S(1)}, u32[]{:S(2)}, u32[]{:S(2)}) collective-permute-start(bf16[32,384]{1,0:T(8,128)(2,1)} %get-tuple-element.86), channel_id=1, source_target_pairs={{64,0},{128,64},{192,128},{65,1},{129,65},{193,129},{66,2},{130,66... | collective-permute-start | bytes 73736 | tf_op jit(solution)/shard_map/ppermute | solution.py:401
